TPU v7x, 32 devices: a whole 2x2x4 slice. The times are simulated.
32 devices in a mesh: dp: 4 (over y, x), fsdp: 8 (over z, core).
Axes of the slice: x: 2, y: 2, z: 4, core: 2. Of those that a mesh axis runs over, the one named last changes fastest.
Arguments:
- tokens: bfloat16 [32, 1024, 768], P(('dp', 'fsdp')), may hold values from -6 to 6
- row_lengths: int32 [32], P(('dp', 'fsdp')), may hold values from 256 to 1024, as said below
- live_mask: int32 [2, 32, 1024], P(None, ('dp', 'fsdp')), may hold values 0 or 1
- pass_index: int32 [32], P(('dp', 'fsdp')), may hold values from 1 to 4
- w_qkv: bfloat16 [768, 2304], P(None, ('dp', 'fsdp')), may hold values from -0.21875 to 0.21875
- w_out: bfloat16 [768, 768], P(None, ('dp', 'fsdp')), may hold values from -2.5 to 2.5
- w_up: bfloat16 [768, 3072], P(None, ('dp', 'fsdp')), may hold values from -0.21875 to 0.21875
- w_down: bfloat16 [3072, 768], P(('dp', 'fsdp')), may hold values from -0.109375 to 0.109375
- norm_gains: bfloat16 [2, 768], P(None, ('dp', 'fsdp')), may hold values from 0.099609375 to 1.8984375
- norm_shifts: bfloat16 [2, 768], P(None, ('dp', 'fsdp')), may hold values from -4 to 4
- pass_table: bfloat16 [5, 768], P(None, ('dp', 'fsdp')), may hold values from -6 to 6
- cotangent: float32 [32, 1024, 768], P(('dp', 'fsdp')), may hold values from -6 to 6
Outputs:
- activations: bfloat16 [32, 1024, 768], P(('dp', 'fsdp'))
- input_grad: float32 [32, 1024, 768], P(('dp', 'fsdp'))
- grad_qkv: float32 [768, 2304], P(None, ('dp', 'fsdp'))
- grad_out: float32 [768, 768], P(None, ('dp', 'fsdp'))
- grad_up: float32 [768, 3072], P(None, ('dp', 'fsdp'))
- grad_down: float32 [3072, 768], P(('dp', 'fsdp'))
- grad_gains: float32 [2, 768], P(None, ('dp', 'fsdp'))
- grad_shifts: float32 [768], P(('dp', 'fsdp'))
- grad_second_shift: float32 [768], P(('dp', 'fsdp'))
- grad_table: float32 [5, 768], P(None, ('dp', 'fsdp'))
Inputs may be any that keep to these rules, and one draw needn't show every extreme that they name: `row_lengths`: some row uses all 1024 positions and some row only 256.
All inputs are finite; a program needn't handle non-finite values. No bound on the sum of `live_mask` on one device may be relied on, other than what follows from the above.
Results may differ from a plain program's by a relative error of at most 0.015.
Values may be sent and summed in bfloat16 or wider, within the bound.
No kernel may reach another device: no remote copies, remote signals or barrier semaphores. Data moves between devices by JAX's collectives and lax.ppermute only.
A program may use at most 320 MiB of HBM per device.

v0:
```python
import functools

import jax
import jax.numpy as jnp
from jax import lax
from jax.experimental import pallas as pl
from jax.experimental.pallas import tpu as pltpu
from jax.sharding import PartitionSpec as P

HEAD = 64
LANES = 128
AXES = ("dp", "fsdp")
bf16 = jnp.bfloat16
f32 = jnp.float32

norm_epsilon = 1e-05
masked_score = -1000000000.0
curve_one = 0.7978845608028654
curve_three = 0.7978845608028654 * 0.044715

VMEM_LIMIT = 60 * 1024 * 1024


def dot_nn(left, right):
    return lax.dot_general(left, right, (((1,), (0,)), ((), ())), preferred_element_type=f32)


def dot_nt(left, right):
    return lax.dot_general(left, right, (((1,), (1,)), ((), ())), preferred_element_type=f32)


def dot_tn(left, right):
    return lax.dot_general(left, right, (((0,), (0,)), ((), ())), preferred_element_type=f32)


def normalize(values):
    center = jnp.mean(values, axis=-1, keepdims=True)
    centered = values - center
    spread = jnp.mean(centered * centered, axis=-1, keepdims=True)
    scale = lax.rsqrt(spread + norm_epsilon)
    return centered * scale, scale


def norm_back(grad, gain, xhat, scale):
    gained = grad * gain
    first = jnp.mean(gained, axis=-1, keepdims=True)
    second = jnp.mean(gained * xhat, axis=-1, keepdims=True)
    return scale * (gained - first - xhat * second)


def gelu_pair(lifted):
    square = lifted * lifted
    cubic = curve_three * square
    half = 0.5 + 0.5 * jnp.tanh(lifted * (curve_one + cubic))
    value = lifted * half
    slope = half + value * ((1.0 - half) * (2.0 * curve_one + 6.0 * cubic))
    return value, slope


def call(kernel, grid, in_specs, out_specs, out_shape, flops, args, scratch=(), hold=()):
    moved = sum(a.size * a.dtype.itemsize for a in args)
    moved += sum(o.size * o.dtype.itemsize for o in out_shape)
    given, held = len(args), len(hold)

    def run(*refs):
        kernel(*refs[:given], *refs[given + held :])

    return pl.pallas_call(
        run,
        grid=grid,
        in_specs=list(in_specs) + [pl.BlockSpec(memory_space=pl.ANY)] * held,
        out_specs=out_specs,
        out_shape=out_shape,
        scratch_shapes=list(scratch),
        compiler_params=pltpu.CompilerParams(
            dimension_semantics=("arbitrary",) * len(grid), vmem_limit_bytes=VMEM_LIMIT
        ),
        cost_estimate=pl.CostEstimate(
            flops=flops // 4096, bytes_accessed=moved // 4096, transcendentals=0
        ),
    )(*args, *hold)


def rows_spec(block_rows, width):
    return pl.BlockSpec((block_rows, width), lambda i: (i, 0))


def whole_spec(array):
    zeros = (0,) * len(array.shape)
    return pl.BlockSpec(array.shape, lambda i: zeros, pipeline_mode=pl.Buffered(1))


def sds(shape, dtype):
    return jax.ShapeDtypeStruct(shape, dtype)


def head_part(x, gain, shift, w_qkv, mixed_ref, xhat_ref):
    xhat, _ = normalize(x)
    normed = (xhat * gain + shift).astype(bf16)
    xhat_ref[...] = xhat.astype(bf16)
    mixed_ref[...] = dot_nt(normed, w_qkv[...]).astype(bf16)


def first_kernel(x_ref, norms_ref, wq_ref, mixed_ref, xhat_ref):
    head_part(
        x_ref[...].astype(f32), norms_ref[0:1, :], norms_ref[2:3, :], wq_ref, mixed_ref, xhat_ref
    )


def ff_chunks(order, place_ref, packed_ref, share):
    found = []
    if share >= 768:
        for at in range(0, share, 768):
            up, down = pl.ds(at, 768), pl.ds(share + at, 768)
            found.append((lambda r=up: packed_ref[0, r, :], lambda r=down: packed_ref[0, r, :], pl.ds(at, 768)))
        return found
    per = 768 // share
    for first in range(0, len(order), per):

        def rows(at, first=first):
            return jnp.concatenate(
                [
                    packed_ref[place_ref[3] ^ mask, pl.ds(at, share), :]
                    for mask in order[first : first + per]
                ],
                axis=0,
            )

        found.append(
            (functools.partial(rows, 0), functools.partial(rows, share), pl.ds(first * share, 768))
        )
    return found


def middle_kernel(order, share, place_ref, packed_ref, *refs):
    chunks = ff_chunks(order, place_ref, packed_ref, share)
    atts, refs = refs[:-13], refs[-13:]
    (
        x_ref, live_ref, norms_ref, emb_ref, wo_ref, wq_ref,
        hidden_ref, second_ref, act_ref, slope_ref, later_ref, mixed_ref, xhat_ref,
    ) = refs
    live = live_ref[...]
    branch, at = 0.0, 0
    for ref in atts:
        branch = branch + dot_nt(ref[...], wo_ref[:, at : at + ref.shape[1]])
        at += ref.shape[1]
    hidden = x_ref[...].astype(f32) + live * branch
    hidden_ref[...] = hidden
    xhat, _ = normalize(hidden)
    second = (xhat * norms_ref[1:2, :] + norms_ref[3:4, :]).astype(bf16)
    second_ref[...] = second
    total = jnp.zeros_like(hidden)
    for up, down, to in chunks:
        value, slope = gelu_pair(dot_nt(second, up()))
        value = value.astype(bf16)
        act_ref[:, to] = value
        slope_ref[:, to] = slope.astype(bf16)
        total = total + dot_nn(value, down())
    later = hidden + live * total + emb_ref[...]
    later_ref[...] = later
    head_part(later, norms_ref[0:1, :], norms_ref[2:3, :], wq_ref, mixed_ref, xhat_ref)


def mlp_back_tail(
    grad, live, hidden, second_grad, norms_ref, wo_ref, branch_ref, hgrad_ref, agrad_ref
):
    xhat, scale = normalize(hidden)
    hgrad = grad + norm_back(second_grad, norms_ref[1:2, :], xhat, scale)
    hgrad_ref[...] = hgrad
    branch = (live * hgrad).astype(bf16)
    branch_ref[...] = branch
    agrad_ref[...] = dot_nn(branch, wo_ref[...]).astype(bf16)
    gain_sum = jnp.sum(second_grad * xhat, axis=0, keepdims=True)
    shift_sum = jnp.sum(second_grad, axis=0, keepdims=True)
    return gain_sum, shift_sum


def add_sums(sums_ref, sums):
    @pl.when(pl.program_id(0) == 0)
    def _():
        sums_ref[...] = jnp.zeros_like(sums_ref)

    for place, value in enumerate(sums):
        sums_ref[place : place + 1, :] += value


def turn_kernel(order, share, place_ref, packed_ref, *refs):
    chunks = ff_chunks(order, place_ref, packed_ref, share)
    (
        att_ref, x_ref, live_ref, norms_ref, grad_ref, wo_ref,
        out_ref, second_ref, act_ref, drop_ref, lift_ref, branch_ref, hgrad_ref, agrad_ref, sums_ref,
    ) = refs
    live = live_ref[...]
    hidden = x_ref[...] + live * dot_nt(att_ref[...], wo_ref[...])
    xhat, _ = normalize(hidden)
    second = (xhat * norms_ref[1:2, :] + norms_ref[3:4, :]).astype(bf16)
    second_ref[...] = second
    grad = grad_ref[...]
    drop = (live * grad).astype(bf16)
    drop_ref[...] = drop
    total = jnp.zeros_like(hidden)
    second_grad = jnp.zeros_like(hidden)
    for up, down, to in chunks:
        up, down = up(), down()
        value, slope = gelu_pair(dot_nt(second, up))
        value = value.astype(bf16)
        act_ref[:, to] = value
        total = total + dot_nn(value, down)
        lift = (dot_nt(drop, down) * slope).astype(bf16)
        lift_ref[:, to] = lift
        second_grad = second_grad + dot_nn(lift, up)
    out_ref[...] = (hidden + live * total).astype(bf16)
    sums = mlp_back_tail(
        grad, live, hidden, second_grad, norms_ref, wo_ref, branch_ref, hgrad_ref, agrad_ref
    )
    add_sums(sums_ref, sums)


def head_back(mixed_grad_refs, wq_ref, x, hgrad, norms_ref):
    width = x.shape[1]
    normed_grad = jnp.zeros_like(x)
    for part in range(3):
        at = part * width
        for ref in mixed_grad_refs:
            normed_grad += dot_nn(ref[part], wq_ref[at : at + ref.shape[2], :])
            at += ref.shape[2]
    xhat, scale = normalize(x)
    return hgrad + norm_back(normed_grad, norms_ref[0:1, :], xhat, scale)


def back_kernel(order, share, place_ref, packed_ref, *refs):
    chunks = ff_chunks(order, place_ref, packed_ref, share)
    (
        mgrad_ref, later_ref, hgrad1_ref, norms_ref, live_ref, hidden_ref, slope_ref, wq_ref, wo_ref,
        drop_ref, lift_ref, branch_ref, hgrad_ref, agrad_ref, sums_ref,
    ) = refs
    grad = head_back([mgrad_ref], wq_ref, later_ref[...], hgrad1_ref[...], norms_ref)
    table_sum = jnp.sum(grad, axis=0, keepdims=True)
    live = live_ref[...]
    drop = (live * grad).astype(bf16)
    drop_ref[...] = drop
    second_grad = jnp.zeros_like(grad)
    for up, down, to in chunks:
        lift = (dot_nt(drop, down()) * slope_ref[:, to].astype(f32)).astype(bf16)
        lift_ref[:, to] = lift
        second_grad = second_grad + dot_nn(lift, up())
    sums = mlp_back_tail(
        grad, live, hidden_ref[...], second_grad, norms_ref, wo_ref, branch_ref, hgrad_ref, agrad_ref
    )
    add_sums(sums_ref, sums + (table_sum,))


def last_kernel(groups, *refs):
    mgrad_refs, (x_ref, hgrad_ref, norms_ref, wq_ref, out_ref) = refs[:groups], refs[groups:]
    out_ref[...] = head_back(
        mgrad_refs, wq_ref, x_ref[...].astype(f32), hgrad_ref[...], norms_ref
    )


def both_layers(left0, left1, right0, right1):
    return dot_tn(left0[...], right0[...]) + dot_tn(left1[...], right1[...])


def pair_grad_kernel(left0, left1, right0, right1, out_ref):
    out_ref[...] = both_layers(left0, left1, right0, right1).astype(bf16)


def pair_grads(left0, left1, right0, right1, start, size, hold=()):
    tokens = left0.shape[0]
    width = right0.shape[1]
    step = 384 if size % 384 == 0 else size
    first = start // step
    cols = pl.BlockSpec((tokens, step), lambda i: (0, first + i))
    return call(
        pair_grad_kernel,
        (size // step,),
        [cols] * 2 + [whole_spec(right0)] * 2,
        [rows_spec(step, width)],
        [sds((size, width), bf16)],
        4 * tokens * size * width,
        [left0, left1, right0, right1],
        hold=hold,
    )[0]


def blocks_spec(shape, index):
    return pl.BlockSpec(shape, lambda i: (index(i), 0, 0))


def other_grad_kernel(high, left0, left1, right0, right1, *refs):
    extra, out_ref = refs[:-1], refs[-1]
    total = both_layers(left0, left1, right0, right1).astype(bf16)
    for place in range(out_ref.shape[0]):
        out_ref[place, :high, :] = total[place * high : (place + 1) * high]
        for ref in extra:
            out_ref[place, high:, :] = ref[place]


def other_grads(cube, high, left0, left1, right0, right1, extra=(), hold=()):
    tokens = left0.shape[0]
    width = right0.shape[1]
    lines, turns = cube.count_line, cube.count_turns
    first = turns
    cols = pl.BlockSpec((tokens, lines * high), lambda i: (0, first + i))
    rows = high + sum(a.shape[1] for a in extra)
    return call(
        functools.partial(other_grad_kernel, high),
        (turns,),
        [cols] * 2
        + [whole_spec(right0)] * 2
        + [blocks_spec((lines,) + a.shape[1:], lambda i: i) for a in extra],
        [blocks_spec((lines, rows, width), lambda i: i)],
        [sds((cube.pairs, rows, width), bf16)],
        4 * tokens * cube.pairs * high * width,
        [left0, left1, right0, right1, *extra],
        hold=hold,
    )[0]


def own_grad_kernel(high, left0, left1, right0, right1, got, *refs):
    extra, (low_keep, low_send, late_keep, late_send) = refs[:-4], refs[-4:]
    middle = high // 2
    half = pl.num_programs(0) // 2
    step = pl.program_id(0)
    total = both_layers(left0, left1, right0, right1)

    def low_part(ref):
        for place in range(ref.shape[0]):
            at = place * high
            ref[place, :middle, :] = (
                total[at : at + middle] + got[place, :middle, :].astype(f32)
            ).astype(bf16)
            for more in extra:
                ref[place, middle:, :] = (
                    more[place].astype(f32) + got[place, high:, :].astype(f32)
                ).astype(bf16)

    def late_part(ref):
        for place in range(ref.shape[0]):
            at = place * high
            ref[place] = (
                total[at + middle : at + high] + got[place, middle:high, :].astype(f32)
            ).astype(bf16)

    @pl.when(step < half)
    def _():
        low_part(low_keep)

    @pl.when(step >= half)
    def _():
        low_part(low_send)

    @pl.when(step % 2 == 0)
    def _():
        late_part(late_keep)

    @pl.when(step % 2 == 1)
    def _():
        late_part(late_send)


def own_grads(cube, high, left0, left1, right0, right1, got, extra=(), hold=()):
    tokens = left0.shape[0]
    width = right0.shape[1]
    lines, turns = cube.count_line, cube.count_turns
    half = turns // 2
    cols = pl.BlockSpec((tokens, lines * high), lambda i: (0, i))
    low = high // 2 + sum(a.shape[1] for a in extra)
    late = high - high // 2

    def turned(i):
        found = 0
        for bit in range(1, turns.bit_length() - 1):
            found = found + (((i >> bit) & 1) << (turns.bit_length() - 2 - bit))
        return found

    def first_keep(i):
        return jnp.minimum(i, half - 1)

    def first_send(i):
        return jnp.maximum(i - half, 0)

    return call(
        functools.partial(own_grad_kernel, high),
        (turns,),
        [cols] * 2
        + [whole_spec(right0)] * 2
        + [blocks_spec((lines,) + a.shape[1:], lambda i: i) for a in (got, *extra)],
        [
            blocks_spec((lines, low, width), first_keep),
            blocks_spec((lines, low, width), first_send),
            blocks_spec((lines, late, width), turned),
            blocks_spec((lines, late, width), turned),
        ],
        [sds((cube.pairs // 2, n, width), bf16) for n in (low, low, late, late)],
        4 * tokens * cube.pairs * high * width,
        [left0, left1, right0, right1, got, *extra],
        hold=hold,
    )


def place_blocks(cube, place_ref, total_ref, own_ref, other_ref):
    rows = own_ref.shape[1]
    for chip in range(own_ref.shape[0]):
        if cube.inner == 0:
            own_ref[0] = total_ref[...].astype(bf16)
            continue
        even = total_ref[pl.ds(2 * chip * rows, rows), :].astype(bf16)
        odd = total_ref[pl.ds((2 * chip + 1) * rows, rows), :].astype(bf16)
        first = place_ref[2] == 0
        at = cube.place(2 * chip, 0) ^ place_ref[0]
        own_ref[at] = jnp.where(first, even, odd)
        other_ref[at] = jnp.where(first, odd, even)


def out_grad_kernel(cube, place_ref, left0, left1, right0, right1, own_ref, other_ref, total_ref):
    total_ref[...] = both_layers(left0, left1, right0, right1)
    place_blocks(cube, place_ref, total_ref, own_ref, other_ref)


def block_shapes(cube, rows, width):
    shape = (cube.pairs, rows, width)
    return [sds(shape, bf16)] * 2, [pl.BlockSpec(shape, lambda i: (0, 0, 0))] * 2


def out_grads(cube, place, left0, left1, right0, right1, hold=()):
    tokens, high = left0.shape
    width = right1.shape[1]
    shapes, specs = block_shapes(cube, high // cube.count, width)
    args = [left0, left1, right0, right1]
    return call(
        functools.partial(out_grad_kernel, cube),
        (1,),
        [pl.BlockSpec(memory_space=pltpu.SMEM)] + [whole_spec(a) for a in args],
        specs,
        shapes,
        4 * tokens * high * width,
        [place, *args],
        scratch=[pltpu.VMEM((high, width), f32)],
        hold=hold,
    )


def qkv_grad_kernel(cube, groups, passes, place_ref, pass_ref, *refs):
    lefts0, refs = refs[:groups], refs[groups:]
    left1, right0, right1, wq_ref, norms_ref, sums0_ref, sums1_ref, own_ref, other_ref = refs[:9]
    small_ref, total_ref = refs[9:]
    part = pl.program_id(0)
    high = left1.shape[2]
    width = right0.shape[1]
    gain, shift = norms_ref[0:1, :], norms_ref[2:3, :]
    ones = jnp.ones((8, right0.shape[0]), bf16)
    row = lax.broadcasted_iota(jnp.int32, (8, 1), 0)

    @pl.when(part == 0)
    def _():
        small_ref[...] = jnp.zeros_like(small_ref)
        small_ref[1:2, :] = sums0_ref[0:1, :] + sums1_ref[0:1, :]
        small_ref[3:4, :] = sums0_ref[1:2, :] + sums1_ref[1:2, :]
        for index in range(passes):
            small_ref[4 + index : 5 + index, :] = jnp.where(
                pass_ref[0] == index, sums0_ref[2:3, :], 0.0
            )

    at = 0
    gain_sum = jnp.zeros((1, width), f32)
    shift_sum = jnp.zeros((1, width), f32)
    for left0 in lefts0:
        to = pl.ds(at, left0.shape[2])
        rows = pl.ds(pl.multiple_of(part * high + at, 8), left0.shape[2])
        total = dot_tn(left0[0], right0[...]) + dot_tn(left1[0, :, to], right1[...])
        sums = dot_nn(ones, left0[0]) + dot_nn(ones, left1[0, :, to])
        terms = split_three(sums)
        three = jnp.where(row == 0, terms[0], jnp.where(row == 1, terms[1], terms[2]))
        three = jnp.where(row < 3, three, jnp.zeros_like(three))
        shifts = jnp.broadcast_to(shift, (8, width)).astype(bf16)
        weights = wq_ref[rows, :]
        gain_sum += jnp.sum(total * weights.astype(f32), axis=0, keepdims=True)
        shift_sum += jnp.sum(dot_nn(three, weights), axis=0, keepdims=True)
        total_ref[rows, :] = total * gain + dot_tn(three, shifts)
        at += left0.shape[2]
    small_ref[0:1, :] += gain_sum
    small_ref[2:3, :] += shift_sum

    @pl.when(part == pl.num_programs(0) - 1)
    def _():
        extra = 8
        rows = own_ref.shape[1] - extra
        share = width // cube.count
        half = width // 2
        small = small_ref[...]
        for chip in range(cube.pairs):
            found = []
            for device in range(2 * chip, 2 * chip + 1 + (cube.inner > 0)):
                block = total_ref[pl.ds(device * rows, rows), :]
                line = pltpu.roll(small, width - device * share, 1) if device else small
                line = jnp.concatenate([line[:8, :half], line[8:, :half]], axis=1)
                found.append(jnp.concatenate([block, line], axis=0).astype(bf16))
            if cube.inner == 0:
                own_ref[0] = found[0]
                continue
            first = place_ref[2] == 0
            own = jnp.where(first, found[0], found[1])
            other = jnp.where(first, found[1], found[0])
            for order in range(2):
                lanes = slice(order * half, (order + 1) * half)
                at = cube.place(2 * chip, order) ^ place_ref[order]
                own_ref[at, :, lanes] = own[:, lanes]
                other_ref[at, :, lanes] = other[:, lanes]


def qkv_grads(cube, passes, place, pass_index, lefts0, left1, right0, right1, kept, hold=()):
    parts, tokens, high = left1.shape
    width = right0.shape[1]
    specs = [
        pl.BlockSpec((1, tokens, a.shape[2]), lambda i: (i, 0, 0)) for a in (*lefts0, left1)
    ]
    shapes, out_specs = block_shapes(cube, parts * high // cube.count + 8, width)
    return call(
        functools.partial(qkv_grad_kernel, cube, len(lefts0), passes),
        (parts,),
        [pl.BlockSpec(memory_space=pltpu.SMEM)] * 2
        + specs
        + [whole_spec(a) for a in (right0, right1, *kept)],
        out_specs + [pl.BlockSpec((16, width), lambda i: (0, 0))],
        shapes + [sds((16, width), f32)],
        4 * tokens * parts * high * width,
        [place, pass_index, *lefts0, left1, right0, right1, *kept],
        scratch=[pltpu.VMEM((parts * high, width), f32)],
        hold=hold,
    )


def lane_index(shape):
    return lax.broadcasted_iota(jnp.int32, shape, len(shape) - 1)


def split_three(values):
    high = values.astype(bf16)
    rest = values - high.astype(f32)
    middle = rest.astype(bf16)
    low = (rest - middle.astype(f32)).astype(bf16)
    return high, middle, low


def own_lanes(lane, head):
    return (lane < HEAD) if head == 0 else (lane >= HEAD)


def attend_kernel(
    block, q_ref, k_ref, v_ref, live_col_ref, live_row_ref, out_ref, logs_ref, mask_ref
):
    seq = q_ref.shape[0]
    count = seq // block

    @pl.when(pl.program_id(0) == 0)
    def _():
        query = lax.broadcasted_iota(jnp.int32, (block, block), 0)
        key = lax.broadcasted_iota(jnp.int32, (block, block), 1)
        for i in range(count):
            alive = live_row_ref[:, i * block : (i + 1) * block] > 0.5
            visible = (key <= query) & (alive | (key == query))
            mask_ref[i] = jnp.where(visible, 0.0, masked_score)

    lane = lane_index((seq, LANES))
    q = q_ref[...] * 0.125
    k = k_ref[...]
    v = v_ref[...]
    bias = ((live_col_ref[...] - 1.0) * 1e9).astype(bf16)
    zero = jnp.zeros((seq, LANES), bf16)
    one = jnp.ones((seq, LANES), bf16)
    parts = []
    for head in range(2):
        mine = own_lanes(lane, head)
        spare = (1 - head) * HEAD
        parts.append(
            (
                jnp.where(mine, q, zero),
                jnp.where(mine, q, jnp.where(lane == spare, one, zero)),
                jnp.where(mine, k, jnp.where(lane == spare, bias, zero)),
                jnp.where(mine, v, one),
            )
        )
    low = lane_index((block, LANES)) < HEAD

    def score(i, head):
        at, before = slice(i * block, (i + 1) * block), slice(0, i * block)
        q_plain, q_bias, k_bias, _ = parts[head]
        diag = dot_nt(q_plain[at], k[at]) + mask_ref[i]
        return diag, dot_nt(q_bias[at], k_bias[before]) if i > 0 else None

    def soften(diag, off):
        top = jnp.max(diag, axis=-1, keepdims=True)
        if off is None:
            return top, jnp.exp(diag - top).astype(bf16), None
        top = jnp.maximum(top, jnp.max(off, axis=-1, keepdims=True))
        return top, jnp.exp(diag - top).astype(bf16), jnp.exp(off - top).astype(bf16)

    def finish(i, head, top, diag, off):
        at, before = slice(i * block, (i + 1) * block), slice(0, i * block)
        v_ones = parts[head][3]
        total = dot_nn(diag, v_ones[at])
        if i > 0:
            total += dot_nn(off, v_ones[before])
        spare = (1 - head) * HEAD
        weight = total[:, spare : spare + 1]
        found.append((total * (1.0 / weight), top + jnp.log(weight)))
        if head == 1:
            (out0, log0), (out1, log1) = found[-2:]
            out_ref[at, :] = jnp.where(low, out0, out1).astype(bf16)
            logs_ref[at, :] = jnp.where(low, log0, log1)

    found = []
    steps = [(i, head) for i in range(count) for head in range(2)]
    ahead, behind = score(*steps[0]), None
    for place, step in enumerate(steps):
        scored = ahead
        if place + 1 < len(steps):
            ahead = score(*steps[place + 1])
        softened = soften(*scored)
        if behind is not None:
            finish(*steps[place - 1], *behind)
        behind = softened
    finish(*steps[-1], *behind)


def attend(mixed, live_col, live_row, first=0, count=None, hold=(), block=256):
    seq, triple = mixed.shape
    pairs = triple // 3 // LANES
    count = pairs if count is None else count
    width = count * LANES
    block = min(block, seq)

    def cols(offset):
        return pl.BlockSpec((seq, LANES), lambda h: (0, offset + h))

    return call(
        functools.partial(attend_kernel, block),
        (count,),
        [cols(first), cols(first + pairs), cols(first + 2 * pairs), whole_spec(live_col), whole_spec(live_row)],
        [cols(0), cols(0)],
        [sds((seq, width), bf16), sds((seq, width), f32)],
        4 * seq * seq * width,
        [mixed, mixed, mixed, live_col, live_row],
        scratch=[pltpu.VMEM((seq // block, block, block), f32)],
        hold=hold,
    )


def attend_back_kernel(
    block, q_ref, k_ref, v_ref, grad_ref, att_ref, logs_ref, live_col_ref, out_ref,
    mask_ref, dk_ref, dv_ref,
):
    seq = q_ref.shape[0]
    count = seq // block

    @pl.when(pl.program_id(0) == 0)
    def _():
        key = lax.broadcasted_iota(jnp.int32, (block, block), 0)
        query = lax.broadcasted_iota(jnp.int32, (block, block), 1)
        for i in range(count):
            alive = live_col_ref[i * block : (i + 1) * block, :] > 0.5
            visible = (key <= query) & (alive | (key == query))
            mask_ref[i] = jnp.where(visible, 0.0, masked_score)

    lane = lane_index((seq, LANES))
    q = q_ref[...] * 0.125
    k = k_ref[...]
    v = v_ref[...]
    grad = grad_ref[...]
    logs = logs_ref[...]
    dots = grad.astype(f32) * att_ref[...].astype(f32)
    bias = ((live_col_ref[...] - 1.0) * 1e9).astype(bf16)
    zero = jnp.zeros((seq, LANES), bf16)
    one = jnp.ones((seq, LANES), bf16)
    parts = []
    for head in range(2):
        mine = own_lanes(lane, head)
        spare = (1 - head) * HEAD
        log_terms = split_three(-logs[:, head * HEAD : head * HEAD + 1])
        dot_terms = split_three(-jnp.sum(jnp.where(mine, dots, 0.0), axis=-1, keepdims=True))
        q_more, k_more, k_diag, g_more, v_more = (
            jnp.where(lane == spare, one, zero),
            jnp.where(lane == spare, bias, zero),
            zero,
            zero,
            zero,
        )
        for place in range(3):
            here = lane == spare + 1 + place
            q_more = jnp.where(here, log_terms[place], q_more)
            k_more = jnp.where(here, one, k_more)
            k_diag = jnp.where(here, one, k_diag)
            g_more = jnp.where(here, dot_terms[place], g_more)
            v_more = jnp.where(here, one, v_more)
        parts.append(
            dict(
                q=jnp.where(mine, q, q_more),
                k=jnp.where(mine, k, k_more),
                kd=jnp.where(mine, k, k_diag),
                g=jnp.where(mine, grad, g_more),
                v=jnp.where(mine, v, v_more),
                q0=jnp.where(mine, q, zero),
                k0=jnp.where(mine, k, zero),
                g0=jnp.where(mine, grad, zero),
            )
        )
    def rows(i):
        return slice(i * block, (i + 1) * block)

    def score(i, j, head):
        part = parts[head]
        first = dot_nt(part["kd" if j == i else "k"][rows(j)], part["q"][rows(i)])
        return first, dot_nt(part["v"][rows(j)], part["g"][rows(i)])

    def soften(i, j, head, scores, change):
        if j == i:
            scores = scores + mask_ref[i]
        soft = jnp.exp(scores)
        return soft.astype(bf16), (soft * change).astype(bf16)

    def add(name, value):
        totals[name] = totals[name] + value if name in totals else value

    def finish(i, j, head, soft, change):
        part = parts[head]
        add("v", dot_nn(soft, part["g0"][rows(i)]))
        add("k", dot_nn(change, part["q0"][rows(i)]))
        add("q", dot_tn(change, part["k0"][rows(j)]))
        if head == 1:
            for name, ref in (("v", dv_ref), ("k", dk_ref)):
                if j == i:
                    ref[rows(j), :] = totals.pop(name)
                else:
                    ref[rows(j), :] += totals.pop(name)
            if j == i:
                out_ref[0, rows(i), :] = (totals.pop("q") * 0.125).astype(bf16)

    totals = {}
    steps = [(i, j, head) for i in range(count) for j in range(i + 1) for head in range(2)]
    ahead, behind = score(*steps[0]), None
    for place, step in enumerate(steps):
        scored = ahead
        if place + 1 < len(steps):
            ahead = score(*steps[place + 1])
        softened = soften(*step, *scored)
        if behind is not None:
            finish(*steps[place - 1], *behind)
        behind = softened
    finish(*steps[-1], *behind)
    out_ref[1] = dk_ref[...].astype(bf16)
    out_ref[2] = dv_ref[...].astype(bf16)


def attend_back(mixed, att_grad, att, logs, live_col, first=0, count=None, hold=(), block=256):
    seq, triple = mixed.shape
    pairs = triple // 3 // LANES
    count = pairs if count is None else count
    width = count * LANES
    block = min(block, seq)

    def cols(offset):
        return pl.BlockSpec((seq, LANES), lambda h: (0, offset + h))

    return call(
        functools.partial(attend_back_kernel, block),
        (count,),
        [cols(first), cols(first + pairs), cols(first + 2 * pairs)]
        + [cols(first), cols(first), cols(first), whole_spec(live_col)],
        [pl.BlockSpec((3, seq, LANES), lambda h: (0, 0, h))],
        [sds((3, seq, width), bf16)],
        10 * seq * seq * width,
        [mixed, mixed, mixed, att_grad, att, logs, live_col],
        scratch=[
            pltpu.VMEM((seq // block, block, block), f32),
            pltpu.VMEM((seq, LANES), f32),
            pltpu.VMEM((seq, LANES), f32),
        ],
        hold=hold,
    )[0]


def all_masks(bits):
    masks = [0]
    for bit in bits:
        masks += [m | (1 << bit) for m in masks]
    return masks


class Cube:
    def __init__(self):
        inner = lax.axis_size(AXES[1])
        self.count = lax.axis_size(AXES[0]) * inner
        self.bits = self.count.bit_length() - 1
        self.inner = inner.bit_length() - 1
        self.pairs = self.count >> (self.inner > 0)
        self.me = lax.axis_index(AXES)
        self.outer = list(range(self.inner, self.bits))
        self.rest = list(range(1, self.inner))
        self.turns = list(zip(self.outer, self.outer[::-1]))
        self.count_turns = 1 << len(self.outer)
        self.count_line = 1 << len(self.rest)

    def send(self, value, mask):
        return lax.ppermute(value, AXES, [(d, d ^ mask) for d in range(self.count)])

    def send_all(self, value, bits):
        return [self.send(value, mask) for mask in all_masks(bits)[1:]]

    def place(self, device, order):
        bits = [pair[order] for pair in self.turns] + self.rest[::-1]
        found = 0
        for bit in bits:
            found = found * 2 + ((device >> bit) & 1)
        return found

    def places(self):
        return jnp.stack([self.place(self.me, 0), self.place(self.me, 1), self.me & 1, self.me])

    def order(self):
        return sorted(range(self.count), key=lambda d: (d & (self.inner > 0), self.place(d, 0)))

    def turned(self, value):
        count = len(self.turns)
        shape = value.shape
        value = value.reshape((2,) * count + (-1,) + shape[1:])
        axes = tuple(range(count))[::-1] + tuple(range(count, value.ndim))
        return value.transpose(axes).reshape(shape)


class Gather:
    def __init__(self, cube, block, split):
        self.cube, self.split = cube, split
        self.value = block[None]

    def line(self, make=None):
        got = self.cube.send_all(self.value, self.cube.rest)
        if make is not None:
            got = after(got, make)
        self.value = jnp.concatenate([self.value, *got], axis=0)
        self.halves = self.split(self.value)
        self.turns = self.cube.turns[::-1]
        return self.value

    def turn(self, *others):
        if self.turns:
            bits = self.turns.pop(0)
            got = [self.cube.send(v, 1 << bit) for v, bit in zip(self.halves, bits)]
            if others:
                got = after(got, others)
            self.halves = [jnp.concatenate(pair, axis=0) for pair in zip(self.halves, got)]
        return self.halves


def after(value, others):
    return lax.optimization_barrier((value, others))[0]


def across(cube, value):
    return [cube.send(value, 1)] if cube.inner else []


def turn_sum_kernel(count, *refs):
    for half in range(count):
        keep, got = refs[2 * half], refs[2 * half + 1]
        first, second = refs[2 * count + 2 * half], refs[2 * count + 2 * half + 1]
        total = (keep[...].astype(f32) + got[...].astype(f32)).astype(bf16)
        middle = first.shape[0]
        first[...] = total[:middle]
        second[...] = total[middle:]


def join_kernel(lanes, *refs):
    low, low_got, late, late_got = refs[:4]
    for place, out in enumerate(refs[4:]):
        first = (low[place].astype(f32) + low_got[place].astype(f32)).astype(bf16)
        second = (late[place].astype(f32) + late_got[place].astype(f32)).astype(bf16)
        if lanes:
            out[:, : first.shape[1]] = first
            out[:, first.shape[1] :] = second
        else:
            out[: first.shape[0], :] = first
            out[first.shape[0] :, :] = second


class Scatter:
    def __init__(self, cube, keep, send, lanes):
        self.cube, self.keep, self.sent, self.lanes = cube, list(keep), list(send), lanes
        self.todo = list(cube.turns)
        self.got, self.total = [], None
        if self.todo:
            self.go()
        else:
            self.total = jnp.concatenate(self.keep, axis=2 if lanes else 1)[0].astype(f32)

    def go(self):
        bits = self.todo.pop(0)
        self.got = [self.cube.send(v, 1 << bit) for v, bit in zip(self.sent, bits)]
        self.last = not self.todo

    def step(self, *others):
        if self.total is not None:
            return []
        got = after(self.got, others) if others else self.got
        if self.sent is None:
            total = self.keep.astype(f32)
            for other in got:
                total = total + other.astype(f32)
            self.total = total
            return [total]
        pairs = [v for pair in zip(self.keep, got) for v in pair]
        small = all(v.shape[1] % 16 == 0 or v.shape[1] == 72 for v in self.keep)
        if not self.last:
            middle = self.keep[0].shape[0] // 2
            if small:
                shapes = [sds((middle,) + v.shape[1:], bf16) for v in self.keep for _ in range(2)]
                made = call(
                    functools.partial(turn_sum_kernel, 2), (1,), [whole_spec(v) for v in pairs],
                    [whole_spec(v) for v in shapes], shapes, 0, pairs,
                )
            else:
                made = []
                for keep, other in zip(self.keep, got):
                    total = (keep.astype(f32) + other.astype(f32)).astype(bf16)
                    made += [total[:middle], total[middle:]]
            self.keep, self.sent = list(made[0::2]), list(made[1::2])
            self.go()
            return self.sent
        masks = all_masks(self.cube.rest)
        if small:
            first, second = [v.shape[1:] for v in self.keep]
            shape = (first[0], first[1] + second[1]) if self.lanes else (first[0] + second[0], first[1])
            shapes = [sds(shape, bf16)] * len(masks)
            made = call(
                functools.partial(join_kernel, self.lanes), (1,), [whole_spec(v) for v in pairs],
                [whole_spec(v) for v in shapes], shapes, 0, pairs,
            )
        else:
            total = [
                (a.astype(f32) + b.astype(f32)).astype(bf16) for a, b in zip(self.keep, got)
            ]
            total = jnp.concatenate(total, axis=2 if self.lanes else 1)
            made = [total[i] for i in range(len(masks))]
        self.keep, sent = made[0], list(made[1:])
        self.got = [self.cube.send(v, mask) for v, mask in zip(sent, masks[1:])]
        self.sent = None
        return sent

    def result(self):
        while self.total is None:
            self.step()
        return self.total


def after(value, others):
    return lax.optimization_barrier((value, others))[0]


def across(cube, value):
    return [cube.send(value, 1)] if cube.inner else []


def set_down_kernel(cube, sizes, share, place_ref, pass_ref, *refs):
    sources, (wq_ref, wo_ref, norms_ref, emb_ref) = refs[:-4], refs[-4:]
    per = len(sources) // 2
    half = wq_ref.shape[2] // 2
    mid = sizes[0] + sizes[1]
    extra = sources[0].shape[1] - mid
    row = lax.broadcasted_iota(jnp.int32, (extra, 1), 0)
    picked = (row < 8) | (row == 8 + pass_ref[0])
    empty = jnp.zeros((extra, half), f32)
    small = jnp.zeros((extra, 2 * half), f32)
    for device in range(cube.count):
        for order in range(2):
            at = cube.place(device, order) ^ place_ref[order]
            block = sources[order * per][at]
            if per > 1:
                own = ((device & 1) ^ place_ref[2]) == 0
                block = jnp.where(own, block, sources[order * per + 1][at])
            block = block.astype(f32)
            lanes = slice(order * half, (order + 1) * half)
            wq_ref[device, :, lanes] = block[: sizes[0]].astype(bf16)
            wo_ref[device, :, lanes] = block[sizes[0] : mid].astype(bf16)
            if order * half < share:
                line = [jnp.where(picked, block[mid:], 0.0), empty]
                line = jnp.concatenate(line[::-1] if order else line, axis=1)
                small = small + (pltpu.roll(line, device * share, 1) if device else line)
    norms_ref[...] = small[:8]
    emb_ref[...] = jnp.sum(small[8:], axis=0, keepdims=True)


def set_down(cube, place, pass_index, sources, sizes, share):
    width = 2 * sources[0].shape[2]
    shapes = [(cube.count, n, width) for n in sizes]
    wq, wo, norms, emb = call(
        functools.partial(set_down_kernel, cube, sizes, share), (1,),
        [pl.BlockSpec(memory_space=pltpu.SMEM)] * 2 + [whole_spec(a) for a in sources],
        [pl.BlockSpec(n, lambda i: (0, 0, 0)) for n in shapes]
        + [pl.BlockSpec((n, width), lambda i: (0, 0)) for n in (8, 1)],
        [sds(n, bf16) for n in shapes] + [sds((n, width), f32) for n in (8, 1)], 0,
        [place, pass_index, *sources],
    )
    return wq.reshape(-1, width), wo.reshape(-1, width), norms, emb


def body(
    tokens, row_lengths, live_mask, pass_index,
    w_qkv, w_out, w_up, w_down, norm_gains, norm_shifts, pass_table, cotangent,
):
    _, seq, width = tokens.shape
    cube = Cube()
    place = cube.places()
    ff = w_up.shape[1] * cube.count
    block = min(256, seq)
    grid = (seq // block,)
    passes = pass_table.shape[0]

    def split_lanes(v):
        half = v.shape[2] // 2
        return [v[:, :, :half], v[:, :, half:]]

    high = w_up.shape[1]
    share = w_out.shape[1]

    def wide_rows(v):
        return jnp.pad(v, ((0, -v.shape[0] % 8), (0, width - v.shape[1])))

    packed = jnp.concatenate([w_up.T, w_down], axis=0)
    packed = lax.all_gather(packed, AXES, axis=0, tiled=False)

    gains_shifts = wide_rows(jnp.concatenate([norm_gains, norm_shifts], axis=0))
    early = [w_qkv.T, w_out.T, gains_shifts, wide_rows(pass_table)]
    part_q = Gather(cube, jnp.concatenate(early, axis=0), split_lanes)
    part_q.line()
    for _ in cube.turns:
        part_q.turn()
    low, late = part_q.halves
    sources = [low, *across(cube, low), late, *across(cube, late)]
    sizes = (w_qkv.shape[1], w_out.shape[1])
    wq, wo, norms, emb = set_down(cube, place, pass_index, sources, sizes, share)

    positions = jnp.arange(seq, dtype=jnp.int32)
    inside = positions < row_lengths[0]
    live = jnp.where(inside[None, :] & (live_mask[:, 0] > 0), 1.0, 0.0).astype(f32)
    live_cols = [live[0][:, None], live[1][:, None]]
    live_rows = [live[0][None, :], live[1][None, :]]

    x = tokens[0]
    given = cotangent[0]
    rows_w = rows_spec(block, width)
    rows_f = rows_spec(block, ff)
    rows_q = rows_spec(block, 3 * width)
    rows_1 = rows_spec(block, 1)
    rows_3 = pl.BlockSpec((3, block, width), lambda i: (0, i, 0))
    sums_spec = pl.BlockSpec((8, width), lambda i: (0, 0))
    wide = sds((seq, width), f32)
    thin = sds((seq, width), bf16)
    tall = sds((seq, ff), bf16)
    triple = sds((seq, 3 * width), bf16)
    sums_shape = sds((8, width), f32)
    unit = 2 * seq * width

    mixed0, xhat0 = call(
        first_kernel, grid,
        [rows_w, whole_spec(norms), whole_spec(wq)],
        [rows_q, rows_w], [triple, thin], unit * 3 * width, [x, norms, wq],
    )
    pairs = width // LANES
    third = pairs // 3 if pairs % 3 == 0 else pairs
    att0, logs0 = attend(mixed0, live_cols[0], live_rows[0])
    packed = after(packed, att0)
    order, share = cube.order(), high
    if cube.count == 1 or 768 % high or high % 16:
        blocks = [packed[:, at : at + high] for at in (0, high)]
        turned = [
            jnp.take(v, jnp.asarray(order, jnp.int32) ^ cube.me, axis=0).reshape(ff, width)
            for v in blocks
        ]
        packed, share = jnp.concatenate(turned, axis=0)[None], ff
    smem = pl.BlockSpec(memory_space=pltpu.SMEM)
    hidden0, second0, act0, slope0, later, mixed1, xhat1 = call(
        functools.partial(middle_kernel, order, share), grid,
        [smem, whole_spec(packed), rows_w, rows_w, rows_1]
        + [whole_spec(a) for a in (norms, emb, wo, wq)],
        [rows_w, rows_w, rows_f, rows_f, rows_w, rows_q, rows_w],
        [wide, thin, tall, tall, wide, triple, thin],
        unit * (4 * width + 2 * ff),
        [place, packed, att0, x, live_cols[0], norms, emb, wo, wq],
    )
    att1, logs1 = attend(mixed1, live_cols[1], live_rows[1])
    result, second1, act1, drop1, lift1, branch1, hgrad1, agrad1, sums1 = call(
        functools.partial(turn_kernel, order, share), grid,
        [smem, whole_spec(packed), rows_w, rows_w, rows_1, whole_spec(norms), rows_w]
        + [whole_spec(wo)],
        [rows_w, rows_w, rows_f, rows_w, rows_f, rows_w, rows_w, rows_w, sums_spec],
        [thin, thin, tall, thin, tall, thin, wide, thin, sums_shape],
        unit * (2 * width + 4 * ff),
        [place, packed, att1, later, live_cols[1], norms, given, wo],
    )
    mgrad1 = attend_back(mixed1, agrad1, att1, logs1, live_cols[1])
    drop0, lift0, branch0, hgrad0, agrad0, sums0 = call(
        functools.partial(back_kernel, order, share), grid,
        [smem, whole_spec(packed), rows_3, rows_w, rows_w, whole_spec(norms), rows_1, rows_w, rows_f]
        + [whole_spec(a) for a in (wq, wo)],
        [rows_w, rows_f, rows_w, rows_w, rows_w, sums_spec],
        [thin, tall, thin, wide, thin, sums_shape],
        unit * (4 * width + 2 * ff),
        [place, packed, mgrad1, later, hgrad1, norms, live_cols[0], hidden0, slope0, wq, wo],
    )
    chips = cube.pairs * high
    fast = len(cube.turns) == 2 and (cube.count_line * high) % LANES == 0 and high % 32 == 0
    out_own, out_other = out_grads(cube, place, branch0, branch1, att0, att1)
    up_args = (lift0, lift1, second0, second1)
    down_args = (act0, act1, drop0, drop1)

    def split_rows(v):
        start = high // 2
        return [v[:, :start], cube.turned(v[:, start:])]

    def turn_halves(halves):
        middle = cube.pairs // 2
        return [v[:middle] for v in halves], [v[middle:] for v in halves]

    if fast:
        up_other = other_grads(cube, high, *up_args, extra=[out_other])
        (up_got,) = across(cube, up_other)
        down_other = other_grads(cube, high, *down_args, hold=[up_other])
        (down_got,) = across(cube, down_other)
        made = own_grads(cube, high, *up_args, up_got, extra=[out_own], hold=[down_other])
        up_out = Scatter(cube, made[0::2], made[1::2], False)
        made = own_grads(cube, high, *down_args, down_got, hold=made)
        down = Scatter(cube, made[0::2], made[1::2], False)
    else:
        found = []
        for args, more, more_other in ((up_args, out_own, out_other), (down_args, None, None)):
            own = pair_grads(*args, 0, chips)
            if cube.inner:
                got = across(cube, pair_grads(*args, chips, chips))[0]
                own = (own.astype(f32) + got.astype(f32)).astype(bf16)
                if more is not None:
                    got = across(cube, more_other)[0]
                    more = (more.astype(f32) + got.astype(f32)).astype(bf16)
            halves = split_rows(own.reshape(cube.pairs, high, width))
            if more is not None:
                halves[0] = jnp.concatenate([halves[0], more], axis=1)
            keep, send = turn_halves(halves) if cube.turns else (halves, [])
            found.append(Scatter(cube, keep, send, False))
        up_out, down = found
        made = send
    hold = made
    groups = []
    for first in range(0, pairs, third):
        group = attend_back(mixed0, agrad0, att0, logs0, live_cols[0], first, third, hold)
        groups.append(group)
        hold = [group]
        if first == 0:
            hold = hold + up_out.step(group)
        elif first == third:
            hold = hold + down.step(group) + up_out.step(group)
        else:
            hold = hold + down.step(group) + up_out.step(group)
    own, other, small = qkv_grads(
        cube, passes, place, pass_index, groups, mgrad1, xhat0, xhat1,
        [wq, norms, sums0, sums1], hold,
    )
    got = across(cube, other)
    if got:
        own = (own.astype(f32) + got[0].astype(f32)).astype(bf16)
    halves = split_lanes(own)
    keep, send = turn_halves(halves) if cube.turns else (halves, [])
    qkv = Scatter(cube, keep, send, True)
    hold = send
    specs_g = [
        pl.BlockSpec((3, block, a.shape[2]), lambda i: (0, i, 0)) for a in groups
    ]
    input_grad = call(
        functools.partial(last_kernel, len(groups)), grid,
        specs_g + [rows_w, rows_w, whole_spec(norms), whole_spec(wq)],
        [rows_w], [wide], unit * 3 * width,
        [*groups, x, hgrad0, norms, wq],
        hold=hold,
    )[0]
    qkv.step(input_grad)
    down = down.result()
    up_out = up_out.result()
    qkv = qkv.result()
    share = w_out.shape[1]
    count = w_qkv.shape[1]
    if cube.count > 1:
        half = width // 2
        small = jnp.concatenate([qkv[count:, :share], qkv[count:, half : half + share]], axis=0)
    qkv = qkv[:count].T
    low_end = high // 2
    out_end = low_end + share
    up = jnp.concatenate([up_out[:low_end], up_out[out_end:]], axis=0).T
    out = up_out[low_end:out_end].T
    return (
        result[None], input_grad[None], qkv, out, up, down,
        small[:2], small[2], small[3], small[4 : 4 + passes],
    )


def solution(mesh):
    placed = (
        P(AXES, None, None),
        P(AXES),
        P(None, AXES, None),
        P(AXES),
        P(None, AXES),
        P(None, AXES),
        P(None, AXES),
        P(AXES, None),
        P(None, AXES),
        P(None, AXES),
        P(None, AXES),
        P(AXES, None, None),
    )
    return jax.shard_map(
        body,
        mesh=mesh,
        in_specs=placed,
        out_specs=(
            P(AXES, None, None),
            P(AXES, None, None),
            P(None, AXES),
            P(None, AXES),
            P(None, AXES),
            P(AXES, None),
            P(None, AXES),
            P(AXES),
            P(AXES),
            P(None, AXES),
        ),
        check_vma=False,
    )
```

profile of v0, /device:TPU:0, one launch (start us, length us, event | category | flops | bytes accessed | tf_op | source)
XLA Modules:
  0.0 433.3 jit_solution(2921860466392598043)
XLA Ops:
  10.6 5.1 %collective-permute-start.2 = (bf16[1,112,768]{2,1,0:T(8,128)(2,1)S(1)}, bf16[1,112,768]{2,1,0:T(8,128)(2,1)S(1)}, u32[]{:S(2)}, u32[]{:S(2)}) collective-permute-start(bf16[1,112,768]{2,1,0:T(8,128)(2,1)S(1)} %fusion.2), channel_id=1, source_target_pairs={{0,6},{1,7},{2,4},{3,5},{4,2},{5,3},{6,0},{7,1},{8,14},{9,15},{10,... | collective-permute-start | bytes 516104 | tf_op jit(solution)/shard_map/ppermute | solution.py:805
  16.4 4.7 %collective-permute-done.2 = bf16[1,112,768]{2,1,0:T(8,128)(2,1)S(1)} collective-permute-done((bf16[1,112,768]{2,1,0:T(8,128)(2,1)S(1)}, bf16[1,112,768]{2,1,0:T(8,128)(2,1)S(1)}, u32[]{:S(2)}, u32[]{:S(2)}) %collective-permute-start.2) | collective-permute-done | bytes 172064 | tf_op jit(solution)/shard_map/ppermute | solution.py:805
  21.0 15.3 %collective-permute-done.1 = bf16[1,112,768]{2,1,0:T(8,128)(2,1)S(1)} collective-permute-done((bf16[1,112,768]{2,1,0:T(8,128)(2,1)S(1)}, bf16[1,112,768]{2,1,0:T(8,128)(2,1)S(1)}, u32[]{:S(2)}, u32[]{:S(2)}) %collective-permute-start.1) | collective-permute-done | bytes 172064 | tf_op jit(solution)/shard_map/ppermute | solution.py:805
  39.5 5.0 %collective-permute-done.3 = bf16[4,112,384]{2,1,0:T(8,128)(2,1)S(1)} collective-permute-done((bf16[4,112,384]{2,1,0:T(8,128)(2,1)S(1)}, bf16[4,112,384]{2,1,0:T(8,128)(2,1)S(1)}, u32[]{:S(2)}, u32[]{:S(2)}) %collective-permute-start.3) | collective-permute-done | bytes 344096 | tf_op jit(solution)/shard_map/ppermute | solution.py:805
  44.6 3.3 collective-permute-start.4
  47.8 3.9 collective-permute-done.6
  52.0 16.7 %collective-permute-done.4 = bf16[8,112,384]{2,1,0:T(8,128)(2,1)S(1)} collective-permute-done((bf16[8,112,384]{2,1,0:T(8,128)(2,1)S(1)}, bf16[8,112,384]{2,1,0:T(8,128)(2,1)S(1)}, u32[]{:S(2)}, u32[]{:S(2)}) %collective-permute-start.4) | collective-permute-done | bytes 688160 | tf_op jit(solution)/shard_map/ppermute | solution.py:805
  74.4 5.7 %shard_map.195 = (bf16[32,72,768]{2,1,0:T(8,128)(2,1)}, bf16[32,24,768]{2,1,0:T(8,128)(2,1)}, f32[8,768]{1,0:T(8,128)}, f32[1,768]{1,0:T(1,128)}) custom-call(s32[4]{0:T(128)} %pad_add_fusion.refs_0_, s32[1]{0:T(128)S(6)} %copy.35.refs_1_, bf16[16,112,384]{2,1,0:T(8,128)(2,1)} %copy-done, bf16[16,112,384]{2,1,0:T(8,128)(2,1)} %collective-permute-done.5.refs_3_, ...), custom_call_target="tpu_custom_call" | custom-call | bytes 2502 | tf_op jit(solution)/shard_map/pallas_call | solution.py:68
  80.0 8.8 %shard_map.196 = (bf16[1024,2304]{1,0:T(8,128)(2,1)}, bf16[1024,768]{1,0:T(8,128)(2,1)}) custom-call(bf16[1024,768]{1,0:T(8,128)(2,1)} %bitcast.44, f32[8,768]{1,0:T(8,128)} %get-tuple-element.92.refs_1_.refs_5_.refs_9_, bf16[2304,768]{1,0:T(8,128)(2,1)} %bitcast.36), custom_call_target="tpu_custom_call" | custom-call | flops 884736 | bytes 2790 | tf_op jit(solution)/shard_map/pallas_call | solution.py:68
  88.8 16.0 %shard_map.197 = (bf16[1024,768]{1,0:T(8,128)(2,1)}, f32[1024,768]{1,0:T(8,128)}) custom-call(bf16[1024,2304]{1,0:T(8,128)(2,1)} %get-tuple-element.94.refs_0_.refs_1_.refs_2_, bf16[1024,2304]{1,0:T(8,128)(2,1)} %get-tuple-element.94.refs_0_.refs_1_.refs_2_, bf16[1024,2304]{1,0:T(8,128)(2,1)} %get-tuple-element.94.refs_0_.refs_1_.refs_2_, ...), custom_call_target="tpu_custom_call" | custom-call | flops 786432 | bytes 4610 | tf_op jit(solution)/shard_map/pallas_call | solution.py:68
  106.1 28.6 %shard_map.198 = (f32[1024,768]{1,0:T(8,128)}, bf16[1024,768]{1,0:T(8,128)(2,1)}, bf16[1024,3072]{1,0:T(8,128)(2,1)}, bf16[1024,3072]{1,0:T(8,128)(2,1)}, f32[10...) custom-call(s32[4]{0:T(128)} %pad_add_fusion.refs_0_, bf16[32,192,768]{2,1,0:T(8,128)(2,1)} %bitcast.41, ...), custom_call_target="tpu_custom_call" | custom-call | flops 3538944 | bytes 10759 | tf_op jit(solution)/shard_map/pallas_call | solution.py:68
  134.7 16.0 %shard_map.199 = (bf16[1024,768]{1,0:T(8,128)(2,1)}, f32[1024,768]{1,0:T(8,128)}) custom-call(bf16[1024,2304]{1,0:T(8,128)(2,1)} %get-tuple-element.99.refs_0_.refs_1_.refs_2_, bf16[1024,2304]{1,0:T(8,128)(2,1)} %get-tuple-element.99.refs_0_.refs_1_.refs_2_, bf16[1024,2304]{1,0:T(8,128)(2,1)} %get-tuple-element.99.refs_0_.refs_1_.refs_2_, ...), custom_call_target="tpu_custom_call" | custom-call | flops 786432 | bytes 4610 | tf_op jit(solution)/shard_map/pallas_call | solution.py:68
  150.7 35.8 %shard_map.200 = (bf16[1024,768]{1,0:T(8,128)(2,1)}, bf16[1024,768]{1,0:T(8,128)(2,1)}, bf16[1024,3072]{1,0:T(8,128)(2,1)}, bf16[1024,768]{1,0:T(8,128)(2,1)}, b...) custom-call(s32[4]{0:T(128)} %pad_add_fusion.refs_0_, ...), custom_call_target="tpu_custom_call" | custom-call | flops 5308416 | bytes 10285 | tf_op jit(solution)/shard_map/pallas_call | solution.py:68
  186.5 28.0 %shard_map.201.refs_2_.refs_5_ = bf16[3,1024,768]{2,1,0:T(8,128)(2,1)} custom-call(bf16[1024,2304]{1,0:T(8,128)(2,1)} %get-tuple-element.99.refs_0_.refs_1_.refs_2_, bf16[1024,2304]{1,0:T(8,128)(2,1)} %get-tuple-element.99.refs_0_.refs_1_.refs_2_, bf16[1024,2304]{1,0:T(8,128)(2,1)} %get-tuple-element.99.refs_0_.refs_1_.refs_2_, ...), custom_call_target="tpu_custom_call" | custom-call | flops 1966080 | bytes 6145 | tf_op jit(solution)/shard_map/pallas_call | solution.py:68
  214.5 30.2 %shard_map.202 = (bf16[1024,768]{1,0:T(8,128)(2,1)}, bf16[1024,3072]{1,0:T(8,128)(2,1)}, bf16[1024,768]{1,0:T(8,128)(2,1)}, f32[1024,768]{1,0:T(8,128)}, bf16[1024,768]{1,0:T(8,128)(2,1)}, /*index=5*/f32[8,768]{1,0:T(8,128)}) custom-call(s32[4]{0:T(128)} %pad_add_fusion.refs_0_, bf16[32,192,768]{2,1,0:T(8,128)(2,1)} %bitcast.43, ...), custom_call_target="tpu_custom_call" | custom-call | flops 3538944 | bytes 11917 | tf_op jit(solution)/shard_map/pallas_call | solution.py:68
  244.7 6.5 %shard_map.203 = (bf16[16,24,768]{2,1,0:T(8,128)(2,1)}, bf16[16,24,768]{2,1,0:T(8,128)(2,1)}) custom-call(s32[4]{0:T(128)} %pad_add_fusion.refs_0_, bf16[1024,768]{1,0:T(8,128)(2,1)} %get-tuple-element.118.refs_1_, bf16[1024,768]{1,0:T(8,128)(2,1)} %get-tuple-element.119.refs_2_, bf16[1024,768]{1,0:T(8,128)(2,1)} %get-tuple-element.95.refs_2_.refs_3_.refs_4_, ...), custom_call_target="tpu_custom_call" | custom-call | flops 589824 | bytes 1824 | tf_op jit(solution)/shard_map/pallas_call | solution.py:68
  251.2 9.6 %shard_map.204.refs_4_ = bf16[16,120,768]{2,1,0:T(8,128)(2,1)} custom-call(bf16[1024,3072]{1,0:T(8,128)(2,1)} %get-tuple-element.114.refs_0_, bf16[1024,3072]{1,0:T(8,128)(2,1)} %get-tuple-element.115.refs_1_, bf16[1024,768]{1,0:T(8,128)(2,1)} %get-tuple-element.116.refs_2_, bf16[1024,768]{1,0:T(8,128)(2,1)} %get-tuple-element.117.refs_3_, ...), custom_call_target="tpu_custom_call" | custom-call | flops 1179648 | bytes 4704 | tf_op jit(solution)/shard_map/pallas_call | solution.py:68
  261.1 9.1 %shard_map.205.refs_6_ = bf16[16,96,768]{2,1,0:T(8,128)(2,1)} custom-call(bf16[1024,3072]{1,0:T(8,128)(2,1)} %get-tuple-element.110.refs_0_, bf16[1024,3072]{1,0:T(8,128)(2,1)} %get-tuple-element.111.refs_1_, bf16[1024,768]{1,0:T(8,128)(2,1)} %get-tuple-element.112.refs_2_, bf16[1024,768]{1,0:T(8,128)(2,1)} %get-tuple-element.113.refs_3_, ...), custom_call_target="tpu_custom_call" | custom-call | flops 1179648 | bytes 4416 | tf_op jit(solution)/shard_map/pallas_call | solution.py:68
  272.0 10.7 %shard_map.206 = (bf16[8,72,768]{2,1,0:T(8,128)(2,1)}, bf16[8,72,768]{2,1,0:T(8,128)(2,1)}, bf16[8,48,768]{2,1,0:T(8,128)(2,1)}, bf16[8,48,768]{2,1,0:T(8,128)(2,1)}) custom-call(bf16[1024,3072]{1,0:T(8,128)(2,1)} %get-tuple-element.114.refs_0_, bf16[1024,3072]{1,0:T(8,128)(2,1)} %get-tuple-element.115.refs_1_, ...), custom_call_target="tpu_custom_call" | custom-call | flops 1179648 | bytes 5424 | tf_op jit(solution)/shard_map/pallas_call | solution.py:68
  284.8 10.3 %shard_map.207 = (bf16[8,48,768]{2,1,0:T(8,128)(2,1)}, bf16[8,48,768]{2,1,0:T(8,128)(2,1)}, bf16[8,48,768]{2,1,0:T(8,128)(2,1)}, bf16[8,48,768]{2,1,0:T(8,128)(2,1)}) custom-call(bf16[1024,3072]{1,0:T(8,128)(2,1)} %get-tuple-element.110.refs_0_, bf16[1024,3072]{1,0:T(8,128)(2,1)} %get-tuple-element.111.refs_1_, ...), custom_call_target="tpu_custom_call" | custom-call | flops 1179648 | bytes 4992 | tf_op jit(solution)/shard_map/pallas_call | solution.py:68
  297.1 11.5 %shard_map.208.refs_7_.refs_2_.refs_0_ = bf16[3,1024,256]{2,1,0:T(8,128)(2,1)} custom-call(bf16[1024,2304]{1,0:T(8,128)(2,1)} %get-tuple-element.94.refs_0_.refs_1_.refs_2_, bf16[1024,2304]{1,0:T(8,128)(2,1)} %get-tuple-element.94.refs_0_.refs_1_.refs_2_, bf16[1024,2304]{1,0:T(8,128)(2,1)} %get-tuple-element.94.refs_0_.refs_1_.refs_2_, ...), custom_call_target="tpu_custom_call" | custom-call | flops 655360 | bytes 5377 | tf_op jit(solution)/shard_map/pallas_call | solution.py:68
  310.4 3.0 shard_map.209
  315.4 11.3 %shard_map.210.refs_7_.refs_3_.refs_1_ = bf16[3,1024,256]{2,1,0:T(8,128)(2,1)} custom-call(bf16[1024,2304]{1,0:T(8,128)(2,1)} %get-tuple-element.94.refs_0_.refs_1_.refs_2_, bf16[1024,2304]{1,0:T(8,128)(2,1)} %get-tuple-element.94.refs_0_.refs_1_.refs_2_, bf16[1024,2304]{1,0:T(8,128)(2,1)} %get-tuple-element.94.refs_0_.refs_1_.refs_2_, ...), custom_call_target="tpu_custom_call" | custom-call | flops 655360 | bytes 5377 | tf_op jit(solution)/shard_map/pallas_call | solution.py:68
  328.4 2.7 shard_map.211
  340.6 11.6 %shard_map.213.refs_4_.refs_12_.refs_2_ = bf16[3,1024,256]{2,1,0:T(8,128)(2,1)} custom-call(bf16[1024,2304]{1,0:T(8,128)(2,1)} %get-tuple-element.94.refs_0_.refs_1_.refs_2_, bf16[1024,2304]{1,0:T(8,128)(2,1)} %get-tuple-element.94.refs_0_.refs_1_.refs_2_, bf16[1024,2304]{1,0:T(8,128)(2,1)} %get-tuple-element.94.refs_0_.refs_1_.refs_2_, ...), custom_call_target="tpu_custom_call" | custom-call | flops 655360 | bytes 5377 | tf_op jit(solution)/shard_map/pallas_call | solution.py:68
  356.0 18.5 %shard_map.215 = (bf16[16,80,768]{2,1,0:T(8,128)(2,1)}, bf16[16,80,768]{2,1,0:T(8,128)(2,1)}, f32[16,768]{1,0:T(8,128)}) custom-call(s32[4]{0:T(128)} %pad_add_fusion.refs_0_, s32[1]{0:T(128)S(6)} %copy.35.refs_1_, bf16[3,1024,256]{2,1,0:T(8,128)(2,1)} %shard_map.208.refs_7_.refs_2_.refs_0_, bf16[3,1024,256]{2,1,0:T(8,128)(2,1)} %shard_map.210.refs_7_.refs_3_.refs_1_, ...), custom_call_target="tpu_custom_call" | custom-call | flops 1769472 | bytes 4926 | tf_op jit(solution)/shard_map/pallas_call | solution.py:68
  374.6 4.2 collective-permute-done.22
  388.5 9.7 %shard_map.216 = f32[1024,768]{1,0:T(8,128)} custom-call(bf16[3,1024,256]{2,1,0:T(8,128)(2,1)} %shard_map.208.refs_7_.refs_2_.refs_0_, bf16[3,1024,256]{2,1,0:T(8,128)(2,1)} %shard_map.210.refs_7_.refs_3_.refs_1_, bf16[3,1024,256]{2,1,0:T(8,128)(2,1)} %shard_map.213.refs_4_.refs_12_.refs_2_, bf16[1024,768]{1,0:T(8,128)(2,1)} %bitcast.46, ...), custom_call_target="tpu_custom_call" | custom-call | flops 884736 | bytes 3942 | tf_op jit(solution)/shard_map/pallas_call | solution.py:68
  399.1 2.5 shard_map.217
  404.5 3.9 collective-permute-done.25.refs_1_
  412.4 2.5 collective-permute-start.28
  419.2 3.7 collective-permute-done.28
  (137 shorter events, 63.1 us)
Async XLA Ops:
  7.2 98.9 %all-gather.3.cloned.1.call-start = ((), (), s32[]{:S(2)}) async-start(), calls=%async_computation | async-start | bytes 9732096 | tf_op jit(solution)/shard_map/all_gather | solution.py:1029
  10.6 10.4 %collective-permute-start.2 = (bf16[1,112,768]{2,1,0:T(8,128)(2,1)S(1)}, bf16[1,112,768]{2,1,0:T(8,128)(2,1)S(1)}, u32[]{:S(2)}, u32[]{:S(2)}) collective-permute-start(bf16[1,112,768]{2,1,0:T(8,128)(2,1)S(1)} %fusion.2), channel_id=1, source_target_pairs={{0,6},{1,7},{2,4},{3,5},{4,2},{5,3},{6,0},{7,1},{8,14},{9,15},{10,... | collective-permute-start | bytes 516104 | tf_op jit(solution)/shard_map/ppermute | solution.py:805
  15.7 20.6 %collective-permute-start.1 = (bf16[1,112,768]{2,1,0:T(8,128)(2,1)S(1)}, bf16[1,112,768]{2,1,0:T(8,128)(2,1)S(1)}, u32[]{:S(2)}, u32[]{:S(2)}) collective-permute-start(bf16[1,112,768]{2,1,0:T(8,128)(2,1)S(1)} %fusion.2), channel_id=1, source_target_pairs={{0,4},{1,5},{2,6},{3,7},{4,0},{5,1},{6,2},{7,3},{8,12},{9,13},{10,... | collective-permute-start | bytes 516104 | tf_op jit(solution)/shard_map/ppermute | solution.py:805
  15.7 20.6 %collective-permute-start = (bf16[1,112,768]{2,1,0:T(8,128)(2,1)S(1)}, bf16[1,112,768]{2,1,0:T(8,128)(2,1)S(1)}, u32[]{:S(2)}, u32[]{:S(2)}) collective-permute-start(bf16[1,112,768]{2,1,0:T(8,128)(2,1)S(1)} %fusion.2), channel_id=1, source_target_pairs={{0,2},{1,3},{2,0},{3,1},{4,6},{5,7},{6,4},{7,5},{8,10},{9,11},{10,... | collective-permute-start | bytes 516104 | tf_op jit(solution)/shard_map/ppermute | solution.py:805
  36.5 8.0 %collective-permute-start.3 = (bf16[4,112,384]{2,1,0:T(8,128)(2,1)S(1)}, bf16[4,112,384]{2,1,0:T(8,128)(2,1)S(1)}, u32[]{:S(2)}, u32[]{:S(2)}) collective-permute-start(bf16[4,112,384]{2,1,0:T(8,128)(2,1)S(1)} %get-tuple-element.179), channel_id=1, source_target_pairs={{0,16},{1,17},{2,18},{3,19},{4,20},{5,21},{6,22},{7,23},{8,24},{9,... | collective-permute-start | bytes 1032200 | tf_op jit(solution)/shard_map/ppermute | solution.py:805
  38.0 13.8 %collective-permute-start.6 = (bf16[4,112,384]{2,1,0:T(8,128)(2,1)S(1)}, bf16[4,112,384]{2,1,0:T(8,128)(2,1)S(1)}, u32[]{:S(2)}, u32[]{:S(2)}) collective-permute-start(bf16[4,112,384]{2,1,0:T(8,128)(2,1)S(1)} %get-tuple-element.178), channel_id=1, source_target_pairs={{0,8},{1,9},{2,10},{3,11},{4,12},{5,13},{6,14},{7,15},{8,0},{9,1},... | collective-permute-start | bytes 1032200 | tf_op jit(solution)/shard_map/ppermute | solution.py:805
  44.6 24.1 %collective-permute-start.4 = (bf16[8,112,384]{2,1,0:T(8,128)(2,1)S(1)}, bf16[8,112,384]{2,1,0:T(8,128)(2,1)S(1)}, u32[]{:S(2)}, u32[]{:S(2)}) collective-permute-start(bf16[8,112,384]{2,1,0:T(8,128)(2,1)S(1)} %pad_maximum_fusion.3), channel_id=1, source_target_pairs={{0,8},{1,9},{2,10},{3,11},{4,12},{5,13},{6,14},{7,15},{8,0},{9,1},... | collective-permute-start | bytes 2064392 | tf_op jit(solution)/shard_map/ppermute | solution.py:805
  51.9 17.1 %collective-permute-start.7 = (bf16[8,112,384]{2,1,0:T(8,128)(2,1)S(1)}, bf16[8,112,384]{2,1,0:T(8,128)(2,1)S(1)}, u32[]{:S(2)}, u32[]{:S(2)}) collective-permute-start(bf16[8,112,384]{2,1,0:T(8,128)(2,1)S(1)} %pad_maximum_fusion.4), channel_id=1, source_target_pairs={{0,16},{1,17},{2,18},{3,19},{4,20},{5,21},{6,22},{7,23},{8,24},{9,... | collective-permute-start | bytes 2064392 | tf_op jit(solution)/shard_map/ppermute | solution.py:805
  68.9 5.5 %collective-permute-start.5 = (bf16[16,112,384]{2,1,0:T(8,128)(2,1)S(1)}, bf16[16,112,384]{2,1,0:T(8,128)(2,1)}, u32[]{:S(2)}, u32[]{:S(2)}) collective-permute-start(bf16[16,112,384]{2,1,0:T(8,128)(2,1)S(1)} %pad_maximum_fusion.refs_2_), channel_id=1, source_target_pairs={{0,1},{1,0},{2,3},{3,2},{4,5},{5,4},{6,7},{7,6},{8,9},{9,8},{10,11... | collective-permute-start | bytes 4128776 | tf_op jit(solution)/shard_map/ppermute | solution.py:805
  260.8 9.6 %collective-permute-start.10 = (bf16[16,120,768]{2,1,0:T(8,128)(2,1)}, bf16[16,120,768]{2,1,0:T(8,128)(2,1)S(1)}, u32[]{:S(2)}, u32[]{:S(2)}) collective-permute-start(bf16[16,120,768]{2,1,0:T(8,128)(2,1)} %shard_map.204.refs_4_), channel_id=1, source_target_pairs={{0,1},{1,0},{2,3},{3,2},{4,5},{5,4},{6,7},{7,6},{8,9},{9,8},{10,11... | collective-permute-start | bytes 8847368 | tf_op jit(solution)/shard_map/ppermute | solution.py:805
  270.2 14.6 %collective-permute-start.9 = (bf16[16,96,768]{2,1,0:T(8,128)(2,1)}, bf16[16,96,768]{2,1,0:T(8,128)(2,1)}, u32[]{:S(2)}, u32[]{:S(2)}) collective-permute-start(bf16[16,96,768]{2,1,0:T(8,128)(2,1)} %shard_map.205.refs_6_), channel_id=1, source_target_pairs={{0,1},{1,0},{2,3},{3,2},{4,5},{5,4},{6,7},{7,6},{8,9},{9,8},{10,11... | collective-permute-start | bytes 7077896 | tf_op jit(solution)/shard_map/ppermute | solution.py:805
  282.7 25.9 %collective-permute-start.11 = (bf16[8,72,768]{2,1,0:T(8,128)(2,1)}, bf16[8,72,768]{2,1,0:T(8,128)(2,1)S(1)}, u32[]{:S(2)}, u32[]{:S(2)}) collective-permute-start(bf16[8,72,768]{2,1,0:T(8,128)(2,1)} %get-tuple-element.123.refs_6_), channel_id=1, source_target_pairs={{0,8},{1,9},{2,10},{3,11},{4,12},{5,13},{6,14},{7,15},{8,0},{9,1},... | collective-permute-start | bytes 2654216 | tf_op jit(solution)/shard_map/ppermute | solution.py:805
  284.2 24.5 %collective-permute-start.12 = (bf16[8,48,768]{2,1,0:T(8,128)(2,1)}, bf16[8,48,768]{2,1,0:T(8,128)(2,1)S(1)}, u32[]{:S(2)}, u32[]{:S(2)}) collective-permute-start(bf16[8,48,768]{2,1,0:T(8,128)(2,1)} %get-tuple-element.125.refs_8_), channel_id=1, source_target_pairs={{0,16},{1,17},{2,18},{3,19},{4,20},{5,21},{6,22},{7,23},{8,24},{9,... | collective-permute-start | bytes 1769480 | tf_op jit(solution)/shard_map/ppermute | solution.py:805
  295.1 31.6 %collective-permute-start.13 = (bf16[8,48,768]{2,1,0:T(8,128)(2,1)}, bf16[8,48,768]{2,1,0:T(8,128)(2,1)S(1)}, u32[]{:S(2)}, u32[]{:S(2)}) collective-permute-start(bf16[8,48,768]{2,1,0:T(8,128)(2,1)} %get-tuple-element.127.refs_8_), channel_id=1, source_target_pairs={{0,8},{1,9},{2,10},{3,11},{4,12},{5,13},{6,14},{7,15},{8,0},{9,1},... | collective-permute-start | bytes 1769480 | tf_op jit(solution)/shard_map/ppermute | solution.py:805
  296.6 30.2 %collective-permute-start.14 = (bf16[8,48,768]{2,1,0:T(8,128)(2,1)}, bf16[8,48,768]{2,1,0:T(8,128)(2,1)S(1)}, u32[]{:S(2)}, u32[]{:S(2)}) collective-permute-start(bf16[8,48,768]{2,1,0:T(8,128)(2,1)} %get-tuple-element.129.refs_10_), channel_id=1, source_target_pairs={{0,16},{1,17},{2,18},{3,19},{4,20},{5,21},{6,22},{7,23},{8,24},{9,... | collective-permute-start | bytes 1769480 | tf_op jit(solution)/shard_map/ppermute | solution.py:805
  313.4 19.8 %collective-permute-start.15 = (bf16[4,72,768]{2,1,0:T(8,128)(2,1)}, bf16[4,72,768]{2,1,0:T(8,128)(2,1)S(1)}, u32[]{:S(2)}, u32[]{:S(2)}) collective-permute-start(bf16[4,72,768]{2,1,0:T(8,128)(2,1)} %get-tuple-element.132.refs_8_), channel_id=1, source_target_pairs={{0,16},{1,17},{2,18},{3,19},{4,20},{5,21},{6,22},{7,23},{8,24},{9,... | collective-permute-start | bytes 1327112 | tf_op jit(solution)/shard_map/ppermute | solution.py:805
  314.9 18.3 %collective-permute-start.16 = (bf16[4,48,768]{2,1,0:T(8,128)(2,1)}, bf16[4,48,768]{2,1,0:T(8,128)(2,1)S(1)}, u32[]{:S(2)}, u32[]{:S(2)}) collective-permute-start(bf16[4,48,768]{2,1,0:T(8,128)(2,1)} %get-tuple-element.133.refs_9_), channel_id=1, source_target_pairs={{0,8},{1,9},{2,10},{3,11},{4,12},{5,13},{6,14},{7,15},{8,0},{9,1},... | collective-permute-start | bytes 884744 | tf_op jit(solution)/shard_map/ppermute | solution.py:805
  331.1 21.1 %collective-permute-start.17 = (bf16[4,48,768]{2,1,0:T(8,128)(2,1)}, bf16[4,48,768]{2,1,0:T(8,128)(2,1)S(1)}, u32[]{:S(2)}, u32[]{:S(2)}) collective-permute-start(bf16[4,48,768]{2,1,0:T(8,128)(2,1)} %get-tuple-element.136.refs_8_), channel_id=1, source_target_pairs={{0,16},{1,17},{2,18},{3,19},{4,20},{5,21},{6,22},{7,23},{8,24},{9,... | collective-permute-start | bytes 884744 | tf_op jit(solution)/shard_map/ppermute | solution.py:805
  332.5 19.7 %collective-permute-start.18 = (bf16[4,48,768]{2,1,0:T(8,128)(2,1)}, bf16[4,48,768]{2,1,0:T(8,128)(2,1)S(1)}, u32[]{:S(2)}, u32[]{:S(2)}) collective-permute-start(bf16[4,48,768]{2,1,0:T(8,128)(2,1)} %get-tuple-element.137.refs_9_), channel_id=1, source_target_pairs={{0,8},{1,9},{2,10},{3,11},{4,12},{5,13},{6,14},{7,15},{8,0},{9,1},... | collective-permute-start | bytes 884744 | tf_op jit(solution)/shard_map/ppermute | solution.py:805
  336.3 18.9 %collective-permute-start.19 = (bf16[120,768]{1,0:T(8,128)(2,1)}, bf16[120,768]{1,0:T(8,128)(2,1)S(1)}, u32[]{:S(2)}, u32[]{:S(2)}) collective-permute-start(bf16[120,768]{1,0:T(8,128)(2,1)} %get-tuple-element.142.refs_10_), channel_id=1, source_target_pairs={{0,2},{1,3},{2,0},{3,1},{4,6},{5,7},{6,4},{7,5},{8,10},{9,11},{10,... | collective-permute-start | bytes 552968 | tf_op jit(solution)/shard_map/ppermute | solution.py:805
  337.7 17.4 %collective-permute-start.20 = (bf16[120,768]{1,0:T(8,128)(2,1)}, bf16[120,768]{1,0:T(8,128)(2,1)S(1)}, u32[]{:S(2)}, u32[]{:S(2)}) collective-permute-start(bf16[120,768]{1,0:T(8,128)(2,1)} %get-tuple-element.143.refs_11_), channel_id=1, source_target_pairs={{0,4},{1,5},{2,6},{3,7},{4,0},{5,1},{6,2},{7,3},{8,12},{9,13},{10,... | collective-permute-start | bytes 552968 | tf_op jit(solution)/shard_map/ppermute | solution.py:805
  338.7 16.4 %collective-permute-start.21 = (bf16[120,768]{1,0:T(8,128)(2,1)}, bf16[120,768]{1,0:T(8,128)(2,1)S(1)}, u32[]{:S(2)}, u32[]{:S(2)}) collective-permute-start(bf16[120,768]{1,0:T(8,128)(2,1)} %get-tuple-element.144.refs_12_), channel_id=1, source_target_pairs={{0,6},{1,7},{2,4},{3,5},{4,2},{5,3},{6,0},{7,1},{8,14},{9,15},{10,... | collective-permute-start | bytes 552968 | tf_op jit(solution)/shard_map/ppermute | solution.py:805
  382.0 16.1 %collective-permute-start.24 = (bf16[8,80,384]{2,1,0:T(8,128)(2,1)S(1)}, bf16[8,80,384]{2,1,0:T(8,128)(2,1)S(1)}, u32[]{:S(2)}, u32[]{:S(2)}) collective-permute-start(bf16[8,80,384]{2,1,0:T(8,128)(2,1)S(1)} %get-tuple-element.176.refs_8_), channel_id=1, source_target_pairs={{0,16},{1,17},{2,18},{3,19},{4,20},{5,21},{6,22},{7,23},{8,24},{9,... | collective-permute-start | bytes 1474568 | tf_op jit(solution)/shard_map/ppermute | solution.py:805
  383.6 14.6 %collective-permute-start.23 = (bf16[8,80,384]{2,1,0:T(8,128)(2,1)S(1)}, bf16[8,80,384]{2,1,0:T(8,128)(2,1)S(1)}, u32[]{:S(2)}, u32[]{:S(2)}) collective-permute-start(bf16[8,80,384]{2,1,0:T(8,128)(2,1)S(1)} %get-tuple-element.177.refs_7_), channel_id=1, source_target_pairs={{0,8},{1,9},{2,10},{3,11},{4,12},{5,13},{6,14},{7,15},{8,0},{9,1},... | collective-permute-start | bytes 1474568 | tf_op jit(solution)/shard_map/ppermute | solution.py:805
  384.1 19.6 %collective-permute-start.30 = (bf16[96,768]{1,0:T(8,128)(2,1)S(1)}, bf16[96,768]{1,0:T(8,128)(2,1)S(1)}, u32[]{:S(2)}, u32[]{:S(2)}) collective-permute-start(bf16[96,768]{1,0:T(8,128)(2,1)S(1)} %copy-done.21), channel_id=1, source_target_pairs={{0,2},{1,3},{2,0},{3,1},{4,6},{5,7},{6,4},{7,5},{8,10},{9,11},{10,... | collective-permute-start | bytes 442376 | tf_op jit(solution)/shard_map/ppermute | solution.py:805
  384.6 19.0 %collective-permute-start.31 = (bf16[96,768]{1,0:T(8,128)(2,1)S(1)}, bf16[96,768]{1,0:T(8,128)(2,1)S(1)}, u32[]{:S(2)}, u32[]{:S(2)}) collective-permute-start(bf16[96,768]{1,0:T(8,128)(2,1)S(1)} %copy-done.20), channel_id=1, source_target_pairs={{0,4},{1,5},{2,6},{3,7},{4,0},{5,1},{6,2},{7,3},{8,12},{9,13},{10,... | collective-permute-start | bytes 442376 | tf_op jit(solution)/shard_map/ppermute | solution.py:805
  386.9 16.7 %collective-permute-start.32 = (bf16[96,768]{1,0:T(8,128)(2,1)S(1)}, bf16[96,768]{1,0:T(8,128)(2,1)S(1)}, u32[]{:S(2)}, u32[]{:S(2)}) collective-permute-start(bf16[96,768]{1,0:T(8,128)(2,1)S(1)} %copy-done.19), channel_id=1, source_target_pairs={{0,6},{1,7},{2,4},{3,5},{4,2},{5,3},{6,0},{7,1},{8,14},{9,15},{10,... | collective-permute-start | bytes 442376 | tf_op jit(solution)/shard_map/ppermute | solution.py:805
  401.6 6.8 %collective-permute-start.25 = (bf16[4,80,384]{2,1,0:T(8,128)(2,1)}, bf16[4,80,384]{2,1,0:T(8,128)(2,1)S(1)}, u32[]{:S(2)}, u32[]{:S(2)}) collective-permute-start(bf16[4,80,384]{2,1,0:T(8,128)(2,1)} %get-tuple-element.166), channel_id=1, source_target_pairs={{0,16},{1,17},{2,18},{3,19},{4,20},{5,21},{6,22},{7,23},{8,24},{9,... | collective-permute-start | bytes 737288 | tf_op jit(solution)/shard_map/ppermute | solution.py:805
  403.1 6.5 %collective-permute-start.26 = (bf16[4,80,384]{2,1,0:T(8,128)(2,1)}, bf16[4,80,384]{2,1,0:T(8,128)(2,1)S(1)}, u32[]{:S(2)}, u32[]{:S(2)}) collective-permute-start(bf16[4,80,384]{2,1,0:T(8,128)(2,1)} %get-tuple-element.168), channel_id=1, source_target_pairs={{0,8},{1,9},{2,10},{3,11},{4,12},{5,13},{6,14},{7,15},{8,0},{9,1},... | collective-permute-start | bytes 737288 | tf_op jit(solution)/shard_map/ppermute | solution.py:805
  412.4 6.8 %collective-permute-start.27 = (bf16[80,768]{1,0:T(8,128)(2,1)}, bf16[80,768]{1,0:T(8,128)(2,1)S(1)}, u32[]{:S(2)}, u32[]{:S(2)}) collective-permute-start(bf16[80,768]{1,0:T(8,128)(2,1)} %get-tuple-element.170), channel_id=1, source_target_pairs={{0,2},{1,3},{2,0},{3,1},{4,6},{5,7},{6,4},{7,5},{8,10},{9,11},{10,... | collective-permute-start | bytes 368648 | tf_op jit(solution)/shard_map/ppermute | solution.py:805
  412.4 10.5 %collective-permute-start.28 = (bf16[80,768]{1,0:T(8,128)(2,1)}, bf16[80,768]{1,0:T(8,128)(2,1)S(1)}, u32[]{:S(2)}, u32[]{:S(2)}) collective-permute-start(bf16[80,768]{1,0:T(8,128)(2,1)} %get-tuple-element.171), channel_id=1, source_target_pairs={{0,4},{1,5},{2,6},{3,7},{4,0},{5,1},{6,2},{7,3},{8,12},{9,13},{10,... | collective-permute-start | bytes 368648 | tf_op jit(solution)/shard_map/ppermute | solution.py:805
  414.9 8.0 %collective-permute-start.29 = (bf16[80,768]{1,0:T(8,128)(2,1)}, bf16[80,768]{1,0:T(8,128)(2,1)S(1)}, u32[]{:S(2)}, u32[]{:S(2)}) collective-permute-start(bf16[80,768]{1,0:T(8,128)(2,1)} %get-tuple-element.172), channel_id=1, source_target_pairs={{0,6},{1,7},{2,4},{3,5},{4,2},{5,3},{6,0},{7,1},{8,14},{9,15},{10,... | collective-permute-start | bytes 368648 | tf_op jit(solution)/shard_map/ppermute | solution.py:805
  (26 other events, 88.4 us)
Sparse Core Ops, SparseCore 0:
  11.6 94.4 all-gather.2
where the time goes:
time: 437 us; the launch traced here: 433 us
  Pallas kernels  292 us (67%)
  waiting for transfers between devices  61 us (14%)
  starting transfers between devices  38.7 us (9%)
  between operations  16 us (4%)
  local copies, waits for them, and re-layouts  14.7 us (3%)
  other arithmetic  10.5 us (2%)
    pallas_call x24, Pallas kernels, call(): pl.pallas_call(run, grid=grid, in_specs=list(in_specs) + [pl.BlockSpec(me...  292 us
    ppermute x33, waiting for transfers between devices, send(): return lax.ppermute(value, AXES, [(d, d ^ mask) for d in range(self.count)])  59.7 us
    ppermute x33, starting transfers between devices, send(): return lax.ppermute(value, AXES, [(d, d ^ mask) for d in range(self.count)])  38.7 us
  transfers between devices with their start and end apart: 34, of which 11 were waited for; matrix products, arithmetic and copies ran while one was open for 2% of the time, Pallas kernels for 27%

commit v1 on v0

--- a/solution.py
+++ b/solution.py
@@ -18,7 +18,9 @@
 curve_one = 0.7978845608028654
 curve_three = 0.7978845608028654 * 0.044715
 
-VMEM_LIMIT = 60 * 1024 * 1024
+MIB = 1024 * 1024
+VMEM_LIMIT = 52
+LATE_LIMIT = 47
 
 
 def dot_nn(left, right):
@@ -57,7 +59,9 @@
     return value, slope
 
 
-def call(kernel, grid, in_specs, out_specs, out_shape, flops, args, scratch=(), hold=()):
+def call(
+    kernel, grid, in_specs, out_specs, out_shape, flops, args, scratch=(), hold=(), room=VMEM_LIMIT
+):
     moved = sum(a.size * a.dtype.itemsize for a in args)
     moved += sum(o.size * o.dtype.itemsize for o in out_shape)
     given, held = len(args), len(hold)
@@ -73,10 +77,10 @@
         out_shape=out_shape,
         scratch_shapes=list(scratch),
         compiler_params=pltpu.CompilerParams(
-            dimension_semantics=("arbitrary",) * len(grid), vmem_limit_bytes=VMEM_LIMIT
+            dimension_semantics=("arbitrary",) * len(grid), vmem_limit_bytes=room * MIB
         ),
         cost_estimate=pl.CostEstimate(
-            flops=flops // 4096, bytes_accessed=moved // 4096, transcendentals=0
+            flops=flops, bytes_accessed=moved, transcendentals=0
         ),
     )(*args, *hold)
 
@@ -279,7 +283,7 @@
         [sds((size, width), bf16)],
         4 * tokens * size * width,
         [left0, left1, right0, right1],
-        hold=hold,
+        hold=hold, room=LATE_LIMIT,
     )[0]
 
 
@@ -313,7 +317,7 @@
         [sds((cube.pairs, rows, width), bf16)],
         4 * tokens * cube.pairs * high * width,
         [left0, left1, right0, right1, *extra],
-        hold=hold,
+        hold=hold, room=LATE_LIMIT,
     )[0]
 
 
@@ -395,7 +399,7 @@
         [sds((cube.pairs // 2, n, width), bf16) for n in (low, low, late, late)],
         4 * tokens * cube.pairs * high * width,
         [left0, left1, right0, right1, got, *extra],
-        hold=hold,
+        hold=hold, room=LATE_LIMIT,
     )
 
 
@@ -437,19 +441,17 @@
         4 * tokens * high * width,
         [place, *args],
         scratch=[pltpu.VMEM((high, width), f32)],
-        hold=hold,
+        hold=hold, room=LATE_LIMIT,
     )
 
 
 def qkv_grad_kernel(cube, groups, passes, place_ref, pass_ref, *refs):
     lefts0, refs = refs[:groups], refs[groups:]
-    left1, right0, right1, wq_ref, norms_ref, sums0_ref, sums1_ref, own_ref, other_ref = refs[:9]
-    small_ref, total_ref = refs[9:]
+    left1, right0, right1, wq_ref, sums0_ref, sums1_ref, own_ref, other_ref = refs[:8]
+    small_ref, total_ref, count_ref = refs[8:]
     part = pl.program_id(0)
     high = left1.shape[2]
     width = right0.shape[1]
-    gain, shift = norms_ref[0:1, :], norms_ref[2:3, :]
-    ones = jnp.ones((8, right0.shape[0]), bf16)
     row = lax.broadcasted_iota(jnp.int32, (8, 1), 0)
 
     @pl.when(part == 0)
@@ -469,33 +471,38 @@
         to = pl.ds(at, left0.shape[2])
         rows = pl.ds(pl.multiple_of(part * high + at, 8), left0.shape[2])
         total = dot_tn(left0[0], right0[...]) + dot_tn(left1[0, :, to], right1[...])
-        sums = dot_nn(ones, left0[0]) + dot_nn(ones, left1[0, :, to])
-        terms = split_three(sums)
+        total_ref[rows, :] = total
+        sums = jnp.sum(left0[0].astype(f32) + left1[0, :, to].astype(f32), axis=0, keepdims=True)
+        count_ref[pl.ds(part, 1), to] = sums
+        terms = split_three(jnp.broadcast_to(sums, (8, left0.shape[2])))
         three = jnp.where(row == 0, terms[0], jnp.where(row == 1, terms[1], terms[2]))
         three = jnp.where(row < 3, three, jnp.zeros_like(three))
-        shifts = jnp.broadcast_to(shift, (8, width)).astype(bf16)
-        weights = wq_ref[rows, :]
+        weights = wq_ref[to, :]
         gain_sum += jnp.sum(total * weights.astype(f32), axis=0, keepdims=True)
         shift_sum += jnp.sum(dot_nn(three, weights), axis=0, keepdims=True)
-        total_ref[rows, :] = total * gain + dot_tn(three, shifts)
         at += left0.shape[2]
     small_ref[0:1, :] += gain_sum
     small_ref[2:3, :] += shift_sum
 
     @pl.when(part == pl.num_programs(0) - 1)
     def _():
-        extra = 8
+        extra = 16
         rows = own_ref.shape[1] - extra
         share = width // cube.count
         half = width // 2
         small = small_ref[...]
+        counts = jnp.concatenate([count_ref[p : p + 1, :] for p in range(3)], axis=1)
+        counts = jnp.broadcast_to(counts, (8, counts.shape[1]))
         for chip in range(cube.pairs):
             found = []
             for device in range(2 * chip, 2 * chip + 1 + (cube.inner > 0)):
                 block = total_ref[pl.ds(device * rows, rows), :]
                 line = pltpu.roll(small, width - device * share, 1) if device else small
                 line = jnp.concatenate([line[:8, :half], line[8:, :half]], axis=1)
-                found.append(jnp.concatenate([block, line], axis=0).astype(bf16))
+                own = counts
+                if device:
+                    own = pltpu.roll(counts, counts.shape[1] - device * rows, 1)
+                found.append(jnp.concatenate([block, line, own[:, :width]], axis=0).astype(bf16))
             if cube.inner == 0:
                 own_ref[0] = found[0]
                 continue
@@ -515,19 +522,22 @@
     specs = [
         pl.BlockSpec((1, tokens, a.shape[2]), lambda i: (i, 0, 0)) for a in (*lefts0, left1)
     ]
-    shapes, out_specs = block_shapes(cube, parts * high // cube.count + 8, width)
+    shapes, out_specs = block_shapes(cube, parts * high // cube.count + 16, width)
     return call(
         functools.partial(qkv_grad_kernel, cube, len(lefts0), passes),
         (parts,),
         [pl.BlockSpec(memory_space=pltpu.SMEM)] * 2
         + specs
-        + [whole_spec(a) for a in (right0, right1, *kept)],
+        + [whole_spec(a) for a in (right0, right1)]
+        + [rows_spec(high, width)]
+        + [whole_spec(a) for a in kept[1:]],
         out_specs + [pl.BlockSpec((16, width), lambda i: (0, 0))],
         shapes + [sds((16, width), f32)],
         4 * tokens * parts * high * width,
         [place, pass_index, *lefts0, left1, right0, right1, *kept],
-        scratch=[pltpu.VMEM((parts * high, width), f32)],
+        scratch=[pltpu.VMEM((parts * high, width), f32), pltpu.VMEM((8, high), f32)],
         hold=hold,
+        room=LATE_LIMIT,
     )
 
 
@@ -643,7 +653,7 @@
         4 * seq * seq * width,
         [mixed, mixed, mixed, live_col, live_row],
         scratch=[pltpu.VMEM((seq // block, block, block), f32)],
-        hold=hold,
+        hold=hold, room=VMEM_LIMIT,
     )
 
 
@@ -752,7 +762,7 @@
     out_ref[2] = dv_ref[...].astype(bf16)
 
 
-def attend_back(mixed, att_grad, att, logs, live_col, first=0, count=None, hold=(), block=256):
+def attend_back(mixed, att_grad, att, logs, live_col, first=0, count=None, hold=(), block=256, room=VMEM_LIMIT):
     seq, triple = mixed.shape
     pairs = triple // 3 // LANES
     count = pairs if count is None else count
@@ -776,7 +786,7 @@
             pltpu.VMEM((seq, LANES), f32),
             pltpu.VMEM((seq, LANES), f32),
         ],
-        hold=hold,
+        hold=hold, room=room,
     )[0]
 
 
@@ -916,7 +926,7 @@
                 shapes = [sds((middle,) + v.shape[1:], bf16) for v in self.keep for _ in range(2)]
                 made = call(
                     functools.partial(turn_sum_kernel, 2), (1,), [whole_spec(v) for v in pairs],
-                    [whole_spec(v) for v in shapes], shapes, 0, pairs,
+                    [whole_spec(v) for v in shapes], shapes, 0, pairs, room=24,
                 )
             else:
                 made = []
@@ -933,7 +943,7 @@
             shapes = [sds(shape, bf16)] * len(masks)
             made = call(
                 functools.partial(join_kernel, self.lanes), (1,), [whole_spec(v) for v in pairs],
-                [whole_spec(v) for v in shapes], shapes, 0, pairs,
+                [whole_spec(v) for v in shapes], shapes, 0, pairs, room=24,
             )
         else:
             total = [
@@ -1150,7 +1160,9 @@
     hold = made
     groups = []
     for first in range(0, pairs, third):
-        group = attend_back(mixed0, agrad0, att0, logs0, live_cols[0], first, third, hold)
+        group = attend_back(
+            mixed0, agrad0, att0, logs0, live_cols[0], first, third, hold, room=LATE_LIMIT
+        )
         groups.append(group)
         hold = [group]
         if first == 0:
@@ -1161,7 +1173,7 @@
             hold = hold + down.step(group) + up_out.step(group)
     own, other, small = qkv_grads(
         cube, passes, place, pass_index, groups, mgrad1, xhat0, xhat1,
-        [wq, norms, sums0, sums1], hold,
+        [wq, sums0, sums1], hold,
     )
     got = across(cube, other)
     if got:
@@ -1179,6 +1191,7 @@
         [rows_w], [wide], unit * 3 * width,
         [*groups, x, hgrad0, norms, wq],
         hold=hold,
+        room=LATE_LIMIT,
     )[0]
     qkv.step(input_grad)
     down = down.result()
@@ -1188,8 +1201,14 @@
     count = w_qkv.shape[1]
     if cube.count > 1:
         half = width // 2
-        small = jnp.concatenate([qkv[count:, :share], qkv[count:, half : half + share]], axis=0)
-    qkv = qkv[:count].T
+        ends = qkv[count : count + 8]
+        small = jnp.concatenate([ends[:, :share], ends[:, half : half + share]], axis=0)
+    counts = qkv[count + 8, :count]
+    if cube.count == 1:
+        counts = jnp.sum(
+            sum(jnp.concatenate(v, axis=2) for v in (groups, [mgrad1])).astype(f32), axis=1
+        ).reshape(-1)
+    qkv = (qkv[:count] * norms[0:1] + counts[:, None] * norms[2:3]).T
     low_end = high // 2
     out_end = low_end + share
     up = jnp.concatenate([up_out[:low_end], up_out[out_end:]], axis=0).T

time: 437 us -> 407 us (0.931)
  Pallas kernels: 292 us -> 258 us
  waiting for transfers between devices: 61 us -> 68.7 us
  local copies, waits for them, and re-layouts: 14.7 us -> 9.49 us
    pallas_call x24 -> x22, Pallas kernels: 292 us -> 258 us  [call(): pl.pallas_call(run, grid=grid, in_specs=list(in_specs) + [pl.BlockSpec(me...]
  transfers between devices with their start and end apart: 34 -> 34, of which waited for: 11 -> 15; matrix products, arithmetic and copies ran while one was open for 2% -> 2% of each run, Pallas kernels for 27% -> 23%
where the time goes in v1:
time: 407 us; the launch traced here: 404 us
  Pallas kernels  258 us (63%)
  waiting for transfers between devices  68.7 us (17%)
  starting transfers between devices  40.9 us (10%)
  between operations  16 us (4%)
  other arithmetic  10.9 us (3%)
  local copies, waits for them, and re-layouts  9.49 us (2%)
    pallas_call x22, Pallas kernels, call(): pl.pallas_call(run, grid=grid, in_specs=list(in_specs) + [pl.BlockSpec(me...  258 us
    ppermute x33, waiting for transfers between devices, send(): return lax.ppermute(value, AXES, [(d, d ^ mask) for d in range(self.count)])  63 us
    ppermute x33, starting transfers between devices, send(): return lax.ppermute(value, AXES, [(d, d ^ mask) for d in range(self.count)])  40.9 us
  transfers between devices with their start and end apart: 34, of which 15 were waited for; matrix products, arithmetic and copies ran while one was open for 2% of the time, Pallas kernels for 23%

profile of v1, /device:TPU:0, one launch (start us, length us, event | category | flops | bytes accessed | tf_op | source)
XLA Modules:
  0.0 404.0 jit_solution(7565142219908288013)
XLA Ops:
  10.6 3.1 collective-permute-start
  13.7 2.6 collective-permute-start.1
  16.3 4.5 %collective-permute-done = bf16[1,112,768]{2,1,0:T(8,128)(2,1)S(1)} collective-permute-done((bf16[1,112,768]{2,1,0:T(8,128)(2,1)S(1)}, bf16[1,112,768]{2,1,0:T(8,128)(2,1)S(1)}, u32[]{:S(2)}, u32[]{:S(2)}) %collective-permute-start) | collective-permute-done | bytes 172064 | tf_op jit(solution)/shard_map/ppermute | solution.py:815
  20.8 11.4 %collective-permute-done.1 = bf16[1,112,768]{2,1,0:T(8,128)(2,1)S(1)} collective-permute-done((bf16[1,112,768]{2,1,0:T(8,128)(2,1)S(1)}, bf16[1,112,768]{2,1,0:T(8,128)(2,1)S(1)}, u32[]{:S(2)}, u32[]{:S(2)}) %collective-permute-start.1) | collective-permute-done | bytes 172064 | tf_op jit(solution)/shard_map/ppermute | solution.py:815
  35.4 6.3 %collective-permute-done.6 = bf16[4,112,384]{2,1,0:T(8,128)(2,1)S(1)} collective-permute-done((bf16[4,112,384]{2,1,0:T(8,128)(2,1)S(1)}, bf16[4,112,384]{2,1,0:T(8,128)(2,1)S(1)}, u32[]{:S(2)}, u32[]{:S(2)}) %collective-permute-start.6) | collective-permute-done | bytes 344096 | tf_op jit(solution)/shard_map/ppermute | solution.py:815
  46.2 12.6 %collective-permute-done.7 = bf16[8,112,384]{2,1,0:T(8,128)(2,1)S(1)} collective-permute-done((bf16[8,112,384]{2,1,0:T(8,128)(2,1)S(1)}, bf16[8,112,384]{2,1,0:T(8,128)(2,1)S(1)}, u32[]{:S(2)}, u32[]{:S(2)}) %collective-permute-start.7) | collective-permute-done | bytes 688160 | tf_op jit(solution)/shard_map/ppermute | solution.py:815
  59.0 3.8 collective-permute-done.4
  67.6 5.6 %shard_map.195 = (bf16[32,72,768]{2,1,0:T(8,128)(2,1)}, bf16[32,24,768]{2,1,0:T(8,128)(2,1)S(1)}, f32[8,768]{1,0:T(8,128)S(1)}, f32[1,768]{1,0:T(1,128)S(1)}) custom-call(s32[4]{0:T(128)S(1)} %pad_add_fusion.refs_0_, s32[1]{0:T(128)S(6)} %copy.35.refs_1_, bf16[16,112,384]{2,1,0:T(8,128)(2,1)} %pad_maximum_fusion.refs_2_, ...), custom_call_target="tpu_custom_call" | custom-call | bytes 10251284 | tf_op jit(solution)/shard_map/pallas_call | solution.py:72
  73.2 8.6 %shard_map.196 = (bf16[1024,2304]{1,0:T(8,128)(2,1)}, bf16[1024,768]{1,0:T(8,128)(2,1)S(1)}) custom-call(bf16[1024,768]{1,0:T(8,128)(2,1)} %bitcast.58, f32[8,768]{1,0:T(8,128)S(1)} %get-tuple-element.84.refs_1_.refs_5_, bf16[2304,768]{1,0:T(8,128)(2,1)} %bitcast.52), custom_call_target="tpu_custom_call" | custom-call | flops 3623878656 | bytes 11427840 | tf_op jit(solution)/shard_map/pallas_call | solution.py:72
  83.0 15.6 %shard_map.197 = (bf16[1024,768]{1,0:T(8,128)(2,1)}, f32[1024,768]{1,0:T(8,128)}) custom-call(bf16[1024,2304]{1,0:T(8,128)(2,1)} %get-tuple-element.86.refs_0_.refs_1_.refs_2_, bf16[1024,2304]{1,0:T(8,128)(2,1)} %get-tuple-element.86.refs_0_.refs_1_.refs_2_, bf16[1024,2304]{1,0:T(8,128)(2,1)} %get-tuple-element.86.refs_0_.refs_1_.refs_2_, ...), custom_call_target="tpu_custom_call" | custom-call | flops 3221225472 | bytes 18882560 | tf_op jit(solution)/shard_map/pallas_call | solution.py:72
  98.5 5.7 %all-gather.3.cloned.1.call-done = bf16[6144,768]{1,0:T(8,128)(2,1)} async-done(((bf16[192,768]{1,0:T(8,128)(2,1)}), bf16[6144,768]{1,0:T(8,128)(2,1)}) %all-gather.3.cloned.1.call-update) | async-done | bytes 9437200 | tf_op jit(solution)/shard_map/all_gather | solution.py:1039
  104.2 27.9 %shard_map.198 = (f32[1024,768]{1,0:T(8,128)}, bf16[1024,768]{1,0:T(8,128)(2,1)}, bf16[1024,3072]{1,0:T(8,128)(2,1)}, bf16[1024,3072]{1,0:T(8,128)(2,1)}, f32[10...) custom-call(s32[4]{0:T(128)S(1)} %pad_add_fusion.refs_0_, bf16[32,192,768]{2,1,0:T(8,128)(2,1)} %bitcast.64, ...), custom_call_target="tpu_custom_call" | custom-call | flops 14495514624 | bytes 44071952 | tf_op jit(solution)/shard_map/pallas_call | solution.py:72
  132.2 15.7 %shard_map.199 = (bf16[1024,768]{1,0:T(8,128)(2,1)}, f32[1024,768]{1,0:T(8,128)}) custom-call(bf16[1024,2304]{1,0:T(8,128)(2,1)} %get-tuple-element.91.refs_0_.refs_1_.refs_2_, bf16[1024,2304]{1,0:T(8,128)(2,1)} %get-tuple-element.91.refs_0_.refs_1_.refs_2_, bf16[1024,2304]{1,0:T(8,128)(2,1)} %get-tuple-element.91.refs_0_.refs_1_.refs_2_, ...), custom_call_target="tpu_custom_call" | custom-call | flops 3221225472 | bytes 18882560 | tf_op jit(solution)/shard_map/pallas_call | solution.py:72
  147.8 35.6 %shard_map.200 = (bf16[1024,768]{1,0:T(8,128)(2,1)}, bf16[1024,768]{1,0:T(8,128)(2,1)}, bf16[1024,3072]{1,0:T(8,128)(2,1)}, bf16[1024,768]{1,0:T(8,128)(2,1)}, b...) custom-call(s32[4]{0:T(128)S(1)} %pad_add_fusion.refs_0_, ...), custom_call_target="tpu_custom_call" | custom-call | flops 21743271936 | bytes 42127376 | tf_op jit(solution)/shard_map/pallas_call | solution.py:72
  183.4 27.7 %shard_map.201.refs_2_.refs_5_ = bf16[3,1024,768]{2,1,0:T(8,128)(2,1)} custom-call(bf16[1024,2304]{1,0:T(8,128)(2,1)} %get-tuple-element.91.refs_0_.refs_1_.refs_2_, bf16[1024,2304]{1,0:T(8,128)(2,1)} %get-tuple-element.91.refs_0_.refs_1_.refs_2_, bf16[1024,2304]{1,0:T(8,128)(2,1)} %get-tuple-element.91.refs_0_.refs_1_.refs_2_, ...), custom_call_target="tpu_custom_call" | custom-call | flops 8053063680 | bytes 25169920 | tf_op jit(solution)/shard_map/pallas_call | solution.py:72
  211.1 30.3 %shard_map.202 = (bf16[1024,768]{1,0:T(8,128)(2,1)}, bf16[1024,3072]{1,0:T(8,128)(2,1)}, bf16[1024,768]{1,0:T(8,128)(2,1)}, f32[1024,768]{1,0:T(8,128)}, bf16[10...) custom-call(s32[4]{0:T(128)S(1)} %pad_add_fusion.refs_0_, bf16[32,192,768]{2,1,0:T(8,128)(2,1)} %bitcast.66, ...), custom_call_target="tpu_custom_call" | custom-call | flops 14495514624 | bytes 48812048 | tf_op jit(solution)/shard_map/pallas_call | solution.py:72
  242.9 4.2 %shard_map.203 = (bf16[16,24,768]{2,1,0:T(8,128)(2,1)S(1)}, bf16[16,24,768]{2,1,0:T(8,128)(2,1)S(1)}) custom-call(s32[4]{0:T(128)S(1)} %pad_add_fusion.refs_0_, bf16[1024,768]{1,0:T(8,128)(2,1)S(1)} %copy-done.14, bf16[1024,768]{1,0:T(8,128)(2,1)S(1)} %copy-done.13, bf16[1024,768]{1,0:T(8,128)(2,1)S(1)} %copy-done, ...), custom_call_target="tpu_custom_call" | custom-call | flops 2415919104 | bytes 7471120 | tf_op jit(solution)/shard_map/pallas_call | solution.py:72
  247.1 7.4 %shard_map.204.refs_4_ = bf16[16,120,768]{2,1,0:T(8,128)(2,1)S(1)} custom-call(bf16[1024,3072]{1,0:T(8,128)(2,1)} %get-tuple-element.106.refs_0_, bf16[1024,3072]{1,0:T(8,128)(2,1)} %get-tuple-element.107.refs_1_, bf16[1024,768]{1,0:T(8,128)(2,1)S(1)} %copy-done.11, bf16[1024,768]{1,0:T(8,128)(2,1)S(1)} %copy-done.12, ...), custom_call_target="tpu_custom_call" | custom-call | flops 4831838208 | bytes 19267584 | tf_op jit(solution)/shard_map/pallas_call | solution.py:72
  256.1 7.1 %shard_map.205.refs_6_ = bf16[16,96,768]{2,1,0:T(8,128)(2,1)S(1)} custom-call(bf16[1024,3072]{1,0:T(8,128)(2,1)} %get-tuple-element.102.refs_0_, bf16[1024,3072]{1,0:T(8,128)(2,1)} %get-tuple-element.103.refs_1_, bf16[1024,768]{1,0:T(8,128)(2,1)S(1)} %copy-done.10, bf16[1024,768]{1,0:T(8,128)(2,1)S(1)} %copy-done.9, bf16[16,120,768]{2,1,0:T(8,128)(2,1)} %copy-done.7), custom_call_target="tpu_custom_call" | custom-call | flops 4831838208 | bytes 18087936 | tf_op jit(solution)/shard_map/pallas_call | solution.py:72
  265.5 8.0 %shard_map.206 = (bf16[8,72,768]{2,1,0:T(8,128)(2,1)S(1)}, bf16[8,72,768]{2,1,0:T(8,128)(2,1)S(1)}, bf16[8,48,768]{2,1,0:T(8,128)(2,1)S(1)}, bf16[8,48,768]{2,1,0:T(8,128)(2,1)S(1)}) custom-call(bf16[1024,3072]{1,0:T(8,128)(2,1)} %get-tuple-element.106.refs_0_, bf16[1024,3072]{1,0:T(8,128)(2,1)} %get-tuple-element.107.refs_1_, ...), custom_call_target="tpu_custom_call" | custom-call | flops 4831838208 | bytes 22216704 | tf_op jit(solution)/shard_map/pallas_call | solution.py:72
  275.7 8.6 %shard_map.207 = (bf16[8,48,768]{2,1,0:T(8,128)(2,1)S(1)}, bf16[8,48,768]{2,1,0:T(8,128)(2,1)S(1)}, bf16[8,48,768]{2,1,0:T(8,128)(2,1)S(1)}, bf16[8,48,768]{2,1,0:T(8,128)(2,1)S(1)}) custom-call(bf16[1024,3072]{1,0:T(8,128)(2,1)} %get-tuple-element.102.refs_0_, bf16[1024,3072]{1,0:T(8,128)(2,1)} %get-tuple-element.103.refs_1_, ...), custom_call_target="tpu_custom_call" | custom-call | flops 4831838208 | bytes 20447232 | tf_op jit(solution)/shard_map/pallas_call | solution.py:72
  286.4 10.4 %shard_map.208.refs_7_.refs_2_.refs_0_ = bf16[3,1024,256]{2,1,0:T(8,128)(2,1)S(1)} custom-call(bf16[1024,2304]{1,0:T(8,128)(2,1)} %get-tuple-element.86.refs_0_.refs_1_.refs_2_, bf16[1024,2304]{1,0:T(8,128)(2,1)} %get-tuple-element.86.refs_0_.refs_1_.refs_2_, bf16[1024,2304]{1,0:T(8,128)(2,1)} %get-tuple-element.86.refs_0_.refs_1_.refs_2_, ...), custom_call_target="tpu_custom_call" | custom-call | flops 2684354560 | bytes 22024192 | tf_op jit(solution)/shard_map/pallas_call | solution.py:72
  300.5 10.1 %shard_map.210.refs_7_.refs_3_.refs_1_ = bf16[3,1024,256]{2,1,0:T(8,128)(2,1)S(1)} custom-call(bf16[1024,2304]{1,0:T(8,128)(2,1)} %get-tuple-element.86.refs_0_.refs_1_.refs_2_, bf16[1024,2304]{1,0:T(8,128)(2,1)} %get-tuple-element.86.refs_0_.refs_1_.refs_2_, bf16[1024,2304]{1,0:T(8,128)(2,1)} %get-tuple-element.86.refs_0_.refs_1_.refs_2_, ...), custom_call_target="tpu_custom_call" | custom-call | flops 2684354560 | bytes 22024192 | tf_op jit(solution)/shard_map/pallas_call | solution.py:72
  319.7 10.5 %shard_map.213.refs_4_.refs_11_.refs_2_ = bf16[3,1024,256]{2,1,0:T(8,128)(2,1)S(1)} custom-call(bf16[1024,2304]{1,0:T(8,128)(2,1)} %get-tuple-element.86.refs_0_.refs_1_.refs_2_, bf16[1024,2304]{1,0:T(8,128)(2,1)} %get-tuple-element.86.refs_0_.refs_1_.refs_2_, bf16[1024,2304]{1,0:T(8,128)(2,1)} %get-tuple-element.86.refs_0_.refs_1_.refs_2_, ...), custom_call_target="tpu_custom_call" | custom-call | flops 2684354560 | bytes 22024192 | tf_op jit(solution)/shard_map/pallas_call | solution.py:72
  332.5 14.8 %shard_map.215 = (bf16[16,88,768]{2,1,0:T(8,128)(2,1)}, bf16[16,88,768]{2,1,0:T(8,128)(2,1)}, f32[16,768]{1,0:T(8,128)}) custom-call(s32[4]{0:T(128)S(1)} %pad_add_fusion.refs_0_, s32[1]{0:T(128)S(6)} %copy.35.refs_1_, bf16[3,1024,256]{2,1,0:T(8,128)(2,1)S(1)} %copy-done.3, bf16[3,1024,256]{2,1,0:T(8,128)(2,1)S(1)} %copy-done.6, ...), custom_call_target="tpu_custom_call" | custom-call | flops 7247757312 | bytes 20545556 | tf_op jit(solution)/shard_map/pallas_call | solution.py:72
  347.3 4.5 %collective-permute-done.22 = bf16[16,88,768]{2,1,0:T(8,128)(2,1)S(1)} collective-permute-done((bf16[16,88,768]{2,1,0:T(8,128)(2,1)}, bf16[16,88,768]{2,1,0:T(8,128)(2,1)S(1)}, u32[]{:S(2)}, u32[]{:S(2)}) %collective-permute-start.22) | collective-permute-done | bytes 2162720 | tf_op jit(solution)/shard_map/ppermute | solution.py:815
  351.8 2.2 add_convert_fusion
  356.1 2.9 collective-permute-start.30
  361.5 8.9 %shard_map.216 = f32[1024,768]{1,0:T(8,128)} custom-call(bf16[3,1024,256]{2,1,0:T(8,128)(2,1)S(1)} %copy-done.3, bf16[3,1024,256]{2,1,0:T(8,128)(2,1)S(1)} %copy-done.6, bf16[3,1024,256]{2,1,0:T(8,128)(2,1)S(1)} %shard_map.213.refs_4_.refs_11_.refs_2_, bf16[1024,768]{1,0:T(8,128)(2,1)} %bitcast.60, f32[1024,768]{1,0:T(8,128)} %get-tuple-element.137.refs_4_, ...), custom_call_target="tpu_custom_call" | custom-call | flops 3623878656 | bytes 16146432 | tf_op jit(solution)/shard_map/pallas_call | solution.py:72
  375.0 3.2 collective-permute-done.26
  380.4 2.8 collective-permute-start.27
  387.0 7.3 %collective-permute-done.28 = bf16[88,768]{1,0:T(8,128)(2,1)S(1)} collective-permute-done((bf16[88,768]{1,0:T(8,128)(2,1)S(1)}, bf16[88,768]{1,0:T(8,128)(2,1)S(1)}, u32[]{:S(2)}, u32[]{:S(2)}) %collective-permute-start.28) | collective-permute-done | bytes 135200 | tf_op jit(solution)/shard_map/ppermute | solution.py:815
  (135 shorter events, 58.1 us)
Async XLA Ops:
  7.2 97.0 %all-gather.3.cloned.1.call-start = ((), (), s32[]{:S(2)}) async-start(), calls=%async_computation | async-start | bytes 9732096 | tf_op jit(solution)/shard_map/all_gather | solution.py:1039
  10.6 10.2 %collective-permute-start = (bf16[1,112,768]{2,1,0:T(8,128)(2,1)S(1)}, bf16[1,112,768]{2,1,0:T(8,128)(2,1)S(1)}, u32[]{:S(2)}, u32[]{:S(2)}) collective-permute-start(bf16[1,112,768]{2,1,0:T(8,128)(2,1)S(1)} %fusion.6), channel_id=1, source_target_pairs={{0,2},{1,3},{2,0},{3,1},{4,6},{5,7},{6,4},{7,5},{8,10},{9,11},{10,... | collective-permute-start | bytes 516104 | tf_op jit(solution)/shard_map/ppermute | solution.py:815
  13.7 18.5 %collective-permute-start.1 = (bf16[1,112,768]{2,1,0:T(8,128)(2,1)S(1)}, bf16[1,112,768]{2,1,0:T(8,128)(2,1)S(1)}, u32[]{:S(2)}, u32[]{:S(2)}) collective-permute-start(bf16[1,112,768]{2,1,0:T(8,128)(2,1)S(1)} %fusion.6), channel_id=1, source_target_pairs={{0,4},{1,5},{2,6},{3,7},{4,0},{5,1},{6,2},{7,3},{8,12},{9,13},{10,... | collective-permute-start | bytes 516104 | tf_op jit(solution)/shard_map/ppermute | solution.py:815
  16.3 15.9 %collective-permute-start.2 = (bf16[1,112,768]{2,1,0:T(8,128)(2,1)S(1)}, bf16[1,112,768]{2,1,0:T(8,128)(2,1)S(1)}, u32[]{:S(2)}, u32[]{:S(2)}) collective-permute-start(bf16[1,112,768]{2,1,0:T(8,128)(2,1)S(1)} %fusion.6), channel_id=1, source_target_pairs={{0,6},{1,7},{2,4},{3,5},{4,2},{5,3},{6,0},{7,1},{8,14},{9,15},{10,... | collective-permute-start | bytes 516104 | tf_op jit(solution)/shard_map/ppermute | solution.py:815
  32.3 9.4 %collective-permute-start.6 = (bf16[4,112,384]{2,1,0:T(8,128)(2,1)S(1)}, bf16[4,112,384]{2,1,0:T(8,128)(2,1)S(1)}, u32[]{:S(2)}, u32[]{:S(2)}) collective-permute-start(bf16[4,112,384]{2,1,0:T(8,128)(2,1)S(1)} %get-tuple-element.164), channel_id=1, source_target_pairs={{0,8},{1,9},{2,10},{3,11},{4,12},{5,13},{6,14},{7,15},{8,0},{9,1},... | collective-permute-start | bytes 1032200 | tf_op jit(solution)/shard_map/ppermute | solution.py:815
  33.9 11.0 %collective-permute-start.3 = (bf16[4,112,384]{2,1,0:T(8,128)(2,1)S(1)}, bf16[4,112,384]{2,1,0:T(8,128)(2,1)S(1)}, u32[]{:S(2)}, u32[]{:S(2)}) collective-permute-start(bf16[4,112,384]{2,1,0:T(8,128)(2,1)S(1)} %get-tuple-element.165), channel_id=1, source_target_pairs={{0,16},{1,17},{2,18},{3,19},{4,20},{5,21},{6,22},{7,23},{8,24},{9,... | collective-permute-start | bytes 1032200 | tf_op jit(solution)/shard_map/ppermute | solution.py:815
  41.8 16.9 %collective-permute-start.7 = (bf16[8,112,384]{2,1,0:T(8,128)(2,1)S(1)}, bf16[8,112,384]{2,1,0:T(8,128)(2,1)S(1)}, u32[]{:S(2)}, u32[]{:S(2)}) collective-permute-start(bf16[8,112,384]{2,1,0:T(8,128)(2,1)S(1)} %pad_maximum_fusion.4), channel_id=1, source_target_pairs={{0,16},{1,17},{2,18},{3,19},{4,20},{5,21},{6,22},{7,23},{8,24},{9,... | collective-permute-start | bytes 2064392 | tf_op jit(solution)/shard_map/ppermute | solution.py:815
  45.0 17.9 %collective-permute-start.4 = (bf16[8,112,384]{2,1,0:T(8,128)(2,1)S(1)}, bf16[8,112,384]{2,1,0:T(8,128)(2,1)S(1)}, u32[]{:S(2)}, u32[]{:S(2)}) collective-permute-start(bf16[8,112,384]{2,1,0:T(8,128)(2,1)S(1)} %pad_maximum_fusion.3), channel_id=1, source_target_pairs={{0,8},{1,9},{2,10},{3,11},{4,12},{5,13},{6,14},{7,15},{8,0},{9,1},... | collective-permute-start | bytes 2064392 | tf_op jit(solution)/shard_map/ppermute | solution.py:815
  59.0 7.0 %collective-permute-start.8 = (bf16[16,112,384]{2,1,0:T(8,128)(2,1)S(1)}, bf16[16,112,384]{2,1,0:T(8,128)(2,1)}, u32[]{:S(2)}, u32[]{:S(2)}) collective-permute-start(bf16[16,112,384]{2,1,0:T(8,128)(2,1)S(1)} %pad_maximum_fusion.1.refs_4_), channel_id=1, source_target_pairs={{0,1},{1,0},{2,3},{3,2},{4,5},{5,4},{6,7},{7,6},{8,9},{9,8},{10,11... | collective-permute-start | bytes 4128776 | tf_op jit(solution)/shard_map/ppermute | solution.py:815
  254.5 9.0 %collective-permute-start.10 = (bf16[16,120,768]{2,1,0:T(8,128)(2,1)S(1)}, bf16[16,120,768]{2,1,0:T(8,128)(2,1)S(1)}, u32[]{:S(2)}, u32[]{:S(2)}) collective-permute-start(bf16[16,120,768]{2,1,0:T(8,128)(2,1)S(1)} %shard_map.204.refs_4_), channel_id=1, source_target_pairs={{0,1},{1,0},{2,3},{3,2},{4,5},{5,4},{6,7},{7,6},{8,9},{9,8},{10,11... | collective-permute-start | bytes 8847368 | tf_op jit(solution)/shard_map/ppermute | solution.py:815
  263.2 12.5 %collective-permute-start.9 = (bf16[16,96,768]{2,1,0:T(8,128)(2,1)S(1)}, bf16[16,96,768]{2,1,0:T(8,128)(2,1)}, u32[]{:S(2)}, u32[]{:S(2)}) collective-permute-start(bf16[16,96,768]{2,1,0:T(8,128)(2,1)S(1)} %shard_map.205.refs_6_), channel_id=1, source_target_pairs={{0,1},{1,0},{2,3},{3,2},{4,5},{5,4},{6,7},{7,6},{8,9},{9,8},{10,11... | collective-permute-start | bytes 7077896 | tf_op jit(solution)/shard_map/ppermute | solution.py:815
  273.6 24.4 %collective-permute-start.11 = (bf16[8,72,768]{2,1,0:T(8,128)(2,1)S(1)}, bf16[8,72,768]{2,1,0:T(8,128)(2,1)S(1)}, u32[]{:S(2)}, u32[]{:S(2)}) collective-permute-start(bf16[8,72,768]{2,1,0:T(8,128)(2,1)S(1)} %get-tuple-element.115.refs_6_), channel_id=1, source_target_pairs={{0,8},{1,9},{2,10},{3,11},{4,12},{5,13},{6,14},{7,15},{8,0},{9,1},... | collective-permute-start | bytes 2654216 | tf_op jit(solution)/shard_map/ppermute | solution.py:815
  275.1 22.9 %collective-permute-start.12 = (bf16[8,48,768]{2,1,0:T(8,128)(2,1)S(1)}, bf16[8,48,768]{2,1,0:T(8,128)(2,1)S(1)}, u32[]{:S(2)}, u32[]{:S(2)}) collective-permute-start(bf16[8,48,768]{2,1,0:T(8,128)(2,1)S(1)} %get-tuple-element.117.refs_8_), channel_id=1, source_target_pairs={{0,16},{1,17},{2,18},{3,19},{4,20},{5,21},{6,22},{7,23},{8,24},{9,... | collective-permute-start | bytes 1769480 | tf_op jit(solution)/shard_map/ppermute | solution.py:815
  284.4 26.2 %collective-permute-start.13 = (bf16[8,48,768]{2,1,0:T(8,128)(2,1)S(1)}, bf16[8,48,768]{2,1,0:T(8,128)(2,1)S(1)}, u32[]{:S(2)}, u32[]{:S(2)}) collective-permute-start(bf16[8,48,768]{2,1,0:T(8,128)(2,1)S(1)} %get-tuple-element.119.refs_8_), channel_id=1, source_target_pairs={{0,8},{1,9},{2,10},{3,11},{4,12},{5,13},{6,14},{7,15},{8,0},{9,1},... | collective-permute-start | bytes 1769480 | tf_op jit(solution)/shard_map/ppermute | solution.py:815
  285.8 24.8 %collective-permute-start.14 = (bf16[8,48,768]{2,1,0:T(8,128)(2,1)S(1)}, bf16[8,48,768]{2,1,0:T(8,128)(2,1)S(1)}, u32[]{:S(2)}, u32[]{:S(2)}) collective-permute-start(bf16[8,48,768]{2,1,0:T(8,128)(2,1)S(1)} %get-tuple-element.121.refs_10_), channel_id=1, source_target_pairs={{0,16},{1,17},{2,18},{3,19},{4,20},{5,21},{6,22},{7,23},{8,24},{9,... | collective-permute-start | bytes 1769480 | tf_op jit(solution)/shard_map/ppermute | solution.py:815
  298.3 16.8 %collective-permute-start.15 = (bf16[4,72,768]{2,1,0:T(8,128)(2,1)S(1)}, bf16[4,72,768]{2,1,0:T(8,128)(2,1)S(1)}, u32[]{:S(2)}, u32[]{:S(2)}) collective-permute-start(bf16[4,72,768]{2,1,0:T(8,128)(2,1)S(1)} %get-tuple-element.124.refs_8_), channel_id=1, source_target_pairs={{0,16},{1,17},{2,18},{3,19},{4,20},{5,21},{6,22},{7,23},{8,24},{9,... | collective-permute-start | bytes 1327112 | tf_op jit(solution)/shard_map/ppermute | solution.py:815
  299.8 15.2 %collective-permute-start.16 = (bf16[4,48,768]{2,1,0:T(8,128)(2,1)S(1)}, bf16[4,48,768]{2,1,0:T(8,128)(2,1)S(1)}, u32[]{:S(2)}, u32[]{:S(2)}) collective-permute-start(bf16[4,48,768]{2,1,0:T(8,128)(2,1)S(1)} %get-tuple-element.125.refs_9_), channel_id=1, source_target_pairs={{0,8},{1,9},{2,10},{3,11},{4,12},{5,13},{6,14},{7,15},{8,0},{9,1},... | collective-permute-start | bytes 884744 | tf_op jit(solution)/shard_map/ppermute | solution.py:815
  310.9 19.3 %collective-permute-start.17 = (bf16[4,48,768]{2,1,0:T(8,128)(2,1)S(1)}, bf16[4,48,768]{2,1,0:T(8,128)(2,1)S(1)}, u32[]{:S(2)}, u32[]{:S(2)}) collective-permute-start(bf16[4,48,768]{2,1,0:T(8,128)(2,1)S(1)} %get-tuple-element.128.refs_8_), channel_id=1, source_target_pairs={{0,16},{1,17},{2,18},{3,19},{4,20},{5,21},{6,22},{7,23},{8,24},{9,... | collective-permute-start | bytes 884744 | tf_op jit(solution)/shard_map/ppermute | solution.py:815
  312.4 17.8 %collective-permute-start.18 = (bf16[4,48,768]{2,1,0:T(8,128)(2,1)S(1)}, bf16[4,48,768]{2,1,0:T(8,128)(2,1)S(1)}, u32[]{:S(2)}, u32[]{:S(2)}) collective-permute-start(bf16[4,48,768]{2,1,0:T(8,128)(2,1)S(1)} %get-tuple-element.129.refs_9_), channel_id=1, source_target_pairs={{0,8},{1,9},{2,10},{3,11},{4,12},{5,13},{6,14},{7,15},{8,0},{9,1},... | collective-permute-start | bytes 884744 | tf_op jit(solution)/shard_map/ppermute | solution.py:815
  315.2 15.1 %collective-permute-start.19 = (bf16[120,768]{1,0:T(8,128)(2,1)S(1)}, bf16[120,768]{1,0:T(8,128)(2,1)S(1)}, u32[]{:S(2)}, u32[]{:S(2)}) collective-permute-start(bf16[120,768]{1,0:T(8,128)(2,1)S(1)} %get-tuple-element.134.refs_10_), channel_id=1, source_target_pairs={{0,2},{1,3},{2,0},{3,1},{4,6},{5,7},{6,4},{7,5},{8,10},{9,11},{10,... | collective-permute-start | bytes 552968 | tf_op jit(solution)/shard_map/ppermute | solution.py:815
  316.8 15.6 %collective-permute-start.20 = (bf16[120,768]{1,0:T(8,128)(2,1)S(1)}, bf16[120,768]{1,0:T(8,128)(2,1)S(1)}, u32[]{:S(2)}, u32[]{:S(2)}) collective-permute-start(bf16[120,768]{1,0:T(8,128)(2,1)S(1)} %get-tuple-element.135.refs_11_), channel_id=1, source_target_pairs={{0,4},{1,5},{2,6},{3,7},{4,0},{5,1},{6,2},{7,3},{8,12},{9,13},{10,... | collective-permute-start | bytes 552968 | tf_op jit(solution)/shard_map/ppermute | solution.py:815
  317.8 14.6 %collective-permute-start.21 = (bf16[120,768]{1,0:T(8,128)(2,1)S(1)}, bf16[120,768]{1,0:T(8,128)(2,1)S(1)}, u32[]{:S(2)}, u32[]{:S(2)}) collective-permute-start(bf16[120,768]{1,0:T(8,128)(2,1)S(1)} %get-tuple-element.136.refs_12_), channel_id=1, source_target_pairs={{0,6},{1,7},{2,4},{3,5},{4,2},{5,3},{6,0},{7,1},{8,14},{9,15},{10,... | collective-permute-start | bytes 552968 | tf_op jit(solution)/shard_map/ppermute | solution.py:815
  354.1 16.3 %collective-permute-start.23 = (bf16[8,88,384]{2,1,0:T(8,128)(2,1)S(1)}, bf16[8,88,384]{2,1,0:T(8,128)(2,1)S(1)}, u32[]{:S(2)}, u32[]{:S(2)}) collective-permute-start(bf16[8,88,384]{2,1,0:T(8,128)(2,1)S(1)} %get-tuple-element.163.refs_7_), channel_id=1, source_target_pairs={{0,8},{1,9},{2,10},{3,11},{4,12},{5,13},{6,14},{7,15},{8,0},{9,1},... | collective-permute-start | bytes 1622024 | tf_op jit(solution)/shard_map/ppermute | solution.py:815
  355.6 14.8 %collective-permute-start.24 = (bf16[8,88,384]{2,1,0:T(8,128)(2,1)S(1)}, bf16[8,88,384]{2,1,0:T(8,128)(2,1)S(1)}, u32[]{:S(2)}, u32[]{:S(2)}) collective-permute-start(bf16[8,88,384]{2,1,0:T(8,128)(2,1)S(1)} %get-tuple-element.162.refs_8_), channel_id=1, source_target_pairs={{0,16},{1,17},{2,18},{3,19},{4,20},{5,21},{6,22},{7,23},{8,24},{9,... | collective-permute-start | bytes 1622024 | tf_op jit(solution)/shard_map/ppermute | solution.py:815
  356.1 16.1 %collective-permute-start.30 = (bf16[96,768]{1,0:T(8,128)(2,1)S(1)}, bf16[96,768]{1,0:T(8,128)(2,1)S(1)}, u32[]{:S(2)}, u32[]{:S(2)}) collective-permute-start(bf16[96,768]{1,0:T(8,128)(2,1)S(1)} %get-tuple-element.146.refs_12_), channel_id=1, source_target_pairs={{0,2},{1,3},{2,0},{3,1},{4,6},{5,7},{6,4},{7,5},{8,10},{9,11},{10,... | collective-permute-start | bytes 442376 | tf_op jit(solution)/shard_map/ppermute | solution.py:815
  359.0 13.7 %collective-permute-start.31 = (bf16[96,768]{1,0:T(8,128)(2,1)S(1)}, bf16[96,768]{1,0:T(8,128)(2,1)S(1)}, u32[]{:S(2)}, u32[]{:S(2)}) collective-permute-start(bf16[96,768]{1,0:T(8,128)(2,1)S(1)} %get-tuple-element.147.refs_13_), channel_id=1, source_target_pairs={{0,4},{1,5},{2,6},{3,7},{4,0},{5,1},{6,2},{7,3},{8,12},{9,13},{10,... | collective-permute-start | bytes 442376 | tf_op jit(solution)/shard_map/ppermute | solution.py:815
  359.7 13.1 %collective-permute-start.32 = (bf16[96,768]{1,0:T(8,128)(2,1)S(1)}, bf16[96,768]{1,0:T(8,128)(2,1)S(1)}, u32[]{:S(2)}, u32[]{:S(2)}) collective-permute-start(bf16[96,768]{1,0:T(8,128)(2,1)S(1)} %get-tuple-element.148.refs_14_), channel_id=1, source_target_pairs={{0,6},{1,7},{2,4},{3,5},{4,2},{5,3},{6,0},{7,1},{8,14},{9,15},{10,... | collective-permute-start | bytes 442376 | tf_op jit(solution)/shard_map/ppermute | solution.py:815
  370.7 7.5 %collective-permute-start.26 = (bf16[4,88,384]{2,1,0:T(8,128)(2,1)S(1)}, bf16[4,88,384]{2,1,0:T(8,128)(2,1)S(1)}, u32[]{:S(2)}, u32[]{:S(2)}) collective-permute-start(bf16[4,88,384]{2,1,0:T(8,128)(2,1)S(1)} %slice.141), channel_id=1, source_target_pairs={{0,8},{1,9},{2,10},{3,11},{4,12},{5,13},{6,14},{7,15},{8,0},{9,1},... | collective-permute-start | bytes 811016 | tf_op jit(solution)/shard_map/ppermute | solution.py:815
  373.6 6.7 %collective-permute-start.25 = (bf16[4,88,384]{2,1,0:T(8,128)(2,1)S(1)}, bf16[4,88,384]{2,1,0:T(8,128)(2,1)S(1)}, u32[]{:S(2)}, u32[]{:S(2)}) collective-permute-start(bf16[4,88,384]{2,1,0:T(8,128)(2,1)S(1)} %slice.138), channel_id=1, source_target_pairs={{0,16},{1,17},{2,18},{3,19},{4,20},{5,21},{6,22},{7,23},{8,24},{9,... | collective-permute-start | bytes 811016 | tf_op jit(solution)/shard_map/ppermute | solution.py:815
  380.4 6.6 %collective-permute-start.27 = (bf16[88,768]{1,0:T(8,128)(2,1)S(1)}, bf16[88,768]{1,0:T(8,128)(2,1)S(1)}, u32[]{:S(2)}, u32[]{:S(2)}) collective-permute-start(bf16[88,768]{1,0:T(8,128)(2,1)S(1)} %get-tuple-element.166), channel_id=1, source_target_pairs={{0,2},{1,3},{2,0},{3,1},{4,6},{5,7},{6,4},{7,5},{8,10},{9,11},{10,... | collective-permute-start | bytes 405512 | tf_op jit(solution)/shard_map/ppermute | solution.py:815
  383.2 11.1 %collective-permute-start.28 = (bf16[88,768]{1,0:T(8,128)(2,1)S(1)}, bf16[88,768]{1,0:T(8,128)(2,1)S(1)}, u32[]{:S(2)}, u32[]{:S(2)}) collective-permute-start(bf16[88,768]{1,0:T(8,128)(2,1)S(1)} %get-tuple-element.168), channel_id=1, source_target_pairs={{0,4},{1,5},{2,6},{3,7},{4,0},{5,1},{6,2},{7,3},{8,12},{9,13},{10,... | collective-permute-start | bytes 405512 | tf_op jit(solution)/shard_map/ppermute | solution.py:815
  383.9 10.5 %collective-permute-start.29 = (bf16[88,768]{1,0:T(8,128)(2,1)S(1)}, bf16[88,768]{1,0:T(8,128)(2,1)S(1)}, u32[]{:S(2)}, u32[]{:S(2)}) collective-permute-start(bf16[88,768]{1,0:T(8,128)(2,1)S(1)} %get-tuple-element.167), channel_id=1, source_target_pairs={{0,6},{1,7},{2,4},{3,5},{4,2},{5,3},{6,0},{7,1},{8,14},{9,15},{10,... | collective-permute-start | bytes 405512 | tf_op jit(solution)/shard_map/ppermute | solution.py:815
  (22 other events, 163.5 us)
Sparse Core Ops, SparseCore 0:
  11.6 92.5 all-gather.2

commit v2 on v1

--- a/solution.py
+++ b/solution.py
@@ -486,7 +486,7 @@
 
     @pl.when(part == pl.num_programs(0) - 1)
     def _():
-        extra = 16
+        extra = 8
         rows = own_ref.shape[1] - extra
         share = width // cube.count
         half = width // 2
@@ -497,12 +497,13 @@
             found = []
             for device in range(2 * chip, 2 * chip + 1 + (cube.inner > 0)):
                 block = total_ref[pl.ds(device * rows, rows), :]
-                line = pltpu.roll(small, width - device * share, 1) if device else small
-                line = jnp.concatenate([line[:8, :half], line[8:, :half]], axis=1)
-                own = counts
+                line, own = small, counts
                 if device:
+                    line = pltpu.roll(small, width - device * share, 1)
                     own = pltpu.roll(counts, counts.shape[1] - device * rows, 1)
-                found.append(jnp.concatenate([block, line, own[:, :width]], axis=0).astype(bf16))
+                line = [line[:8, :LANES], own[:, : half - LANES], line[8:, :half]]
+                line = jnp.concatenate(line, axis=1)
+                found.append(jnp.concatenate([block, line], axis=0).astype(bf16))
             if cube.inner == 0:
                 own_ref[0] = found[0]
                 continue
@@ -522,7 +523,7 @@
     specs = [
         pl.BlockSpec((1, tokens, a.shape[2]), lambda i: (i, 0, 0)) for a in (*lefts0, left1)
     ]
-    shapes, out_specs = block_shapes(cube, parts * high // cube.count + 16, width)
+    shapes, out_specs = block_shapes(cube, parts * high // cube.count + 8, width)
     return call(
         functools.partial(qkv_grad_kernel, cube, len(lefts0), passes),
         (parts,),
@@ -891,6 +892,14 @@
         else:
             out[: first.shape[0], :] = first
             out[first.shape[0] :, :] = second
+
+
+def core_sum_kernel(own, got, *outs):
+    middle, _, half = outs[0].shape
+    for order in range(2):
+        for part in range(2):
+            at = (slice(part * middle, (part + 1) * middle), slice(None), slice(order * half, (order + 1) * half))
+            outs[2 * order + part][...] = (own[at].astype(f32) + got[at].astype(f32)).astype(bf16)
 
 
 class Scatter:
@@ -1176,10 +1185,18 @@
         [wq, sums0, sums1], hold,
     )
     got = across(cube, other)
-    if got:
-        own = (own.astype(f32) + got[0].astype(f32)).astype(bf16)
-    halves = split_lanes(own)
-    keep, send = turn_halves(halves) if cube.turns else (halves, [])
+    if got and cube.turns and own.shape[1] % 16 == 0:
+        shapes = [sds((cube.pairs // 2, own.shape[1], width // 2), bf16)] * 4
+        made = call(
+            core_sum_kernel, (1,), [whole_spec(own)] * 2, [whole_spec(v) for v in shapes],
+            shapes, 0, [own, got[0]], room=24,
+        )
+        keep, send = made[0::2], made[1::2]
+    else:
+        if got:
+            own = (own.astype(f32) + got[0].astype(f32)).astype(bf16)
+        halves = split_lanes(own)
+        keep, send = turn_halves(halves) if cube.turns else (halves, [])
     qkv = Scatter(cube, keep, send, True)
     hold = send
     specs_g = [
@@ -1203,7 +1220,7 @@
         half = width // 2
         ends = qkv[count : count + 8]
         small = jnp.concatenate([ends[:, :share], ends[:, half : half + share]], axis=0)
-    counts = qkv[count + 8, :count]
+    counts = qkv[count, LANES : LANES + count]
     if cube.count == 1:
         counts = jnp.sum(
             sum(jnp.concatenate(v, axis=2) for v in (groups, [mgrad1])).astype(f32), axis=1

time: 407 us -> 402 us (0.988)
    unnamed x40 -> x42, local copies, waits for them, and re-layouts: 7.02 us -> 8.55 us
    pallas_call x22 -> x25, Pallas kernels: 258 us -> 259 us  [call(): pl.pallas_call(run, grid=grid, in_specs=list(in_specs) + [pl.BlockSpec(me...]
  transfers between devices with their start and end apart: 34 -> 34, of which waited for: 15 -> 15; matrix products, arithmetic and copies ran while one was open for 2% -> 2% of each run, Pallas kernels for 23% -> 24%
where the time goes in v2:
time: 402 us; the launch traced here: 398 us
  Pallas kernels  259 us (64%)
  waiting for transfers between devices  65.6 us (16%)
  starting transfers between devices  39.2 us (10%)
  between operations  16 us (4%)
  local copies, waits for them, and re-layouts  10.9 us (3%)
  other arithmetic  8.16 us (2%)
    pallas_call x25, Pallas kernels, call(): pl.pallas_call(run, grid=grid, in_specs=list(in_specs) + [pl.BlockSpec(me...  259 us
    ppermute x33, waiting for transfers between devices, send(): return lax.ppermute(value, AXES, [(d, d ^ mask) for d in range(self.count)])  59.9 us
    ppermute x33, starting transfers between devices, send(): return lax.ppermute(value, AXES, [(d, d ^ mask) for d in range(self.count)])  39.2 us
    unnamed x42, local copies, waits for them, and re-layouts  8.55 us
  transfers between devices with their start and end apart: 34, of which 15 were waited for; matrix products, arithmetic and copies ran while one was open for 2% of the time, Pallas kernels for 24%

profile of v2, /device:TPU:0, one launch (start us, length us, event | category | flops | bytes accessed | tf_op | source)
XLA Modules:
  0.0 398.4 jit_solution(12749527179121740497)
XLA Ops:
  10.6 3.1 collective-permute-start
  13.7 2.6 collective-permute-start.1
  16.3 4.5 %collective-permute-done = bf16[1,112,768]{2,1,0:T(8,128)(2,1)S(1)} collective-permute-done((bf16[1,112,768]{2,1,0:T(8,128)(2,1)S(1)}, bf16[1,112,768]{2,1,0:T(8,128)(2,1)S(1)}, u32[]{:S(2)}, u32[]{:S(2)}) %collective-permute-start) | collective-permute-done | bytes 172064 | tf_op jit(solution)/shard_map/ppermute | solution.py:816
  20.8 11.4 %collective-permute-done.1 = bf16[1,112,768]{2,1,0:T(8,128)(2,1)S(1)} collective-permute-done((bf16[1,112,768]{2,1,0:T(8,128)(2,1)S(1)}, bf16[1,112,768]{2,1,0:T(8,128)(2,1)S(1)}, u32[]{:S(2)}, u32[]{:S(2)}) %collective-permute-start.1) | collective-permute-done | bytes 172064 | tf_op jit(solution)/shard_map/ppermute | solution.py:816
  35.4 6.3 %collective-permute-done.6 = bf16[4,112,384]{2,1,0:T(8,128)(2,1)S(1)} collective-permute-done((bf16[4,112,384]{2,1,0:T(8,128)(2,1)S(1)}, bf16[4,112,384]{2,1,0:T(8,128)(2,1)S(1)}, u32[]{:S(2)}, u32[]{:S(2)}) %collective-permute-start.6) | collective-permute-done | bytes 344096 | tf_op jit(solution)/shard_map/ppermute | solution.py:816
  46.2 12.6 %collective-permute-done.7 = bf16[8,112,384]{2,1,0:T(8,128)(2,1)S(1)} collective-permute-done((bf16[8,112,384]{2,1,0:T(8,128)(2,1)S(1)}, bf16[8,112,384]{2,1,0:T(8,128)(2,1)S(1)}, u32[]{:S(2)}, u32[]{:S(2)}) %collective-permute-start.7) | collective-permute-done | bytes 688160 | tf_op jit(solution)/shard_map/ppermute | solution.py:816
  59.0 3.8 collective-permute-done.4
  67.6 5.6 %shard_map.195 = (bf16[32,72,768]{2,1,0:T(8,128)(2,1)}, bf16[32,24,768]{2,1,0:T(8,128)(2,1)S(1)}, f32[8,768]{1,0:T(8,128)S(1)}, f32[1,768]{1,0:T(1,128)S(1)}) custom-call(s32[4]{0:T(128)S(1)} %pad_add_fusion.refs_0_, s32[1]{0:T(128)S(6)} %copy.35.refs_1_, bf16[16,112,384]{2,1,0:T(8,128)(2,1)} %pad_maximum_fusion.refs_2_, ...), custom_call_target="tpu_custom_call" | custom-call | bytes 10251284 | tf_op jit(solution)/shard_map/pallas_call | solution.py:72
  73.2 8.6 %shard_map.196 = (bf16[1024,2304]{1,0:T(8,128)(2,1)}, bf16[1024,768]{1,0:T(8,128)(2,1)S(1)}) custom-call(bf16[1024,768]{1,0:T(8,128)(2,1)} %bitcast.47, f32[8,768]{1,0:T(8,128)S(1)} %get-tuple-element.96.refs_1_.refs_5_, bf16[2304,768]{1,0:T(8,128)(2,1)} %bitcast.41), custom_call_target="tpu_custom_call" | custom-call | flops 3623878656 | bytes 11427840 | tf_op jit(solution)/shard_map/pallas_call | solution.py:72
  83.0 15.6 %shard_map.197 = (bf16[1024,768]{1,0:T(8,128)(2,1)}, f32[1024,768]{1,0:T(8,128)}) custom-call(bf16[1024,2304]{1,0:T(8,128)(2,1)} %get-tuple-element.98.refs_0_.refs_1_.refs_2_, bf16[1024,2304]{1,0:T(8,128)(2,1)} %get-tuple-element.98.refs_0_.refs_1_.refs_2_, bf16[1024,2304]{1,0:T(8,128)(2,1)} %get-tuple-element.98.refs_0_.refs_1_.refs_2_, ...), custom_call_target="tpu_custom_call" | custom-call | flops 3221225472 | bytes 18882560 | tf_op jit(solution)/shard_map/pallas_call | solution.py:72
  98.5 5.7 %all-gather.3.cloned.1.call-done = bf16[6144,768]{1,0:T(8,128)(2,1)} async-done(((bf16[192,768]{1,0:T(8,128)(2,1)}), bf16[6144,768]{1,0:T(8,128)(2,1)}) %all-gather.3.cloned.1.call-update) | async-done | bytes 9437200 | tf_op jit(solution)/shard_map/all_gather | solution.py:1048
  104.2 28.0 %shard_map.198 = (f32[1024,768]{1,0:T(8,128)}, bf16[1024,768]{1,0:T(8,128)(2,1)}, bf16[1024,3072]{1,0:T(8,128)(2,1)}, bf16[1024,3072]{1,0:T(8,128)(2,1)}, f32[10...) custom-call(s32[4]{0:T(128)S(1)} %pad_add_fusion.refs_0_, bf16[32,192,768]{2,1,0:T(8,128)(2,1)} %bitcast.53, ...), custom_call_target="tpu_custom_call" | custom-call | flops 14495514624 | bytes 44071952 | tf_op jit(solution)/shard_map/pallas_call | solution.py:72
  132.2 15.7 %shard_map.199 = (bf16[1024,768]{1,0:T(8,128)(2,1)}, f32[1024,768]{1,0:T(8,128)}) custom-call(bf16[1024,2304]{1,0:T(8,128)(2,1)} %get-tuple-element.103.refs_0_.refs_1_.refs_2_, bf16[1024,2304]{1,0:T(8,128)(2,1)} %get-tuple-element.103.refs_0_.refs_1_.refs_2_, bf16[1024,2304]{1,0:T(8,128)(2,1)} %get-tuple-element.103.refs_0_.refs_1_.refs_2_, ...), custom_call_target="tpu_custom_call" | custom-call | flops 3221225472 | bytes 18882560 | tf_op jit(solution)/shard_map/pallas_call | solution.py:72
  147.9 35.6 %shard_map.200 = (bf16[1024,768]{1,0:T(8,128)(2,1)}, bf16[1024,768]{1,0:T(8,128)(2,1)}, bf16[1024,3072]{1,0:T(8,128)(2,1)}, bf16[1024,768]{1,0:T(8,128)(2,1)}, b...) custom-call(s32[4]{0:T(128)S(1)} %pad_add_fusion.refs_0_, ...), custom_call_target="tpu_custom_call" | custom-call | flops 21743271936 | bytes 42127376 | tf_op jit(solution)/shard_map/pallas_call | solution.py:72
  183.5 27.8 %shard_map.201.refs_2_.refs_5_ = bf16[3,1024,768]{2,1,0:T(8,128)(2,1)} custom-call(bf16[1024,2304]{1,0:T(8,128)(2,1)} %get-tuple-element.103.refs_0_.refs_1_.refs_2_, bf16[1024,2304]{1,0:T(8,128)(2,1)} %get-tuple-element.103.refs_0_.refs_1_.refs_2_, bf16[1024,2304]{1,0:T(8,128)(2,1)} %get-tuple-element.103.refs_0_.refs_1_.refs_2_, ...), custom_call_target="tpu_custom_call" | custom-call | flops 8053063680 | bytes 25169920 | tf_op jit(solution)/shard_map/pallas_call | solution.py:72
  211.3 30.3 %shard_map.202 = (bf16[1024,768]{1,0:T(8,128)(2,1)}, bf16[1024,3072]{1,0:T(8,128)(2,1)}, bf16[1024,768]{1,0:T(8,128)(2,1)}, f32[1024,768]{1,0:T(8,128)}, bf16[10...) custom-call(s32[4]{0:T(128)S(1)} %pad_add_fusion.refs_0_, bf16[32,192,768]{2,1,0:T(8,128)(2,1)} %bitcast.55, ...), custom_call_target="tpu_custom_call" | custom-call | flops 14495514624 | bytes 48812048 | tf_op jit(solution)/shard_map/pallas_call | solution.py:72
  243.0 4.2 %shard_map.203 = (bf16[16,24,768]{2,1,0:T(8,128)(2,1)S(1)}, bf16[16,24,768]{2,1,0:T(8,128)(2,1)S(1)}) custom-call(s32[4]{0:T(128)S(1)} %pad_add_fusion.refs_0_, bf16[1024,768]{1,0:T(8,128)(2,1)S(1)} %copy-done.15, bf16[1024,768]{1,0:T(8,128)(2,1)S(1)} %copy-done.14, bf16[1024,768]{1,0:T(8,128)(2,1)S(1)} %copy-done, ...), custom_call_target="tpu_custom_call" | custom-call | flops 2415919104 | bytes 7471120 | tf_op jit(solution)/shard_map/pallas_call | solution.py:72
  247.3 7.3 %shard_map.204.refs_4_ = bf16[16,120,768]{2,1,0:T(8,128)(2,1)S(1)} custom-call(bf16[1024,3072]{1,0:T(8,128)(2,1)} %get-tuple-element.118.refs_0_, bf16[1024,3072]{1,0:T(8,128)(2,1)} %get-tuple-element.119.refs_1_, bf16[1024,768]{1,0:T(8,128)(2,1)S(1)} %copy-done.11, bf16[1024,768]{1,0:T(8,128)(2,1)S(1)} %copy-done.12, ...), custom_call_target="tpu_custom_call" | custom-call | flops 4831838208 | bytes 19267584 | tf_op jit(solution)/shard_map/pallas_call | solution.py:72
  256.2 7.1 %shard_map.205.refs_6_ = bf16[16,96,768]{2,1,0:T(8,128)(2,1)S(1)} custom-call(bf16[1024,3072]{1,0:T(8,128)(2,1)} %get-tuple-element.114.refs_0_, bf16[1024,3072]{1,0:T(8,128)(2,1)} %get-tuple-element.115.refs_1_, bf16[1024,768]{1,0:T(8,128)(2,1)S(1)} %copy-done.10, bf16[1024,768]{1,0:T(8,128)(2,1)S(1)} %copy-done.9, bf16[16,120,768]{2,1,0:T(8,128)(2,1)} %copy-done.7), custom_call_target="tpu_custom_call" | custom-call | flops 4831838208 | bytes 18087936 | tf_op jit(solution)/shard_map/pallas_call | solution.py:72
  265.6 8.0 %shard_map.206 = (bf16[8,72,768]{2,1,0:T(8,128)(2,1)S(1)}, bf16[8,72,768]{2,1,0:T(8,128)(2,1)S(1)}, bf16[8,48,768]{2,1,0:T(8,128)(2,1)S(1)}, bf16[8,48,768]{2,1,0:T(8,128)(2,1)S(1)}) custom-call(bf16[1024,3072]{1,0:T(8,128)(2,1)} %get-tuple-element.118.refs_0_, bf16[1024,3072]{1,0:T(8,128)(2,1)} %get-tuple-element.119.refs_1_, ...), custom_call_target="tpu_custom_call" | custom-call | flops 4831838208 | bytes 22216704 | tf_op jit(solution)/shard_map/pallas_call | solution.py:72
  275.7 8.6 %shard_map.207 = (bf16[8,48,768]{2,1,0:T(8,128)(2,1)S(1)}, bf16[8,48,768]{2,1,0:T(8,128)(2,1)S(1)}, bf16[8,48,768]{2,1,0:T(8,128)(2,1)S(1)}, bf16[8,48,768]{2,1,0:T(8,128)(2,1)S(1)}) custom-call(bf16[1024,3072]{1,0:T(8,128)(2,1)} %get-tuple-element.114.refs_0_, bf16[1024,3072]{1,0:T(8,128)(2,1)} %get-tuple-element.115.refs_1_, ...), custom_call_target="tpu_custom_call" | custom-call | flops 4831838208 | bytes 20447232 | tf_op jit(solution)/shard_map/pallas_call | solution.py:72
  286.4 10.4 %shard_map.208.refs_7_.refs_2_.refs_0_ = bf16[3,1024,256]{2,1,0:T(8,128)(2,1)S(1)} custom-call(bf16[1024,2304]{1,0:T(8,128)(2,1)} %get-tuple-element.98.refs_0_.refs_1_.refs_2_, bf16[1024,2304]{1,0:T(8,128)(2,1)} %get-tuple-element.98.refs_0_.refs_1_.refs_2_, bf16[1024,2304]{1,0:T(8,128)(2,1)} %get-tuple-element.98.refs_0_.refs_1_.refs_2_, ...), custom_call_target="tpu_custom_call" | custom-call | flops 2684354560 | bytes 22024192 | tf_op jit(solution)/shard_map/pallas_call | solution.py:72
  300.4 10.1 %shard_map.210.refs_7_.refs_3_.refs_1_ = bf16[3,1024,256]{2,1,0:T(8,128)(2,1)S(1)} custom-call(bf16[1024,2304]{1,0:T(8,128)(2,1)} %get-tuple-element.98.refs_0_.refs_1_.refs_2_, bf16[1024,2304]{1,0:T(8,128)(2,1)} %get-tuple-element.98.refs_0_.refs_1_.refs_2_, bf16[1024,2304]{1,0:T(8,128)(2,1)} %get-tuple-element.98.refs_0_.refs_1_.refs_2_, ...), custom_call_target="tpu_custom_call" | custom-call | flops 2684354560 | bytes 22024192 | tf_op jit(solution)/shard_map/pallas_call | solution.py:72
  312.9 2.1 collective-permute-done.16.refs_3_
  319.7 10.5 %shard_map.213.refs_4_.refs_11_.refs_2_ = bf16[3,1024,256]{2,1,0:T(8,128)(2,1)S(1)} custom-call(bf16[1024,2304]{1,0:T(8,128)(2,1)} %get-tuple-element.98.refs_0_.refs_1_.refs_2_, bf16[1024,2304]{1,0:T(8,128)(2,1)} %get-tuple-element.98.refs_0_.refs_1_.refs_2_, bf16[1024,2304]{1,0:T(8,128)(2,1)} %get-tuple-element.98.refs_0_.refs_1_.refs_2_, ...), custom_call_target="tpu_custom_call" | custom-call | flops 2684354560 | bytes 22024192 | tf_op jit(solution)/shard_map/pallas_call | solution.py:72
  330.4 2.0 collective-permute-done.20
  332.5 14.5 %shard_map.215 = (bf16[16,80,768]{2,1,0:T(8,128)(2,1)}, bf16[16,80,768]{2,1,0:T(8,128)(2,1)}, f32[16,768]{1,0:T(8,128)}) custom-call(s32[4]{0:T(128)S(1)} %pad_add_fusion.refs_0_, s32[1]{0:T(128)S(6)} %copy.35.refs_1_, bf16[3,1024,256]{2,1,0:T(8,128)(2,1)S(1)} %copy-done.3, bf16[3,1024,256]{2,1,0:T(8,128)(2,1)S(1)} %copy-done.6, ...), custom_call_target="tpu_custom_call" | custom-call | flops 7247757312 | bytes 20152340 | tf_op jit(solution)/shard_map/pallas_call | solution.py:72
  347.0 4.2 %collective-permute-done.22.refs_1_ = bf16[16,80,768]{2,1,0:T(8,128)(2,1)S(1)} collective-permute-done((bf16[16,80,768]{2,1,0:T(8,128)(2,1)}, bf16[16,80,768]{2,1,0:T(8,128)(2,1)S(1)}, u32[]{:S(2)}, u32[]{:S(2)}) %collective-permute-start.22) | collective-permute-done | bytes 1966112 | tf_op jit(solution)/shard_map/ppermute | solution.py:816
  355.2 3.0 collective-permute-start.30
  360.6 8.9 %shard_map.217 = f32[1024,768]{1,0:T(8,128)} custom-call(bf16[3,1024,256]{2,1,0:T(8,128)(2,1)S(1)} %copy-done.3, bf16[3,1024,256]{2,1,0:T(8,128)(2,1)S(1)} %copy-done.6, bf16[3,1024,256]{2,1,0:T(8,128)(2,1)S(1)} %shard_map.213.refs_4_.refs_11_.refs_2_, bf16[1024,768]{1,0:T(8,128)(2,1)} %bitcast.49, f32[1024,768]{1,0:T(8,128)} %get-tuple-element.149.refs_4_, ...), custom_call_target="tpu_custom_call" | custom-call | flops 3623878656 | bytes 16146432 | tf_op jit(solution)/shard_map/pallas_call | solution.py:72
  372.7 4.0 %collective-permute-done.25.refs_1_ = bf16[4,80,384]{2,1,0:T(8,128)(2,1)S(1)} collective-permute-done((bf16[4,80,384]{2,1,0:T(8,128)(2,1)S(1)}, bf16[4,80,384]{2,1,0:T(8,128)(2,1)S(1)}, u32[]{:S(2)}, u32[]{:S(2)}) %collective-permute-start.25) | collective-permute-done | bytes 245792 | tf_op jit(solution)/shard_map/ppermute | solution.py:816
  384.9 3.9 collective-permute-done.28
  (132 shorter events, 56.5 us)
Async XLA Ops:
  7.2 97.1 %all-gather.3.cloned.1.call-start = ((), (), s32[]{:S(2)}) async-start(), calls=%async_computation | async-start | bytes 9732096 | tf_op jit(solution)/shard_map/all_gather | solution.py:1048
  10.6 10.2 %collective-permute-start = (bf16[1,112,768]{2,1,0:T(8,128)(2,1)S(1)}, bf16[1,112,768]{2,1,0:T(8,128)(2,1)S(1)}, u32[]{:S(2)}, u32[]{:S(2)}) collective-permute-start(bf16[1,112,768]{2,1,0:T(8,128)(2,1)S(1)} %fusion.4), channel_id=1, source_target_pairs={{0,2},{1,3},{2,0},{3,1},{4,6},{5,7},{6,4},{7,5},{8,10},{9,11},{10,... | collective-permute-start | bytes 516104 | tf_op jit(solution)/shard_map/ppermute | solution.py:816
  13.7 18.5 %collective-permute-start.1 = (bf16[1,112,768]{2,1,0:T(8,128)(2,1)S(1)}, bf16[1,112,768]{2,1,0:T(8,128)(2,1)S(1)}, u32[]{:S(2)}, u32[]{:S(2)}) collective-permute-start(bf16[1,112,768]{2,1,0:T(8,128)(2,1)S(1)} %fusion.4), channel_id=1, source_target_pairs={{0,4},{1,5},{2,6},{3,7},{4,0},{5,1},{6,2},{7,3},{8,12},{9,13},{10,... | collective-permute-start | bytes 516104 | tf_op jit(solution)/shard_map/ppermute | solution.py:816
  16.3 15.9 %collective-permute-start.2 = (bf16[1,112,768]{2,1,0:T(8,128)(2,1)S(1)}, bf16[1,112,768]{2,1,0:T(8,128)(2,1)S(1)}, u32[]{:S(2)}, u32[]{:S(2)}) collective-permute-start(bf16[1,112,768]{2,1,0:T(8,128)(2,1)S(1)} %fusion.4), channel_id=1, source_target_pairs={{0,6},{1,7},{2,4},{3,5},{4,2},{5,3},{6,0},{7,1},{8,14},{9,15},{10,... | collective-permute-start | bytes 516104 | tf_op jit(solution)/shard_map/ppermute | solution.py:816
  32.3 9.4 %collective-permute-start.6 = (bf16[4,112,384]{2,1,0:T(8,128)(2,1)S(1)}, bf16[4,112,384]{2,1,0:T(8,128)(2,1)S(1)}, u32[]{:S(2)}, u32[]{:S(2)}) collective-permute-start(bf16[4,112,384]{2,1,0:T(8,128)(2,1)S(1)} %get-tuple-element.184), channel_id=1, source_target_pairs={{0,8},{1,9},{2,10},{3,11},{4,12},{5,13},{6,14},{7,15},{8,0},{9,1},... | collective-permute-start | bytes 1032200 | tf_op jit(solution)/shard_map/ppermute | solution.py:816
  33.9 11.0 %collective-permute-start.3 = (bf16[4,112,384]{2,1,0:T(8,128)(2,1)S(1)}, bf16[4,112,384]{2,1,0:T(8,128)(2,1)S(1)}, u32[]{:S(2)}, u32[]{:S(2)}) collective-permute-start(bf16[4,112,384]{2,1,0:T(8,128)(2,1)S(1)} %get-tuple-element.185), channel_id=1, source_target_pairs={{0,16},{1,17},{2,18},{3,19},{4,20},{5,21},{6,22},{7,23},{8,24},{9,... | collective-permute-start | bytes 1032200 | tf_op jit(solution)/shard_map/ppermute | solution.py:816
  41.8 16.9 %collective-permute-start.7 = (bf16[8,112,384]{2,1,0:T(8,128)(2,1)S(1)}, bf16[8,112,384]{2,1,0:T(8,128)(2,1)S(1)}, u32[]{:S(2)}, u32[]{:S(2)}) collective-permute-start(bf16[8,112,384]{2,1,0:T(8,128)(2,1)S(1)} %pad_maximum_fusion.4), channel_id=1, source_target_pairs={{0,16},{1,17},{2,18},{3,19},{4,20},{5,21},{6,22},{7,23},{8,24},{9,... | collective-permute-start | bytes 2064392 | tf_op jit(solution)/shard_map/ppermute | solution.py:816
  45.0 17.9 %collective-permute-start.4 = (bf16[8,112,384]{2,1,0:T(8,128)(2,1)S(1)}, bf16[8,112,384]{2,1,0:T(8,128)(2,1)S(1)}, u32[]{:S(2)}, u32[]{:S(2)}) collective-permute-start(bf16[8,112,384]{2,1,0:T(8,128)(2,1)S(1)} %pad_maximum_fusion.3), channel_id=1, source_target_pairs={{0,8},{1,9},{2,10},{3,11},{4,12},{5,13},{6,14},{7,15},{8,0},{9,1},... | collective-permute-start | bytes 2064392 | tf_op jit(solution)/shard_map/ppermute | solution.py:816
  59.0 7.0 %collective-permute-start.8 = (bf16[16,112,384]{2,1,0:T(8,128)(2,1)S(1)}, bf16[16,112,384]{2,1,0:T(8,128)(2,1)}, u32[]{:S(2)}, u32[]{:S(2)}) collective-permute-start(bf16[16,112,384]{2,1,0:T(8,128)(2,1)S(1)} %pad_maximum_fusion.1.refs_4_), channel_id=1, source_target_pairs={{0,1},{1,0},{2,3},{3,2},{4,5},{5,4},{6,7},{7,6},{8,9},{9,8},{10,11... | collective-permute-start | bytes 4128776 | tf_op jit(solution)/shard_map/ppermute | solution.py:816
  254.6 9.0 %collective-permute-start.10 = (bf16[16,120,768]{2,1,0:T(8,128)(2,1)S(1)}, bf16[16,120,768]{2,1,0:T(8,128)(2,1)S(1)}, u32[]{:S(2)}, u32[]{:S(2)}) collective-permute-start(bf16[16,120,768]{2,1,0:T(8,128)(2,1)S(1)} %shard_map.204.refs_4_), channel_id=1, source_target_pairs={{0,1},{1,0},{2,3},{3,2},{4,5},{5,4},{6,7},{7,6},{8,9},{9,8},{10,11... | collective-permute-start | bytes 8847368 | tf_op jit(solution)/shard_map/ppermute | solution.py:816
  263.3 12.4 %collective-permute-start.9 = (bf16[16,96,768]{2,1,0:T(8,128)(2,1)S(1)}, bf16[16,96,768]{2,1,0:T(8,128)(2,1)}, u32[]{:S(2)}, u32[]{:S(2)}) collective-permute-start(bf16[16,96,768]{2,1,0:T(8,128)(2,1)S(1)} %shard_map.205.refs_6_), channel_id=1, source_target_pairs={{0,1},{1,0},{2,3},{3,2},{4,5},{5,4},{6,7},{7,6},{8,9},{9,8},{10,11... | collective-permute-start | bytes 7077896 | tf_op jit(solution)/shard_map/ppermute | solution.py:816
  273.6 24.4 %collective-permute-start.11 = (bf16[8,72,768]{2,1,0:T(8,128)(2,1)S(1)}, bf16[8,72,768]{2,1,0:T(8,128)(2,1)S(1)}, u32[]{:S(2)}, u32[]{:S(2)}) collective-permute-start(bf16[8,72,768]{2,1,0:T(8,128)(2,1)S(1)} %get-tuple-element.127.refs_6_), channel_id=1, source_target_pairs={{0,8},{1,9},{2,10},{3,11},{4,12},{5,13},{6,14},{7,15},{8,0},{9,1},... | collective-permute-start | bytes 2654216 | tf_op jit(solution)/shard_map/ppermute | solution.py:816
  275.0 22.9 %collective-permute-start.12 = (bf16[8,48,768]{2,1,0:T(8,128)(2,1)S(1)}, bf16[8,48,768]{2,1,0:T(8,128)(2,1)S(1)}, u32[]{:S(2)}, u32[]{:S(2)}) collective-permute-start(bf16[8,48,768]{2,1,0:T(8,128)(2,1)S(1)} %get-tuple-element.129.refs_8_), channel_id=1, source_target_pairs={{0,16},{1,17},{2,18},{3,19},{4,20},{5,21},{6,22},{7,23},{8,24},{9,... | collective-permute-start | bytes 1769480 | tf_op jit(solution)/shard_map/ppermute | solution.py:816
  284.3 26.2 %collective-permute-start.13 = (bf16[8,48,768]{2,1,0:T(8,128)(2,1)S(1)}, bf16[8,48,768]{2,1,0:T(8,128)(2,1)S(1)}, u32[]{:S(2)}, u32[]{:S(2)}) collective-permute-start(bf16[8,48,768]{2,1,0:T(8,128)(2,1)S(1)} %get-tuple-element.131.refs_8_), channel_id=1, source_target_pairs={{0,8},{1,9},{2,10},{3,11},{4,12},{5,13},{6,14},{7,15},{8,0},{9,1},... | collective-permute-start | bytes 1769480 | tf_op jit(solution)/shard_map/ppermute | solution.py:816
  285.8 24.8 %collective-permute-start.14 = (bf16[8,48,768]{2,1,0:T(8,128)(2,1)S(1)}, bf16[8,48,768]{2,1,0:T(8,128)(2,1)S(1)}, u32[]{:S(2)}, u32[]{:S(2)}) collective-permute-start(bf16[8,48,768]{2,1,0:T(8,128)(2,1)S(1)} %get-tuple-element.133.refs_10_), channel_id=1, source_target_pairs={{0,16},{1,17},{2,18},{3,19},{4,20},{5,21},{6,22},{7,23},{8,24},{9,... | collective-permute-start | bytes 1769480 | tf_op jit(solution)/shard_map/ppermute | solution.py:816
  298.3 16.8 %collective-permute-start.15 = (bf16[4,72,768]{2,1,0:T(8,128)(2,1)S(1)}, bf16[4,72,768]{2,1,0:T(8,128)(2,1)S(1)}, u32[]{:S(2)}, u32[]{:S(2)}) collective-permute-start(bf16[4,72,768]{2,1,0:T(8,128)(2,1)S(1)} %get-tuple-element.136.refs_8_), channel_id=1, source_target_pairs={{0,16},{1,17},{2,18},{3,19},{4,20},{5,21},{6,22},{7,23},{8,24},{9,... | collective-permute-start | bytes 1327112 | tf_op jit(solution)/shard_map/ppermute | solution.py:816
  299.8 15.2 %collective-permute-start.16 = (bf16[4,48,768]{2,1,0:T(8,128)(2,1)S(1)}, bf16[4,48,768]{2,1,0:T(8,128)(2,1)S(1)}, u32[]{:S(2)}, u32[]{:S(2)}) collective-permute-start(bf16[4,48,768]{2,1,0:T(8,128)(2,1)S(1)} %get-tuple-element.137.refs_9_), channel_id=1, source_target_pairs={{0,8},{1,9},{2,10},{3,11},{4,12},{5,13},{6,14},{7,15},{8,0},{9,1},... | collective-permute-start | bytes 884744 | tf_op jit(solution)/shard_map/ppermute | solution.py:816
  310.9 19.3 %collective-permute-start.17 = (bf16[4,48,768]{2,1,0:T(8,128)(2,1)S(1)}, bf16[4,48,768]{2,1,0:T(8,128)(2,1)S(1)}, u32[]{:S(2)}, u32[]{:S(2)}) collective-permute-start(bf16[4,48,768]{2,1,0:T(8,128)(2,1)S(1)} %get-tuple-element.140.refs_8_), channel_id=1, source_target_pairs={{0,16},{1,17},{2,18},{3,19},{4,20},{5,21},{6,22},{7,23},{8,24},{9,... | collective-permute-start | bytes 884744 | tf_op jit(solution)/shard_map/ppermute | solution.py:816
  312.3 17.9 %collective-permute-start.18 = (bf16[4,48,768]{2,1,0:T(8,128)(2,1)S(1)}, bf16[4,48,768]{2,1,0:T(8,128)(2,1)S(1)}, u32[]{:S(2)}, u32[]{:S(2)}) collective-permute-start(bf16[4,48,768]{2,1,0:T(8,128)(2,1)S(1)} %get-tuple-element.141.refs_9_), channel_id=1, source_target_pairs={{0,8},{1,9},{2,10},{3,11},{4,12},{5,13},{6,14},{7,15},{8,0},{9,1},... | collective-permute-start | bytes 884744 | tf_op jit(solution)/shard_map/ppermute | solution.py:816
  315.2 15.1 %collective-permute-start.19 = (bf16[120,768]{1,0:T(8,128)(2,1)S(1)}, bf16[120,768]{1,0:T(8,128)(2,1)S(1)}, u32[]{:S(2)}, u32[]{:S(2)}) collective-permute-start(bf16[120,768]{1,0:T(8,128)(2,1)S(1)} %get-tuple-element.146.refs_10_), channel_id=1, source_target_pairs={{0,2},{1,3},{2,0},{3,1},{4,6},{5,7},{6,4},{7,5},{8,10},{9,11},{10,... | collective-permute-start | bytes 552968 | tf_op jit(solution)/shard_map/ppermute | solution.py:816
  316.8 15.6 %collective-permute-start.20 = (bf16[120,768]{1,0:T(8,128)(2,1)S(1)}, bf16[120,768]{1,0:T(8,128)(2,1)S(1)}, u32[]{:S(2)}, u32[]{:S(2)}) collective-permute-start(bf16[120,768]{1,0:T(8,128)(2,1)S(1)} %get-tuple-element.147.refs_11_), channel_id=1, source_target_pairs={{0,4},{1,5},{2,6},{3,7},{4,0},{5,1},{6,2},{7,3},{8,12},{9,13},{10,... | collective-permute-start | bytes 552968 | tf_op jit(solution)/shard_map/ppermute | solution.py:816
  317.8 14.7 %collective-permute-start.21 = (bf16[120,768]{1,0:T(8,128)(2,1)S(1)}, bf16[120,768]{1,0:T(8,128)(2,1)S(1)}, u32[]{:S(2)}, u32[]{:S(2)}) collective-permute-start(bf16[120,768]{1,0:T(8,128)(2,1)S(1)} %get-tuple-element.148.refs_12_), channel_id=1, source_target_pairs={{0,6},{1,7},{2,4},{3,5},{4,2},{5,3},{6,0},{7,1},{8,14},{9,15},{10,... | collective-permute-start | bytes 552968 | tf_op jit(solution)/shard_map/ppermute | solution.py:816
  353.2 16.3 %collective-permute-start.23 = (bf16[8,80,384]{2,1,0:T(8,128)(2,1)S(1)}, bf16[8,80,384]{2,1,0:T(8,128)(2,1)S(1)}, u32[]{:S(2)}, u32[]{:S(2)}) collective-permute-start(bf16[8,80,384]{2,1,0:T(8,128)(2,1)S(1)} %get-tuple-element.167.refs_7_), channel_id=1, source_target_pairs={{0,8},{1,9},{2,10},{3,11},{4,12},{5,13},{6,14},{7,15},{8,0},{9,1},... | collective-permute-start | bytes 1474568 | tf_op jit(solution)/shard_map/ppermute | solution.py:816
  354.7 14.8 %collective-permute-start.24 = (bf16[8,80,384]{2,1,0:T(8,128)(2,1)S(1)}, bf16[8,80,384]{2,1,0:T(8,128)(2,1)S(1)}, u32[]{:S(2)}, u32[]{:S(2)}) collective-permute-start(bf16[8,80,384]{2,1,0:T(8,128)(2,1)S(1)} %get-tuple-element.168.refs_8_), channel_id=1, source_target_pairs={{0,16},{1,17},{2,18},{3,19},{4,20},{5,21},{6,22},{7,23},{8,24},{9,... | collective-permute-start | bytes 1474568 | tf_op jit(solution)/shard_map/ppermute | solution.py:816
  355.2 16.7 %collective-permute-start.30 = (bf16[96,768]{1,0:T(8,128)(2,1)S(1)}, bf16[96,768]{1,0:T(8,128)(2,1)S(1)}, u32[]{:S(2)}, u32[]{:S(2)}) collective-permute-start(bf16[96,768]{1,0:T(8,128)(2,1)S(1)} %get-tuple-element.158.refs_12_), channel_id=1, source_target_pairs={{0,2},{1,3},{2,0},{3,1},{4,6},{5,7},{6,4},{7,5},{8,10},{9,11},{10,... | collective-permute-start | bytes 442376 | tf_op jit(solution)/shard_map/ppermute | solution.py:816
  358.2 13.7 %collective-permute-start.31 = (bf16[96,768]{1,0:T(8,128)(2,1)S(1)}, bf16[96,768]{1,0:T(8,128)(2,1)S(1)}, u32[]{:S(2)}, u32[]{:S(2)}) collective-permute-start(bf16[96,768]{1,0:T(8,128)(2,1)S(1)} %get-tuple-element.159.refs_13_), channel_id=1, source_target_pairs={{0,4},{1,5},{2,6},{3,7},{4,0},{5,1},{6,2},{7,3},{8,12},{9,13},{10,... | collective-permute-start | bytes 442376 | tf_op jit(solution)/shard_map/ppermute | solution.py:816
  358.7 13.1 %collective-permute-start.32 = (bf16[96,768]{1,0:T(8,128)(2,1)S(1)}, bf16[96,768]{1,0:T(8,128)(2,1)S(1)}, u32[]{:S(2)}, u32[]{:S(2)}) collective-permute-start(bf16[96,768]{1,0:T(8,128)(2,1)S(1)} %get-tuple-element.160.refs_14_), channel_id=1, source_target_pairs={{0,6},{1,7},{2,4},{3,5},{4,2},{5,3},{6,0},{7,1},{8,14},{9,15},{10,... | collective-permute-start | bytes 442376 | tf_op jit(solution)/shard_map/ppermute | solution.py:816
  369.8 6.9 %collective-permute-start.25 = (bf16[4,80,384]{2,1,0:T(8,128)(2,1)S(1)}, bf16[4,80,384]{2,1,0:T(8,128)(2,1)S(1)}, u32[]{:S(2)}, u32[]{:S(2)}) collective-permute-start(bf16[4,80,384]{2,1,0:T(8,128)(2,1)S(1)} %get-tuple-element.174), channel_id=1, source_target_pairs={{0,16},{1,17},{2,18},{3,19},{4,20},{5,21},{6,22},{7,23},{8,24},{9,... | collective-permute-start | bytes 737288 | tf_op jit(solution)/shard_map/ppermute | solution.py:816
  371.2 6.6 %collective-permute-start.26 = (bf16[4,80,384]{2,1,0:T(8,128)(2,1)S(1)}, bf16[4,80,384]{2,1,0:T(8,128)(2,1)S(1)}, u32[]{:S(2)}, u32[]{:S(2)}) collective-permute-start(bf16[4,80,384]{2,1,0:T(8,128)(2,1)S(1)} %get-tuple-element.176), channel_id=1, source_target_pairs={{0,8},{1,9},{2,10},{3,11},{4,12},{5,13},{6,14},{7,15},{8,0},{9,1},... | collective-permute-start | bytes 737288 | tf_op jit(solution)/shard_map/ppermute | solution.py:816
  378.0 6.9 %collective-permute-start.27 = (bf16[80,768]{1,0:T(8,128)(2,1)S(1)}, bf16[80,768]{1,0:T(8,128)(2,1)S(1)}, u32[]{:S(2)}, u32[]{:S(2)}) collective-permute-start(bf16[80,768]{1,0:T(8,128)(2,1)S(1)} %get-tuple-element.178), channel_id=1, source_target_pairs={{0,2},{1,3},{2,0},{3,1},{4,6},{5,7},{6,4},{7,5},{8,10},{9,11},{10,... | collective-permute-start | bytes 368648 | tf_op jit(solution)/shard_map/ppermute | solution.py:816
  378.8 10.0 %collective-permute-start.28 = (bf16[80,768]{1,0:T(8,128)(2,1)S(1)}, bf16[80,768]{1,0:T(8,128)(2,1)S(1)}, u32[]{:S(2)}, u32[]{:S(2)}) collective-permute-start(bf16[80,768]{1,0:T(8,128)(2,1)S(1)} %get-tuple-element.179), channel_id=1, source_target_pairs={{0,4},{1,5},{2,6},{3,7},{4,0},{5,1},{6,2},{7,3},{8,12},{9,13},{10,... | collective-permute-start | bytes 368648 | tf_op jit(solution)/shard_map/ppermute | solution.py:816
  380.5 8.3 %collective-permute-start.29 = (bf16[80,768]{1,0:T(8,128)(2,1)S(1)}, bf16[80,768]{1,0:T(8,128)(2,1)S(1)}, u32[]{:S(2)}, u32[]{:S(2)}) collective-permute-start(bf16[80,768]{1,0:T(8,128)(2,1)S(1)} %get-tuple-element.180), channel_id=1, source_target_pairs={{0,6},{1,7},{2,4},{3,5},{4,2},{5,3},{6,0},{7,1},{8,14},{9,15},{10,... | collective-permute-start | bytes 368648 | tf_op jit(solution)/shard_map/ppermute | solution.py:816
  (23 other events, 164.7 us)
Sparse Core Ops, SparseCore 0:
  11.6 92.5 all-gather.2

commit v3 on v2

--- a/solution.py
+++ b/solution.py
@@ -136,23 +136,22 @@
     return found
 
 
+def project_kernel(att_ref, x_ref, live_ref, norms_ref, wo_ref, hidden_ref, second_ref):
+    hidden = x_ref[...].astype(f32) + live_ref[...] * dot_nt(att_ref[...], wo_ref[...])
+    hidden_ref[...] = hidden
+    xhat, _ = normalize(hidden)
+    second_ref[...] = (xhat * norms_ref[1:2, :] + norms_ref[3:4, :]).astype(bf16)
+
+
 def middle_kernel(order, share, place_ref, packed_ref, *refs):
     chunks = ff_chunks(order, place_ref, packed_ref, share)
-    atts, refs = refs[:-13], refs[-13:]
     (
-        x_ref, live_ref, norms_ref, emb_ref, wo_ref, wq_ref,
-        hidden_ref, second_ref, act_ref, slope_ref, later_ref, mixed_ref, xhat_ref,
+        hidden_ref, second_ref, live_ref, norms_ref, emb_ref, wq_ref,
+        act_ref, slope_ref, later_ref, mixed_ref, xhat_ref,
     ) = refs
     live = live_ref[...]
-    branch, at = 0.0, 0
-    for ref in atts:
-        branch = branch + dot_nt(ref[...], wo_ref[:, at : at + ref.shape[1]])
-        at += ref.shape[1]
-    hidden = x_ref[...].astype(f32) + live * branch
-    hidden_ref[...] = hidden
-    xhat, _ = normalize(hidden)
-    second = (xhat * norms_ref[1:2, :] + norms_ref[3:4, :]).astype(bf16)
-    second_ref[...] = second
+    hidden = hidden_ref[...]
+    second = second_ref[...]
     total = jnp.zeros_like(hidden)
     for up, down, to in chunks:
         value, slope = gelu_pair(dot_nt(second, up()))
@@ -1087,7 +1086,12 @@
     pairs = width // LANES
     third = pairs // 3 if pairs % 3 == 0 else pairs
     att0, logs0 = attend(mixed0, live_cols[0], live_rows[0])
-    packed = after(packed, att0)
+    hidden0, second0 = call(
+        project_kernel, grid,
+        [rows_w, rows_w, rows_1, whole_spec(norms), whole_spec(wo)],
+        [rows_w, rows_w], [wide, thin], unit * width, [att0, x, live_cols[0], norms, wo],
+    )
+    packed = after(packed, second0)
     order, share = cube.order(), high
     if cube.count == 1 or 768 % high or high % 16:
         blocks = [packed[:, at : at + high] for at in (0, high)]
@@ -1097,14 +1101,14 @@
         ]
         packed, share = jnp.concatenate(turned, axis=0)[None], ff
     smem = pl.BlockSpec(memory_space=pltpu.SMEM)
-    hidden0, second0, act0, slope0, later, mixed1, xhat1 = call(
+    act0, slope0, later, mixed1, xhat1 = call(
         functools.partial(middle_kernel, order, share), grid,
         [smem, whole_spec(packed), rows_w, rows_w, rows_1]
-        + [whole_spec(a) for a in (norms, emb, wo, wq)],
-        [rows_w, rows_w, rows_f, rows_f, rows_w, rows_q, rows_w],
-        [wide, thin, tall, tall, wide, triple, thin],
-        unit * (4 * width + 2 * ff),
-        [place, packed, att0, x, live_cols[0], norms, emb, wo, wq],
+        + [whole_spec(a) for a in (norms, emb, wq)],
+        [rows_f, rows_f, rows_w, rows_q, rows_w],
+        [tall, tall, wide, triple, thin],
+        unit * (3 * width + 2 * ff),
+        [place, packed, hidden0, second0, live_cols[0], norms, emb, wq],
     )
     att1, logs1 = attend(mixed1, live_cols[1], live_rows[1])
     result, second1, act1, drop1, lift1, branch1, hgrad1, agrad1, sums1 = call(

time: 402 us -> 402 us (level)
  waiting for transfers between devices: 65.6 us -> 59.9 us
    all_gather x1, waiting for transfers between devices: 5.69 us -> 0.44 us  [body(): packed = lax.all_gather(packed, AXES, axis=0, tiled=False)]
    pallas_call x25 -> x26, Pallas kernels: 259 us -> 261 us  [call(): pl.pallas_call(run, grid=grid, in_specs=list(in_specs) + [pl.BlockSpec(me...]
    unnamed x42 -> x40, local copies, waits for them, and re-layouts: 8.55 us -> 7.37 us
  transfers between devices with their start and end apart: 34 -> 34, of which waited for: 15 -> 16; matrix products, arithmetic and copies ran while one was open for 2% -> 2% of each run, Pallas kernels for 24% -> 25%
where the time goes in v3:
time: 402 us; the launch traced here: 399 us
  Pallas kernels  261 us (65%)
  waiting for transfers between devices  59.9 us (15%)
  starting transfers between devices  42.9 us (11%)
  between operations  16 us (4%)
  local copies, waits for them, and re-layouts  9.67 us (2%)
  other arithmetic  9.23 us (2%)
    pallas_call x26, Pallas kernels, call(): pl.pallas_call(run, grid=grid, in_specs=list(in_specs) + [pl.BlockSpec(me...  261 us
    ppermute x33, waiting for transfers between devices, send(): return lax.ppermute(value, AXES, [(d, d ^ mask) for d in range(self.count)])  59.5 us
    ppermute x33, starting transfers between devices, send(): return lax.ppermute(value, AXES, [(d, d ^ mask) for d in range(self.count)])  42.9 us
  transfers between devices with their start and end apart: 34, of which 16 were waited for; matrix products, arithmetic and copies ran while one was open for 2% of the time, Pallas kernels for 25%

profile of v3, /device:TPU:0, one launch (start us, length us, event | category | flops | bytes accessed | tf_op | source)
XLA Modules:
  0.0 398.9 jit_solution(8245772331569681340)
XLA Ops:
  10.6 3.1 collective-permute-start
  13.7 2.6 collective-permute-start.1
  16.3 4.5 %collective-permute-done = bf16[1,112,768]{2,1,0:T(8,128)(2,1)S(1)} collective-permute-done((bf16[1,112,768]{2,1,0:T(8,128)(2,1)S(1)}, bf16[1,112,768]{2,1,0:T(8,128)(2,1)S(1)}, u32[]{:S(2)}, u32[]{:S(2)}) %collective-permute-start) | collective-permute-done | bytes 172064 | tf_op jit(solution)/shard_map/ppermute | solution.py:815
  20.8 11.4 %collective-permute-done.1 = bf16[1,112,768]{2,1,0:T(8,128)(2,1)S(1)} collective-permute-done((bf16[1,112,768]{2,1,0:T(8,128)(2,1)S(1)}, bf16[1,112,768]{2,1,0:T(8,128)(2,1)S(1)}, u32[]{:S(2)}, u32[]{:S(2)}) %collective-permute-start.1) | collective-permute-done | bytes 172064 | tf_op jit(solution)/shard_map/ppermute | solution.py:815
  35.4 6.3 %collective-permute-done.6 = bf16[4,112,384]{2,1,0:T(8,128)(2,1)S(1)} collective-permute-done((bf16[4,112,384]{2,1,0:T(8,128)(2,1)S(1)}, bf16[4,112,384]{2,1,0:T(8,128)(2,1)S(1)}, u32[]{:S(2)}, u32[]{:S(2)}) %collective-permute-start.6) | collective-permute-done | bytes 344096 | tf_op jit(solution)/shard_map/ppermute | solution.py:815
  46.2 12.6 %collective-permute-done.7 = bf16[8,112,384]{2,1,0:T(8,128)(2,1)S(1)} collective-permute-done((bf16[8,112,384]{2,1,0:T(8,128)(2,1)S(1)}, bf16[8,112,384]{2,1,0:T(8,128)(2,1)S(1)}, u32[]{:S(2)}, u32[]{:S(2)}) %collective-permute-start.7) | collective-permute-done | bytes 688160 | tf_op jit(solution)/shard_map/ppermute | solution.py:815
  60.0 2.8 collective-permute-done.4
  67.6 5.6 %shard_map.195 = (bf16[32,72,768]{2,1,0:T(8,128)(2,1)}, bf16[32,24,768]{2,1,0:T(8,128)(2,1)S(1)}, f32[8,768]{1,0:T(8,128)S(1)}, f32[1,768]{1,0:T(1,128)S(1)}) custom-call(s32[4]{0:T(128)S(1)} %pad_add_fusion.refs_0_, s32[1]{0:T(128)S(6)} %copy.36.refs_1_, bf16[16,112,384]{2,1,0:T(8,128)(2,1)} %pad_maximum_fusion.refs_2_, ...), custom_call_target="tpu_custom_call" | custom-call | bytes 10251284 | tf_op jit(solution)/shard_map/pallas_call | solution.py:72
  73.2 8.6 %shard_map.196 = (bf16[1024,2304]{1,0:T(8,128)(2,1)}, bf16[1024,768]{1,0:T(8,128)(2,1)S(1)}) custom-call(bf16[1024,768]{1,0:T(8,128)(2,1)} %bitcast.41, f32[8,768]{1,0:T(8,128)S(1)} %get-tuple-element.96.refs_1_.refs_3_.refs_5_, bf16[2304,768]{1,0:T(8,128)(2,1)} %bitcast.44), custom_call_target="tpu_custom_call" | custom-call | flops 3623878656 | bytes 11427840 | tf_op jit(solution)/shard_map/pallas_call | solution.py:72
  81.8 16.1 %shard_map.197 = (bf16[1024,768]{1,0:T(8,128)(2,1)}, f32[1024,768]{1,0:T(8,128)}) custom-call(bf16[1024,2304]{1,0:T(8,128)(2,1)} %get-tuple-element.98.refs_0_.refs_1_.refs_2_, bf16[1024,2304]{1,0:T(8,128)(2,1)} %get-tuple-element.98.refs_0_.refs_1_.refs_2_, bf16[1024,2304]{1,0:T(8,128)(2,1)} %get-tuple-element.98.refs_0_.refs_1_.refs_2_, ...), custom_call_target="tpu_custom_call" | custom-call | flops 3221225472 | bytes 18882560 | tf_op jit(solution)/shard_map/pallas_call | solution.py:72
  98.0 5.8 %shard_map.198 = (f32[1024,768]{1,0:T(8,128)}, bf16[1024,768]{1,0:T(8,128)(2,1)}) custom-call(bf16[1024,768]{1,0:T(8,128)(2,1)} %get-tuple-element.99.refs_0_.refs_3_.refs_4_, bf16[1024,768]{1,0:T(8,128)(2,1)} %bitcast.42, f32[1024,1]{1,0:T(8,128)S(1)} %copy.24.refs_3_.refs_2_.refs_4_.refs_6_, f32[8,768]{1,0:T(8,128)S(1)} %get-tuple-element.96.refs_1_.refs_3_.refs_5_, ...), custom_call_target="tpu_custom_call" | custom-call | flops 1207959552 | bytes 9072640 | tf_op jit(solution)/shard_map/pallas_call | solution.py:72
  104.2 24.7 %shard_map.199 = (bf16[1024,3072]{1,0:T(8,128)(2,1)}, bf16[1024,3072]{1,0:T(8,128)(2,1)}, f32[1024,768]{1,0:T(8,128)}, bf16[1024,2304]{1,0:T(8,128)(2,1)}, bf16[1024,768]{1,0:T(8,128)(2,1)}) custom-call(s32[4]{0:T(128)S(1)} %pad_add_fusion.refs_0_, bf16[32,192,768]{2,1,0:T(8,128)(2,1)} %bitcast.53, f32[1024,768]{1,0:T(8,128)} %get-tuple-element.103.refs_2_.refs_7_, ...), custom_call_target="tpu_custom_call" | custom-call | flops 13287555072 | bytes 39746576 | tf_op jit(solution)/shard_map/pallas_call | solution.py:72
  129.0 15.7 %shard_map.200 = (bf16[1024,768]{1,0:T(8,128)(2,1)}, f32[1024,768]{1,0:T(8,128)}) custom-call(bf16[1024,2304]{1,0:T(8,128)(2,1)} %get-tuple-element.105.refs_0_.refs_1_.refs_2_, bf16[1024,2304]{1,0:T(8,128)(2,1)} %get-tuple-element.105.refs_0_.refs_1_.refs_2_, bf16[1024,2304]{1,0:T(8,128)(2,1)} %get-tuple-element.105.refs_0_.refs_1_.refs_2_, ...), custom_call_target="tpu_custom_call" | custom-call | flops 3221225472 | bytes 18882560 | tf_op jit(solution)/shard_map/pallas_call | solution.py:72
  144.6 35.3 %shard_map.201 = (bf16[1024,768]{1,0:T(8,128)(2,1)}, bf16[1024,768]{1,0:T(8,128)(2,1)}, bf16[1024,3072]{1,0:T(8,128)(2,1)}, bf16[1024,768]{1,0:T(8,128)(2,1)}, b...) custom-call(s32[4]{0:T(128)S(1)} %pad_add_fusion.refs_0_, ...), custom_call_target="tpu_custom_call" | custom-call | flops 21743271936 | bytes 42127376 | tf_op jit(solution)/shard_map/pallas_call | solution.py:72
  180.0 27.8 %shard_map.202.refs_2_.refs_5_ = bf16[3,1024,768]{2,1,0:T(8,128)(2,1)} custom-call(bf16[1024,2304]{1,0:T(8,128)(2,1)} %get-tuple-element.105.refs_0_.refs_1_.refs_2_, bf16[1024,2304]{1,0:T(8,128)(2,1)} %get-tuple-element.105.refs_0_.refs_1_.refs_2_, bf16[1024,2304]{1,0:T(8,128)(2,1)} %get-tuple-element.105.refs_0_.refs_1_.refs_2_, ...), custom_call_target="tpu_custom_call" | custom-call | flops 8053063680 | bytes 25169920 | tf_op jit(solution)/shard_map/pallas_call | solution.py:72
  207.7 30.2 %shard_map.203 = (bf16[1024,768]{1,0:T(8,128)(2,1)}, bf16[1024,3072]{1,0:T(8,128)(2,1)}, bf16[1024,768]{1,0:T(8,128)(2,1)}, f32[1024,768]{1,0:T(8,128)}, bf16[10...) custom-call(s32[4]{0:T(128)S(1)} %pad_add_fusion.refs_0_, bf16[32,192,768]{2,1,0:T(8,128)(2,1)} %bitcast.55, ...), custom_call_target="tpu_custom_call" | custom-call | flops 14495514624 | bytes 48812048 | tf_op jit(solution)/shard_map/pallas_call | solution.py:72
  239.3 4.2 %shard_map.204 = (bf16[16,24,768]{2,1,0:T(8,128)(2,1)S(1)}, bf16[16,24,768]{2,1,0:T(8,128)(2,1)S(1)}) custom-call(s32[4]{0:T(128)S(1)} %pad_add_fusion.refs_0_, bf16[1024,768]{1,0:T(8,128)(2,1)S(1)} %copy-done.15, bf16[1024,768]{1,0:T(8,128)(2,1)S(1)} %copy-done.14, bf16[1024,768]{1,0:T(8,128)(2,1)S(1)} %copy-done, ...), custom_call_target="tpu_custom_call" | custom-call | flops 2415919104 | bytes 7471120 | tf_op jit(solution)/shard_map/pallas_call | solution.py:72
  243.6 7.3 %shard_map.205.refs_4_ = bf16[16,120,768]{2,1,0:T(8,128)(2,1)S(1)} custom-call(bf16[1024,3072]{1,0:T(8,128)(2,1)} %get-tuple-element.119.refs_0_, bf16[1024,3072]{1,0:T(8,128)(2,1)} %get-tuple-element.120.refs_1_, bf16[1024,768]{1,0:T(8,128)(2,1)S(1)} %copy-done.11, bf16[1024,768]{1,0:T(8,128)(2,1)S(1)} %copy-done.12, ...), custom_call_target="tpu_custom_call" | custom-call | flops 4831838208 | bytes 19267584 | tf_op jit(solution)/shard_map/pallas_call | solution.py:72
  252.5 7.1 %shard_map.206.refs_6_ = bf16[16,96,768]{2,1,0:T(8,128)(2,1)S(1)} custom-call(bf16[1024,3072]{1,0:T(8,128)(2,1)} %get-tuple-element.115.refs_0_, bf16[1024,3072]{1,0:T(8,128)(2,1)} %get-tuple-element.116.refs_1_, bf16[1024,768]{1,0:T(8,128)(2,1)S(1)} %copy-done.10, bf16[1024,768]{1,0:T(8,128)(2,1)S(1)} %copy-done.9, bf16[16,120,768]{2,1,0:T(8,128)(2,1)} %copy-done.7), custom_call_target="tpu_custom_call" | custom-call | flops 4831838208 | bytes 18087936 | tf_op jit(solution)/shard_map/pallas_call | solution.py:72
  261.9 8.0 %shard_map.207 = (bf16[8,72,768]{2,1,0:T(8,128)(2,1)S(1)}, bf16[8,72,768]{2,1,0:T(8,128)(2,1)S(1)}, bf16[8,48,768]{2,1,0:T(8,128)(2,1)S(1)}, bf16[8,48,768]{2,1,0:T(8,128)(2,1)S(1)}) custom-call(bf16[1024,3072]{1,0:T(8,128)(2,1)} %get-tuple-element.119.refs_0_, bf16[1024,3072]{1,0:T(8,128)(2,1)} %get-tuple-element.120.refs_1_, ...), custom_call_target="tpu_custom_call" | custom-call | flops 4831838208 | bytes 22216704 | tf_op jit(solution)/shard_map/pallas_call | solution.py:72
  272.8 8.6 %shard_map.208 = (bf16[8,48,768]{2,1,0:T(8,128)(2,1)S(1)}, bf16[8,48,768]{2,1,0:T(8,128)(2,1)S(1)}, bf16[8,48,768]{2,1,0:T(8,128)(2,1)S(1)}, bf16[8,48,768]{2,1,0:T(8,128)(2,1)S(1)}) custom-call(bf16[1024,3072]{1,0:T(8,128)(2,1)} %get-tuple-element.115.refs_0_, bf16[1024,3072]{1,0:T(8,128)(2,1)} %get-tuple-element.116.refs_1_, ...), custom_call_target="tpu_custom_call" | custom-call | flops 4831838208 | bytes 20447232 | tf_op jit(solution)/shard_map/pallas_call | solution.py:72
  282.7 10.4 %shard_map.209.refs_7_.refs_2_.refs_0_ = bf16[3,1024,256]{2,1,0:T(8,128)(2,1)S(1)} custom-call(bf16[1024,2304]{1,0:T(8,128)(2,1)} %get-tuple-element.98.refs_0_.refs_1_.refs_2_, bf16[1024,2304]{1,0:T(8,128)(2,1)} %get-tuple-element.98.refs_0_.refs_1_.refs_2_, bf16[1024,2304]{1,0:T(8,128)(2,1)} %get-tuple-element.98.refs_0_.refs_1_.refs_2_, ...), custom_call_target="tpu_custom_call" | custom-call | flops 2684354560 | bytes 22024192 | tf_op jit(solution)/shard_map/pallas_call | solution.py:72
  297.5 10.1 %shard_map.211.refs_7_.refs_3_.refs_1_ = bf16[3,1024,256]{2,1,0:T(8,128)(2,1)S(1)} custom-call(bf16[1024,2304]{1,0:T(8,128)(2,1)} %get-tuple-element.98.refs_0_.refs_1_.refs_2_, bf16[1024,2304]{1,0:T(8,128)(2,1)} %get-tuple-element.98.refs_0_.refs_1_.refs_2_, bf16[1024,2304]{1,0:T(8,128)(2,1)} %get-tuple-element.98.refs_0_.refs_1_.refs_2_, ...), custom_call_target="tpu_custom_call" | custom-call | flops 2684354560 | bytes 22024192 | tf_op jit(solution)/shard_map/pallas_call | solution.py:72
  311.5 5.9 %collective-permute-start.19 = (bf16[120,768]{1,0:T(8,128)(2,1)S(1)}, bf16[120,768]{1,0:T(8,128)(2,1)S(1)}, u32[]{:S(2)}, u32[]{:S(2)}) collective-permute-start(bf16[120,768]{1,0:T(8,128)(2,1)S(1)} %get-tuple-element.146.refs_10_), channel_id=1, source_target_pairs={{0,2},{1,3},{2,0},{3,1},{4,6},{5,7},{6,4},{7,5},{8,10},{9,11},{10,... | collective-permute-start | bytes 552968 | tf_op jit(solution)/shard_map/ppermute | solution.py:815
  319.9 10.5 %shard_map.214.refs_4_.refs_11_.refs_2_ = bf16[3,1024,256]{2,1,0:T(8,128)(2,1)S(1)} custom-call(bf16[1024,2304]{1,0:T(8,128)(2,1)} %get-tuple-element.98.refs_0_.refs_1_.refs_2_, bf16[1024,2304]{1,0:T(8,128)(2,1)} %get-tuple-element.98.refs_0_.refs_1_.refs_2_, bf16[1024,2304]{1,0:T(8,128)(2,1)} %get-tuple-element.98.refs_0_.refs_1_.refs_2_, ...), custom_call_target="tpu_custom_call" | custom-call | flops 2684354560 | bytes 22024192 | tf_op jit(solution)/shard_map/pallas_call | solution.py:72
  330.6 2.3 collective-permute-done.20
  333.0 14.5 %shard_map.216 = (bf16[16,80,768]{2,1,0:T(8,128)(2,1)}, bf16[16,80,768]{2,1,0:T(8,128)(2,1)}, f32[16,768]{1,0:T(8,128)}) custom-call(s32[4]{0:T(128)S(1)} %pad_add_fusion.refs_0_, s32[1]{0:T(128)S(6)} %copy.36.refs_1_, bf16[3,1024,256]{2,1,0:T(8,128)(2,1)S(1)} %copy-done.3, bf16[3,1024,256]{2,1,0:T(8,128)(2,1)S(1)} %copy-done.6, ...), custom_call_target="tpu_custom_call" | custom-call | flops 7247757312 | bytes 20152340 | tf_op jit(solution)/shard_map/pallas_call | solution.py:72
  347.5 4.2 %collective-permute-done.22.refs_1_ = bf16[16,80,768]{2,1,0:T(8,128)(2,1)S(1)} collective-permute-done((bf16[16,80,768]{2,1,0:T(8,128)(2,1)}, bf16[16,80,768]{2,1,0:T(8,128)(2,1)S(1)}, u32[]{:S(2)}, u32[]{:S(2)}) %collective-permute-start.22) | collective-permute-done | bytes 1966112 | tf_op jit(solution)/shard_map/ppermute | solution.py:815
  356.7 2.6 collective-permute-start.30
  361.8 8.9 %shard_map.218 = f32[1024,768]{1,0:T(8,128)} custom-call(bf16[3,1024,256]{2,1,0:T(8,128)(2,1)S(1)} %copy-done.3, bf16[3,1024,256]{2,1,0:T(8,128)(2,1)S(1)} %copy-done.6, bf16[3,1024,256]{2,1,0:T(8,128)(2,1)S(1)} %shard_map.214.refs_4_.refs_11_.refs_2_, bf16[1024,768]{1,0:T(8,128)(2,1)} %bitcast.43, f32[1024,768]{1,0:T(8,128)} %get-tuple-element.149.refs_4_, ...), custom_call_target="tpu_custom_call" | custom-call | flops 3623878656 | bytes 16146432 | tf_op jit(solution)/shard_map/pallas_call | solution.py:72
  374.0 3.9 collective-permute-done.25.refs_1_
  384.4 4.9 %collective-permute-done.28 = bf16[80,768]{1,0:T(8,128)(2,1)S(1)} collective-permute-done((bf16[80,768]{1,0:T(8,128)(2,1)S(1)}, bf16[80,768]{1,0:T(8,128)(2,1)S(1)}, u32[]{:S(2)}, u32[]{:S(2)}) %collective-permute-start.28) | collective-permute-done | bytes 122912 | tf_op jit(solution)/shard_map/ppermute | solution.py:815
  (131 shorter events, 56.4 us)
Async XLA Ops:
  7.2 97.1 %all-gather.3.cloned.1.call-start = ((), (), s32[]{:S(2)}) async-start(), calls=%async_computation | async-start | bytes 9732096 | tf_op jit(solution)/shard_map/all_gather | solution.py:1047
  10.6 10.2 %collective-permute-start = (bf16[1,112,768]{2,1,0:T(8,128)(2,1)S(1)}, bf16[1,112,768]{2,1,0:T(8,128)(2,1)S(1)}, u32[]{:S(2)}, u32[]{:S(2)}) collective-permute-start(bf16[1,112,768]{2,1,0:T(8,128)(2,1)S(1)} %fusion.4), channel_id=1, source_target_pairs={{0,2},{1,3},{2,0},{3,1},{4,6},{5,7},{6,4},{7,5},{8,10},{9,11},{10,... | collective-permute-start | bytes 516104 | tf_op jit(solution)/shard_map/ppermute | solution.py:815
  13.7 18.5 %collective-permute-start.1 = (bf16[1,112,768]{2,1,0:T(8,128)(2,1)S(1)}, bf16[1,112,768]{2,1,0:T(8,128)(2,1)S(1)}, u32[]{:S(2)}, u32[]{:S(2)}) collective-permute-start(bf16[1,112,768]{2,1,0:T(8,128)(2,1)S(1)} %fusion.4), channel_id=1, source_target_pairs={{0,4},{1,5},{2,6},{3,7},{4,0},{5,1},{6,2},{7,3},{8,12},{9,13},{10,... | collective-permute-start | bytes 516104 | tf_op jit(solution)/shard_map/ppermute | solution.py:815
  16.3 15.9 %collective-permute-start.2 = (bf16[1,112,768]{2,1,0:T(8,128)(2,1)S(1)}, bf16[1,112,768]{2,1,0:T(8,128)(2,1)S(1)}, u32[]{:S(2)}, u32[]{:S(2)}) collective-permute-start(bf16[1,112,768]{2,1,0:T(8,128)(2,1)S(1)} %fusion.4), channel_id=1, source_target_pairs={{0,6},{1,7},{2,4},{3,5},{4,2},{5,3},{6,0},{7,1},{8,14},{9,15},{10,... | collective-permute-start | bytes 516104 | tf_op jit(solution)/shard_map/ppermute | solution.py:815
  32.3 9.4 %collective-permute-start.6 = (bf16[4,112,384]{2,1,0:T(8,128)(2,1)S(1)}, bf16[4,112,384]{2,1,0:T(8,128)(2,1)S(1)}, u32[]{:S(2)}, u32[]{:S(2)}) collective-permute-start(bf16[4,112,384]{2,1,0:T(8,128)(2,1)S(1)} %get-tuple-element.184), channel_id=1, source_target_pairs={{0,8},{1,9},{2,10},{3,11},{4,12},{5,13},{6,14},{7,15},{8,0},{9,1},... | collective-permute-start | bytes 1032200 | tf_op jit(solution)/shard_map/ppermute | solution.py:815
  33.9 11.0 %collective-permute-start.3 = (bf16[4,112,384]{2,1,0:T(8,128)(2,1)S(1)}, bf16[4,112,384]{2,1,0:T(8,128)(2,1)S(1)}, u32[]{:S(2)}, u32[]{:S(2)}) collective-permute-start(bf16[4,112,384]{2,1,0:T(8,128)(2,1)S(1)} %get-tuple-element.185), channel_id=1, source_target_pairs={{0,16},{1,17},{2,18},{3,19},{4,20},{5,21},{6,22},{7,23},{8,24},{9,... | collective-permute-start | bytes 1032200 | tf_op jit(solution)/shard_map/ppermute | solution.py:815
  41.8 16.9 %collective-permute-start.7 = (bf16[8,112,384]{2,1,0:T(8,128)(2,1)S(1)}, bf16[8,112,384]{2,1,0:T(8,128)(2,1)S(1)}, u32[]{:S(2)}, u32[]{:S(2)}) collective-permute-start(bf16[8,112,384]{2,1,0:T(8,128)(2,1)S(1)} %pad_maximum_fusion.4), channel_id=1, source_target_pairs={{0,16},{1,17},{2,18},{3,19},{4,20},{5,21},{6,22},{7,23},{8,24},{9,... | collective-permute-start | bytes 2064392 | tf_op jit(solution)/shard_map/ppermute | solution.py:815
  45.0 17.9 %collective-permute-start.4 = (bf16[8,112,384]{2,1,0:T(8,128)(2,1)S(1)}, bf16[8,112,384]{2,1,0:T(8,128)(2,1)S(1)}, u32[]{:S(2)}, u32[]{:S(2)}) collective-permute-start(bf16[8,112,384]{2,1,0:T(8,128)(2,1)S(1)} %pad_maximum_fusion.3), channel_id=1, source_target_pairs={{0,8},{1,9},{2,10},{3,11},{4,12},{5,13},{6,14},{7,15},{8,0},{9,1},... | collective-permute-start | bytes 2064392 | tf_op jit(solution)/shard_map/ppermute | solution.py:815
  60.0 6.0 %collective-permute-start.8 = (bf16[16,112,384]{2,1,0:T(8,128)(2,1)}, bf16[16,112,384]{2,1,0:T(8,128)(2,1)}, u32[]{:S(2)}, u32[]{:S(2)}) collective-permute-start(bf16[16,112,384]{2,1,0:T(8,128)(2,1)} %pad_maximum_fusion.1.refs_4_), channel_id=1, source_target_pairs={{0,1},{1,0},{2,3},{3,2},{4,5},{5,4},{6,7},{7,6},{8,9},{9,8},{10,11... | collective-permute-start | bytes 4128776 | tf_op jit(solution)/shard_map/ppermute | solution.py:815
  250.9 9.0 %collective-permute-start.10 = (bf16[16,120,768]{2,1,0:T(8,128)(2,1)S(1)}, bf16[16,120,768]{2,1,0:T(8,128)(2,1)S(1)}, u32[]{:S(2)}, u32[]{:S(2)}) collective-permute-start(bf16[16,120,768]{2,1,0:T(8,128)(2,1)S(1)} %shard_map.205.refs_4_), channel_id=1, source_target_pairs={{0,1},{1,0},{2,3},{3,2},{4,5},{5,4},{6,7},{7,6},{8,9},{9,8},{10,11... | collective-permute-start | bytes 8847368 | tf_op jit(solution)/shard_map/ppermute | solution.py:815
  259.6 13.2 %collective-permute-start.9 = (bf16[16,96,768]{2,1,0:T(8,128)(2,1)S(1)}, bf16[16,96,768]{2,1,0:T(8,128)(2,1)}, u32[]{:S(2)}, u32[]{:S(2)}) collective-permute-start(bf16[16,96,768]{2,1,0:T(8,128)(2,1)S(1)} %shard_map.206.refs_6_), channel_id=1, source_target_pairs={{0,1},{1,0},{2,3},{3,2},{4,5},{5,4},{6,7},{7,6},{8,9},{9,8},{10,11... | collective-permute-start | bytes 7077896 | tf_op jit(solution)/shard_map/ppermute | solution.py:815
  269.8 24.4 %collective-permute-start.11 = (bf16[8,72,768]{2,1,0:T(8,128)(2,1)S(1)}, bf16[8,72,768]{2,1,0:T(8,128)(2,1)S(1)}, u32[]{:S(2)}, u32[]{:S(2)}) collective-permute-start(bf16[8,72,768]{2,1,0:T(8,128)(2,1)S(1)} %get-tuple-element.127.refs_6_), channel_id=1, source_target_pairs={{0,8},{1,9},{2,10},{3,11},{4,12},{5,13},{6,14},{7,15},{8,0},{9,1},... | collective-permute-start | bytes 2654216 | tf_op jit(solution)/shard_map/ppermute | solution.py:815
  271.3 22.9 %collective-permute-start.12 = (bf16[8,48,768]{2,1,0:T(8,128)(2,1)S(1)}, bf16[8,48,768]{2,1,0:T(8,128)(2,1)S(1)}, u32[]{:S(2)}, u32[]{:S(2)}) collective-permute-start(bf16[8,48,768]{2,1,0:T(8,128)(2,1)S(1)} %get-tuple-element.129.refs_8_), channel_id=1, source_target_pairs={{0,16},{1,17},{2,18},{3,19},{4,20},{5,21},{6,22},{7,23},{8,24},{9,... | collective-permute-start | bytes 1769480 | tf_op jit(solution)/shard_map/ppermute | solution.py:815
  281.4 26.2 %collective-permute-start.13 = (bf16[8,48,768]{2,1,0:T(8,128)(2,1)S(1)}, bf16[8,48,768]{2,1,0:T(8,128)(2,1)S(1)}, u32[]{:S(2)}, u32[]{:S(2)}) collective-permute-start(bf16[8,48,768]{2,1,0:T(8,128)(2,1)S(1)} %get-tuple-element.131.refs_8_), channel_id=1, source_target_pairs={{0,8},{1,9},{2,10},{3,11},{4,12},{5,13},{6,14},{7,15},{8,0},{9,1},... | collective-permute-start | bytes 1769480 | tf_op jit(solution)/shard_map/ppermute | solution.py:815
  282.1 25.5 %collective-permute-start.14 = (bf16[8,48,768]{2,1,0:T(8,128)(2,1)S(1)}, bf16[8,48,768]{2,1,0:T(8,128)(2,1)S(1)}, u32[]{:S(2)}, u32[]{:S(2)}) collective-permute-start(bf16[8,48,768]{2,1,0:T(8,128)(2,1)S(1)} %get-tuple-element.133.refs_10_), channel_id=1, source_target_pairs={{0,16},{1,17},{2,18},{3,19},{4,20},{5,21},{6,22},{7,23},{8,24},{9,... | collective-permute-start | bytes 1769480 | tf_op jit(solution)/shard_map/ppermute | solution.py:815
  294.6 16.8 %collective-permute-start.15 = (bf16[4,72,768]{2,1,0:T(8,128)(2,1)S(1)}, bf16[4,72,768]{2,1,0:T(8,128)(2,1)S(1)}, u32[]{:S(2)}, u32[]{:S(2)}) collective-permute-start(bf16[4,72,768]{2,1,0:T(8,128)(2,1)S(1)} %get-tuple-element.136.refs_8_), channel_id=1, source_target_pairs={{0,16},{1,17},{2,18},{3,19},{4,20},{5,21},{6,22},{7,23},{8,24},{9,... | collective-permute-start | bytes 1327112 | tf_op jit(solution)/shard_map/ppermute | solution.py:815
  296.1 15.2 %collective-permute-start.16 = (bf16[4,48,768]{2,1,0:T(8,128)(2,1)S(1)}, bf16[4,48,768]{2,1,0:T(8,128)(2,1)S(1)}, u32[]{:S(2)}, u32[]{:S(2)}) collective-permute-start(bf16[4,48,768]{2,1,0:T(8,128)(2,1)S(1)} %get-tuple-element.137.refs_9_), channel_id=1, source_target_pairs={{0,8},{1,9},{2,10},{3,11},{4,12},{5,13},{6,14},{7,15},{8,0},{9,1},... | collective-permute-start | bytes 884744 | tf_op jit(solution)/shard_map/ppermute | solution.py:815
  308.0 22.4 %collective-permute-start.17 = (bf16[4,48,768]{2,1,0:T(8,128)(2,1)S(1)}, bf16[4,48,768]{2,1,0:T(8,128)(2,1)S(1)}, u32[]{:S(2)}, u32[]{:S(2)}) collective-permute-start(bf16[4,48,768]{2,1,0:T(8,128)(2,1)S(1)} %get-tuple-element.140.refs_8_), channel_id=1, source_target_pairs={{0,16},{1,17},{2,18},{3,19},{4,20},{5,21},{6,22},{7,23},{8,24},{9,... | collective-permute-start | bytes 884744 | tf_op jit(solution)/shard_map/ppermute | solution.py:815
  308.6 21.8 %collective-permute-start.18 = (bf16[4,48,768]{2,1,0:T(8,128)(2,1)S(1)}, bf16[4,48,768]{2,1,0:T(8,128)(2,1)S(1)}, u32[]{:S(2)}, u32[]{:S(2)}) collective-permute-start(bf16[4,48,768]{2,1,0:T(8,128)(2,1)S(1)} %get-tuple-element.141.refs_9_), channel_id=1, source_target_pairs={{0,8},{1,9},{2,10},{3,11},{4,12},{5,13},{6,14},{7,15},{8,0},{9,1},... | collective-permute-start | bytes 884744 | tf_op jit(solution)/shard_map/ppermute | solution.py:815
  311.5 19.0 %collective-permute-start.19 = (bf16[120,768]{1,0:T(8,128)(2,1)S(1)}, bf16[120,768]{1,0:T(8,128)(2,1)S(1)}, u32[]{:S(2)}, u32[]{:S(2)}) collective-permute-start(bf16[120,768]{1,0:T(8,128)(2,1)S(1)} %get-tuple-element.146.refs_10_), channel_id=1, source_target_pairs={{0,2},{1,3},{2,0},{3,1},{4,6},{5,7},{6,4},{7,5},{8,10},{9,11},{10,... | collective-permute-start | bytes 552968 | tf_op jit(solution)/shard_map/ppermute | solution.py:815
  317.5 15.4 %collective-permute-start.20 = (bf16[120,768]{1,0:T(8,128)(2,1)S(1)}, bf16[120,768]{1,0:T(8,128)(2,1)S(1)}, u32[]{:S(2)}, u32[]{:S(2)}) collective-permute-start(bf16[120,768]{1,0:T(8,128)(2,1)S(1)} %get-tuple-element.147.refs_11_), channel_id=1, source_target_pairs={{0,4},{1,5},{2,6},{3,7},{4,0},{5,1},{6,2},{7,3},{8,12},{9,13},{10,... | collective-permute-start | bytes 552968 | tf_op jit(solution)/shard_map/ppermute | solution.py:815
  318.4 14.5 %collective-permute-start.21 = (bf16[120,768]{1,0:T(8,128)(2,1)S(1)}, bf16[120,768]{1,0:T(8,128)(2,1)S(1)}, u32[]{:S(2)}, u32[]{:S(2)}) collective-permute-start(bf16[120,768]{1,0:T(8,128)(2,1)S(1)} %get-tuple-element.148.refs_12_), channel_id=1, source_target_pairs={{0,6},{1,7},{2,4},{3,5},{4,2},{5,3},{6,0},{7,1},{8,14},{9,15},{10,... | collective-permute-start | bytes 552968 | tf_op jit(solution)/shard_map/ppermute | solution.py:815
  353.7 17.0 %collective-permute-start.23 = (bf16[8,80,384]{2,1,0:T(8,128)(2,1)S(1)}, bf16[8,80,384]{2,1,0:T(8,128)(2,1)S(1)}, u32[]{:S(2)}, u32[]{:S(2)}) collective-permute-start(bf16[8,80,384]{2,1,0:T(8,128)(2,1)S(1)} %get-tuple-element.167.refs_7_), channel_id=1, source_target_pairs={{0,8},{1,9},{2,10},{3,11},{4,12},{5,13},{6,14},{7,15},{8,0},{9,1},... | collective-permute-start | bytes 1474568 | tf_op jit(solution)/shard_map/ppermute | solution.py:815
  355.3 15.4 %collective-permute-start.24 = (bf16[8,80,384]{2,1,0:T(8,128)(2,1)S(1)}, bf16[8,80,384]{2,1,0:T(8,128)(2,1)S(1)}, u32[]{:S(2)}, u32[]{:S(2)}) collective-permute-start(bf16[8,80,384]{2,1,0:T(8,128)(2,1)S(1)} %get-tuple-element.168.refs_8_), channel_id=1, source_target_pairs={{0,16},{1,17},{2,18},{3,19},{4,20},{5,21},{6,22},{7,23},{8,24},{9,... | collective-permute-start | bytes 1474568 | tf_op jit(solution)/shard_map/ppermute | solution.py:815
  356.7 15.5 %collective-permute-start.30 = (bf16[96,768]{1,0:T(8,128)(2,1)S(1)}, bf16[96,768]{1,0:T(8,128)(2,1)S(1)}, u32[]{:S(2)}, u32[]{:S(2)}) collective-permute-start(bf16[96,768]{1,0:T(8,128)(2,1)S(1)} %get-tuple-element.158.refs_12_), channel_id=1, source_target_pairs={{0,2},{1,3},{2,0},{3,1},{4,6},{5,7},{6,4},{7,5},{8,10},{9,11},{10,... | collective-permute-start | bytes 442376 | tf_op jit(solution)/shard_map/ppermute | solution.py:815
  359.3 13.9 %collective-permute-start.31 = (bf16[96,768]{1,0:T(8,128)(2,1)S(1)}, bf16[96,768]{1,0:T(8,128)(2,1)S(1)}, u32[]{:S(2)}, u32[]{:S(2)}) collective-permute-start(bf16[96,768]{1,0:T(8,128)(2,1)S(1)} %get-tuple-element.159.refs_13_), channel_id=1, source_target_pairs={{0,4},{1,5},{2,6},{3,7},{4,0},{5,1},{6,2},{7,3},{8,12},{9,13},{10,... | collective-permute-start | bytes 442376 | tf_op jit(solution)/shard_map/ppermute | solution.py:815
  360.3 12.9 %collective-permute-start.32 = (bf16[96,768]{1,0:T(8,128)(2,1)S(1)}, bf16[96,768]{1,0:T(8,128)(2,1)S(1)}, u32[]{:S(2)}, u32[]{:S(2)}) collective-permute-start(bf16[96,768]{1,0:T(8,128)(2,1)S(1)} %get-tuple-element.160.refs_14_), channel_id=1, source_target_pairs={{0,6},{1,7},{2,4},{3,5},{4,2},{5,3},{6,0},{7,1},{8,14},{9,15},{10,... | collective-permute-start | bytes 442376 | tf_op jit(solution)/shard_map/ppermute | solution.py:815
  370.9 6.9 %collective-permute-start.25 = (bf16[4,80,384]{2,1,0:T(8,128)(2,1)S(1)}, bf16[4,80,384]{2,1,0:T(8,128)(2,1)S(1)}, u32[]{:S(2)}, u32[]{:S(2)}) collective-permute-start(bf16[4,80,384]{2,1,0:T(8,128)(2,1)S(1)} %get-tuple-element.174), channel_id=1, source_target_pairs={{0,16},{1,17},{2,18},{3,19},{4,20},{5,21},{6,22},{7,23},{8,24},{9,... | collective-permute-start | bytes 737288 | tf_op jit(solution)/shard_map/ppermute | solution.py:815
  371.6 6.6 %collective-permute-start.26 = (bf16[4,80,384]{2,1,0:T(8,128)(2,1)S(1)}, bf16[4,80,384]{2,1,0:T(8,128)(2,1)S(1)}, u32[]{:S(2)}, u32[]{:S(2)}) collective-permute-start(bf16[4,80,384]{2,1,0:T(8,128)(2,1)S(1)} %get-tuple-element.176), channel_id=1, source_target_pairs={{0,8},{1,9},{2,10},{3,11},{4,12},{5,13},{6,14},{7,15},{8,0},{9,1},... | collective-permute-start | bytes 737288 | tf_op jit(solution)/shard_map/ppermute | solution.py:815
  378.4 6.0 %collective-permute-start.27 = (bf16[80,768]{1,0:T(8,128)(2,1)S(1)}, bf16[80,768]{1,0:T(8,128)(2,1)S(1)}, u32[]{:S(2)}, u32[]{:S(2)}) collective-permute-start(bf16[80,768]{1,0:T(8,128)(2,1)S(1)} %get-tuple-element.178), channel_id=1, source_target_pairs={{0,2},{1,3},{2,0},{3,1},{4,6},{5,7},{6,4},{7,5},{8,10},{9,11},{10,... | collective-permute-start | bytes 368648 | tf_op jit(solution)/shard_map/ppermute | solution.py:815
  379.3 10.0 %collective-permute-start.28 = (bf16[80,768]{1,0:T(8,128)(2,1)S(1)}, bf16[80,768]{1,0:T(8,128)(2,1)S(1)}, u32[]{:S(2)}, u32[]{:S(2)}) collective-permute-start(bf16[80,768]{1,0:T(8,128)(2,1)S(1)} %get-tuple-element.179), channel_id=1, source_target_pairs={{0,4},{1,5},{2,6},{3,7},{4,0},{5,1},{6,2},{7,3},{8,12},{9,13},{10,... | collective-permute-start | bytes 368648 | tf_op jit(solution)/shard_map/ppermute | solution.py:815
  381.3 8.0 %collective-permute-start.29 = (bf16[80,768]{1,0:T(8,128)(2,1)S(1)}, bf16[80,768]{1,0:T(8,128)(2,1)S(1)}, u32[]{:S(2)}, u32[]{:S(2)}) collective-permute-start(bf16[80,768]{1,0:T(8,128)(2,1)S(1)} %get-tuple-element.180), channel_id=1, source_target_pairs={{0,6},{1,7},{2,4},{3,5},{4,2},{5,3},{6,0},{7,1},{8,14},{9,15},{10,... | collective-permute-start | bytes 368648 | tf_op jit(solution)/shard_map/ppermute | solution.py:815
  (22 other events, 171.5 us)
Sparse Core Ops, SparseCore 0:
  11.6 92.5 all-gather.2
